TPU v7x, 32 devices: a whole 2x2x4 slice. The times are simulated.
32 devices in a mesh: gx: 4 (over z), gy: 8 (over y, x, core).
Axes of the slice: x: 2, y: 2, z: 4, core: 2. Of those that a mesh axis runs over, the one named last changes fastest.
Arguments:
- hidden: float32 [16384, 1024], P(('gx', 'gy')), may hold values from -6 to 6
- memory: bfloat16 [18816, 1024], P(('gx', 'gy')), may hold values from -6 to 6
- lengths: int32 [32], P(('gx', 'gy')), may hold values from 192 to 512, as said below
- page_class: int32 [32], P(('gx', 'gy')), may hold values from 0 to 1
- cotangent: float32 [16384, 1024], P(('gx', 'gy')), may hold values from -6 to 6
- w_self_qkv: bfloat16 [1024, 3072], P(('gx', 'gy')), may hold values from -0.1875 to 0.1875
- w_self_out: bfloat16 [1024, 1024], P(('gx', 'gy')), may hold values from -3 to 3
- w_cross_q: bfloat16 [1024, 1024], P(('gx', 'gy')), may hold values from -0.1875 to 0.1875
- w_cross_kv: bfloat16 [1024, 2048], P(('gx', 'gy')), may hold values from -0.1875 to 0.1875
- w_cross_out: bfloat16 [1024, 1024], P(('gx', 'gy')), may hold values from -3 to 3
- w_fc1: bfloat16 [1024, 4096], P(('gx', 'gy')), may hold values from -0.1875 to 0.1875
- w_fc2: bfloat16 [4096, 1024], P(('gx', 'gy')), may hold values from -0.09375 to 0.09375
- norm_gains: bfloat16 [3, 1024], P(None, ('gx', 'gy')), may hold values from 0.5 to 1.5
- norm_biases: bfloat16 [3, 1024], P(None, ('gx', 'gy')), may hold values from -1.75 to 1.75
Outputs:
- result: float32 [16384, 1024], P(('gx', 'gy'))
- grad_hidden: float32 [16384, 1024], P(('gx', 'gy'))
- grad_memory: float32 [18816, 1024], P(('gx', 'gy'))
- grad_self_qkv: float32 [1024, 3072], P(('gx', 'gy'))
- grad_self_out: float32 [1024, 1024], P(('gx', 'gy'))
- grad_cross_q: float32 [1024, 1024], P(('gx', 'gy'))
- grad_cross_kv: float32 [1024, 2048], P(('gx', 'gy'))
- grad_cross_out: float32 [1024, 1024], P(('gx', 'gy'))
- grad_fc1: float32 [1024, 4096], P(('gx', 'gy'))
- grad_fc2: float32 [4096, 1024], P(('gx', 'gy'))
- grad_gains: float32 [3, 1024], P(None, ('gx', 'gy'))
- grad_biases: float32 [3, 1024], P(None, ('gx', 'gy'))
Inputs may be any that keep to these rules, and one draw needn't show every extreme that they name: `lengths`: some page has exactly 512 decoder tokens; every page has at least 192.
All inputs are finite; a program needn't handle non-finite values.
Results may differ from a plain program's by a relative error of at most 0.017.
Values may be sent and summed in bfloat16 or wider, within the bound.
No kernel may reach another device: no remote copies, remote signals or barrier semaphores. Data moves between devices by JAX's collectives and lax.ppermute only.
A program may use at most 320 MiB of HBM per device.

v0:
```python
import functools

import jax
import jax.numpy as jnp
from jax import lax
from jax.experimental import pallas as pl
from jax.experimental.pallas import tpu as pltpu
from jax.sharding import PartitionSpec as P

HEADS = 16
MEM_BIG = 588
ALL = ("gx", "gy")
BF = jnp.bfloat16
F32 = jnp.float32
PAIR = 128
LIMITS = {'feed_back': 50, 'pass_on': 8, 'plane_sum': 8, 'place': 8, 'hidden_order': 8, 'memory_grad': 12, 'turn': 12, 'wgrad': 44, 'wgrad_down': 44}
FAR_OUTS = {'wgrad': (0, 1, 2), 'wgrad_down': (0, 1, 2), 'feed_up': (0, 1, 2), 'place_dot': (0,), 'feed_back': (0, 1)}
FAR_INS = {'pass_on': (0, 1, 2, 3), 'plane_sum': (0, 1, 2)}


def dot(a, b):
    return jnp.dot(a, b, preferred_element_type=F32)


def dot_nt(a, b):
    return lax.dot_general(a, b, (((1,), (1,)), ((), ())), preferred_element_type=F32)


def dot_tn(a, b):
    return lax.dot_general(a, b, (((0,), (0,)), ((), ())), preferred_element_type=F32)


def run(
    kernel, grid, ins, outs, prefetch=(), scratch=(), deps=(), cost=None, name=None
):
    count = len(prefetch) + len(ins)

    def body(*refs):
        return kernel(*refs[:count], *refs[count + len(deps) :])

    result = pl.pallas_call(
        body,
        grid_spec=pltpu.PrefetchScalarGridSpec(
            num_scalar_prefetch=len(prefetch),
            grid=grid,
            in_specs=[spec for _, spec in ins] + [pl.BlockSpec(memory_space=pl.ANY)] * len(deps),
            out_specs=[spec for _, spec in outs],
            scratch_shapes=scratch,
        ),
        out_shape=[
            pltpu.HBM(shape.shape, shape.dtype) if k in FAR_OUTS.get(name, ()) else shape
            for k, (shape, _) in enumerate(outs)
        ],
        compiler_params=pltpu.CompilerParams(
            dimension_semantics=("arbitrary",) * len(grid), vmem_limit_bytes=LIMITS.get(name, 30) * 1024 * 1024
        ),
        cost_estimate=cost,
        name=name,
    )(
        *prefetch,
        *[
            pltpu.with_memory_space_constraint(a, pltpu.HBM)
            if k in FAR_INS.get(name, ())
            else a
            for k, (a, _) in enumerate(ins)
        ],
        *deps,
    )
    return result if len(outs) > 1 else result[0]


def costs(flops, nbytes, transcendentals=0):
    return pl.CostEstimate(
        flops=flops, bytes_accessed=nbytes, transcendentals=transcendentals
    )


def shaped(shape, dtype):
    return jax.ShapeDtypeStruct(shape, dtype)


def allowed_t(key_count, q0, q1, limit, causal):
    key_at = lax.broadcasted_iota(jnp.int32, (key_count, q1 - q0), 0)
    ok = key_at < limit
    if causal:
        query_at = lax.broadcasted_iota(jnp.int32, (key_count, q1 - q0), 1) + q0
        ok = ok & (key_at <= query_at)
    return ok


def half_mask(width, half):
    lane = lax.broadcasted_iota(jnp.int32, (1, width), 1)
    return ((lane // (width // 2)) == half).astype(F32).astype(BF)


def attn_fwd_kernel(spans, causal, limit_ref, q_ref, k_ref, v_ref, o_ref, lse_ref):
    width = q_ref.shape[1]
    half = width // 2
    limit = limit_ref[0]
    scale = BF(half**-0.5)
    v_t = v_ref[...].T
    for q0, q1, keys in spans:
        query = q_ref[q0:q1, :] * scale
        ok = allowed_t(keys, q0, q1, limit, causal)
        outs = []
        for h in range(2):
            s = dot_nt(k_ref[:keys, :], query * half_mask(width, h))
            s = jnp.where(ok, s, -1e30)
            top = jnp.max(s, axis=0, keepdims=True)
            e = jnp.exp(s - top)
            total = jnp.sum(e, axis=0, keepdims=True)
            outs.append(dot(v_t[h * half : (h + 1) * half, :keys], e.astype(BF)) / total)
            lse_ref[0, h : h + 1, q0:q1] = top + jnp.log(total)
        o_ref[q0:q1, :] = jnp.concatenate(outs, axis=0).T.astype(BF)


def attn_bwd_kernel(
    spans, causal, limit_ref, q_ref, k_ref, v_ref, o_ref, do_ref, lse_ref, *outs_ref
):
    dq_ref = outs_ref[0].at[0]
    dk_ref, dv_ref = (outs_ref[-1].at[k - 2 + outs_ref[-1].shape[0]] for k in range(2))
    width = q_ref.shape[1]
    half = width // 2
    limit = limit_ref[0]
    scale = BF(half**-0.5)
    k_t = k_ref[...].T * scale
    total_k = k_ref.shape[0]
    dk = jnp.zeros((total_k, width), F32)
    dv = jnp.zeros((total_k, width), F32)
    for q0, q1, keys in spans:
        query = q_ref[q0:q1, :] * scale
        grad_o = do_ref[q0:q1, :]
        ok = allowed_t(keys, q0, q1, limit, causal)
        both = (grad_o.astype(F32) * o_ref[q0:q1, :].astype(F32)).T
        outs = []
        dk_part = jnp.zeros((keys, width), F32)
        dv_part = jnp.zeros((keys, width), F32)
        for h in range(2):
            mask = half_mask(width, h)
            query_h = query * mask
            grad_h = grad_o * mask
            inner = jnp.sum(both[h * half : (h + 1) * half], axis=0, keepdims=True)
            s = dot_nt(k_ref[:keys, :], query_h)
            p = jnp.where(ok, jnp.exp(s - lse_ref[0, h : h + 1, q0:q1]), 0.0)
            dv_part += dot(p.astype(BF), grad_h)
            dp = dot_nt(v_ref[:keys, :], grad_h)
            ds = (p * (dp - inner)).astype(BF)
            dk_part += dot(ds, query_h)
            outs.append(dot(k_t[h * half : (h + 1) * half, :keys], ds))
        dq_ref[q0:q1, :] = jnp.concatenate(outs, axis=0).T.astype(BF)
        if keys < total_k:
            pad = jnp.zeros((total_k - keys, width), F32)
            dk_part = jnp.concatenate([dk_part, pad], axis=0)
            dv_part = jnp.concatenate([dv_part, pad], axis=0)
        dk += dk_part
        dv += dv_part
    dk_ref[...] = dk.astype(BF)
    dv_ref[...] = dv.astype(BF)


def make_spans(queries, keys, causal):
    step = 256
    return tuple(
        (q, q + step, min(q + step, keys) if causal else keys) for q in range(0, queries, step)
    )


def attn_fwd(q, kv, k_at, v_at, limit, causal, deps=()):
    q_arr, q_at = q
    queries, keys = q_arr.shape[0], kv.shape[0]
    pairs = HEADS // 2
    return run(
        functools.partial(attn_fwd_kernel, make_spans(queries, keys, causal), causal),
        (pairs,),
        [
            (q_arr, pl.BlockSpec((queries, PAIR), lambda p, _: (0, q_at + p))),
            (kv, pl.BlockSpec((keys, PAIR), lambda p, _: (0, k_at + p))),
            (kv, pl.BlockSpec((keys, PAIR), lambda p, _: (0, v_at + p))),
        ],
        [
            (
                shaped((queries, pairs * PAIR), BF),
                pl.BlockSpec((queries, PAIR), lambda p, _: (0, p)),
            ),
            (
                shaped((pairs, 2, queries), F32),
                pl.BlockSpec((1, 2, queries), lambda p, _: (p, 0, 0)),
            ),
        ],
        prefetch=(limit,),
        deps=deps,
        cost=costs(16 * queries * keys * 1024, 8 * queries * 1024, 16 * queries * keys),
        name="attn_fwd",
    )


def attn_bwd(q, kv, k_at, v_at, o, do, lse, limit, causal, deps=()):
    q_arr, q_at = q
    queries, keys = q_arr.shape[0], kv.shape[0]
    pairs = HEADS // 2
    q_block = pl.BlockSpec((queries, PAIR), lambda p, _: (0, p))

    def stacked(count, rows):
        return (
            shaped((count, rows, pairs * PAIR), BF),
            pl.BlockSpec((count, rows, PAIR), lambda p, _: (0, 0, p)),
        )

    return run(
        functools.partial(attn_bwd_kernel, make_spans(queries, keys, causal), causal),
        (pairs,),
        [
            (q_arr, pl.BlockSpec((queries, PAIR), lambda p, _: (0, q_at + p))),
            (kv, pl.BlockSpec((keys, PAIR), lambda p, _: (0, k_at + p))),
            (kv, pl.BlockSpec((keys, PAIR), lambda p, _: (0, v_at + p))),
            (o, q_block),
            (do, q_block),
            (lse, pl.BlockSpec((1, 2, queries), lambda p, _: (p, 0, 0))),
        ],
        [stacked(3, queries)] if queries == keys else [stacked(1, queries), stacked(2, keys)],
        prefetch=(limit,),
        deps=deps,
        cost=costs(16 * queries * keys * 2560, 16 * queries * 1024, 16 * queries * keys),
        name="attn_bwd",
    )


def norm_parts(v):
    center = v - jnp.mean(v, -1, keepdims=True)
    inverse = lax.rsqrt(jnp.mean(center * center, -1, keepdims=True) + 1e-05)
    return center * inverse, inverse


def norm_back(grad, unit, inverse, gain):
    gain_grad = jnp.sum(grad * unit, axis=0)
    bias_grad = jnp.sum(grad, axis=0)
    scaled = grad * gain
    mean_a = jnp.mean(scaled, -1, keepdims=True)
    mean_b = jnp.mean(scaled * unit, -1, keepdims=True)
    return inverse * (scaled - mean_a - unit * mean_b), gain_grad, bias_grad


def gather_rows(w):
    return lax.all_gather(w, ALL, axis=0, tiled=True)


def scatter_rows(g):
    part = lax.psum_scatter(g, "gy", scatter_dimension=0, tiled=True)
    return lax.psum_scatter(part, "gx", scatter_dimension=0, tiled=True)


def shards_any(
    hidden,
    memory,
    lengths,
    page_class,
    cotangent,
    w_self_qkv,
    w_self_out,
    w_cross_q,
    w_cross_kv,
    w_cross_out,
    w_fc1,
    w_fc2,
    norm_gains,
    norm_biases,
    *,
    nx,
    ny,
):
    n = nx * ny
    tokens, d = hidden.shape
    rows = w_fc1.shape[0]
    ff = w_fc1.shape[1]
    cuts = w_fc2.shape[0] // rows
    mem_rows = -(-memory.shape[0] // 16) * 16
    slots_used = jnp.where(page_class == 0, MEM_BIG, MEM_BIG // 4).astype(jnp.int32)

    norm_cols = jnp.concatenate([norm_gains, norm_biases], axis=0).T
    norm_cols = jnp.pad(norm_cols, ((0, 0), (0, 128 - norm_cols.shape[1])))
    first = jnp.concatenate([w_self_qkv, w_cross_kv, norm_cols], axis=1)
    second = jnp.concatenate([w_self_out, w_cross_q, w_cross_out], axis=1)
    up_local = (
        w_fc1.reshape(rows, nx, ny, cuts, rows).transpose(0, 3, 2, 1, 4).reshape(rows, ff)
    )
    down_local = jnp.concatenate(
        [w_fc2[c * rows : (c + 1) * rows] for c in range(cuts)], axis=1
    )
    w_first = gather_rows(first)
    w_second = gather_rows(second)
    wup = gather_rows(up_local)
    wdown = lax.all_gather(down_local, ("gy", "gx"), axis=0, tiled=True)

    wqkv = w_first[:, : 3 * d]
    wckv = w_first[:, 3 * d : 5 * d]
    norms = w_first[:, 5 * d : 5 * d + 6].T.astype(F32)
    gains, biases = norms[:3], norms[3:]
    wso, wcq, wco = w_second[:, :d], w_second[:, d : 2 * d], w_second[:, 2 * d :]

    place = jnp.arange(d)
    source = place % rows + ((place // rows) % nx * ny + place // (rows * nx)) * rows
    select = (source[:, None] == place[None, :]).astype(BF)

    def turned(a):
        return dot_nt(select, a).astype(BF)

    unit1, inv1 = norm_parts(hidden)
    h1 = (unit1 * gains[0] + biases[0]).astype(BF)
    qkv = dot(h1, wqkv).astype(BF)
    blocks = d // PAIR
    o, lse = attn_fwd((qkv, 0), qkv, blocks, 2 * blocks, lengths, True)
    x1 = hidden + dot(o, wso)
    unit2, inv2 = norm_parts(x1)
    h2 = (unit2 * gains[1] + biases[1]).astype(BF)
    qc = dot(h2, wcq).astype(BF)
    memory_pad = jnp.pad(memory, ((0, mem_rows - memory.shape[0]), (0, 0)))
    kvc = dot(memory_pad, wckv).astype(BF)
    o2, lse2 = attn_fwd((qc, 0), kvc, 0, blocks, slots_used, False)
    x2 = x1 + dot(o2, wco)
    unit3, inv3 = norm_parts(x2)
    h3 = (unit3 * gains[2] + biases[2]).astype(BF)
    u = dot(h3, wup)
    cdf = 0.5 * (1.0 + lax.erf(u * (0.5**0.5)))
    g = (u * cdf).astype(BF)
    slope = (cdf + u * (jnp.exp(-0.5 * u * u) * 0.3989422804014327)).astype(BF)
    result = x2
    for c in range(cuts):
        result = result + dot(g[:, c * d : (c + 1) * d], wdown[:, c * d : (c + 1) * d])

    valid = (jnp.arange(tokens) < lengths[0])[:, None].astype(F32)
    dout = cotangent * valid
    dy3 = dout.astype(BF)
    grad_down = jnp.concatenate(
        [dot_tn(g[:, c * d : (c + 1) * d], dy3).astype(BF) for c in range(cuts)], axis=1
    )
    own_down = scatter_rows(grad_down)
    dg = jnp.concatenate(
        [dot_nt(dy3, wdown[:, c * d : (c + 1) * d]) for c in range(cuts)], axis=1
    )
    du = (dg * slope.astype(F32)).astype(BF)
    grad_up = dot(turned(h3), du).astype(BF)
    own_up = scatter_rows(grad_up)
    dh3 = dot_nt(du, wup)
    back3, gain3, bias3 = norm_back(dh3, unit3, inv3, gains[2])
    dx2 = dout + back3
    dy2 = dx2.astype(BF)
    do2 = dot_nt(dy2, wco).astype(BF)
    dqc, dkv = attn_bwd((qc, 0), kvc, 0, blocks, o2, do2, lse2, slots_used, False)
    dqc = dqc[0]
    dkvc = jnp.concatenate([dkv[0], dkv[1]], axis=1)
    mem_turned = turned(memory_pad)
    grad_mid = jnp.concatenate(
        [
            dot(turned(o2), dy2).astype(BF),
            dot(turned(h2), dqc).astype(BF),
            dot(mem_turned, dkvc).astype(BF),
        ],
        axis=1,
    )
    own_mid = scatter_rows(grad_mid)
    grad_memory = dot_nt(dkvc, wckv)[: memory.shape[0]]
    dh2 = dot_nt(dqc, wcq)
    back2, gain2, bias2 = norm_back(dh2, unit2, inv2, gains[1])
    dx1 = dx2 + back2
    dy1 = dx1.astype(BF)
    do = dot_nt(dy1, wso).astype(BF)
    dqkv = attn_bwd((qkv, 0), qkv, blocks, 2 * blocks, o, do, lse, lengths, True)
    dqkv = jnp.concatenate([dqkv[0], dqkv[1], dqkv[2]], axis=1)
    dh1 = dot_nt(dqkv, wqkv)
    back1, gain1, bias1 = norm_back(dh1, unit1, inv1, gains[0])
    grad_hidden = dx1 + back1
    norm_grads = jnp.stack([gain1, gain2, gain3, bias1, bias2, bias3])
    norm_grads = jnp.pad(norm_grads, ((0, 122), (0, 0))).astype(BF)
    grad_last = jnp.concatenate(
        [
            dot(turned(o), dy1).astype(BF),
            dot(turned(h1), dqkv).astype(BF),
            turned(norm_grads),
        ],
        axis=1,
    )
    own_last = scatter_rows(grad_last)

    own_up = (
        own_up.reshape(rows, cuts, ny, nx, rows).transpose(0, 3, 2, 1, 4).reshape(rows, ff)
    )
    own_down = jnp.concatenate(
        [own_down[:, c * d : (c + 1) * d] for c in range(cuts)], axis=0
    )
    own_norms = own_last[:, 4 * d : 4 * d + 6].T.astype(F32)
    return (
        result,
        grad_hidden,
        grad_memory,
        own_last[:, d : 4 * d].astype(F32),
        own_last[:, :d].astype(F32),
        own_mid[:, d : 2 * d].astype(F32),
        own_mid[:, 2 * d :].astype(F32),
        own_mid[:, :d].astype(F32),
        own_up.astype(F32),
        own_down.astype(F32),
        own_norms[:3],
        own_norms[3:],
    )


CORE, XBIT, YBIT = 1, 2, 4


def swap(a, bit):
    return lax.ppermute(a, ALL, [(i, i ^ bit) for i in range(32)])


def fence(*values):
    return lax.optimization_barrier(values)


def gather_line(w):
    return lax.all_gather(w, "gx", axis=0)


def gather_near(here):
    return here, swap(here, XBIT), swap(here, YBIT)


def gather_far(near):
    return swap(near[2][:2], XBIT), swap(near[1][2:], YBIT)


def swap_cores(pieces):
    return tuple(swap(p, CORE) for p in pieces)


def put_pieces(bits_ref, pieces, out):
    x, y, core = bits_ref[0], bits_ref[1], bits_ref[2]
    for k in range(10):
        at_core = core if k < 5 else 1 - core
        at_x = x if k % 5 in (0, 2) else 1 - x
        at_y = y if k % 5 in (0, 1) else 1 - y
        z0, z1 = {3: (0, 2), 4: (2, 4)}.get(k % 5, (0, 4))
        out[z0:z1, at_y * 4 + at_x * 2 + at_core] = pieces[k][...]


def place_kernel(bits_ref, *refs):
    put_pieces(bits_ref, refs[:10], refs[-1])


def place_dot_kernel(bits_ref, *refs):
    a, w, y = refs[10], refs[11], refs[12]
    put_pieces(bits_ref, refs[:10], w)
    whole = w[...].reshape(a.shape[1], w.shape[3])
    y[...] = dot(a[...], whole).astype(y.dtype)


def piece_specs(pieces, start, block):
    rows = pieces[0].shape[1]
    return [
        (p, pl.BlockSpec((p.shape[0], rows, block), lambda j, _: (0, 0, start // block + j)))
        for p in pieces
    ]


def place_out(rows, width, block):
    return (
        shaped((4, 8, rows, width), BF),
        pl.BlockSpec((4, 8, rows, block), lambda j, _: (0, 0, 0, j)),
    )


def place(pieces, start, width, bits, deps=()):
    rows = pieces[0].shape[1]
    block = min(width, 512)
    out = run(
        place_kernel,
        (width // block,),
        piece_specs(pieces, start, block),
        [place_out(rows, width, block)],
        prefetch=(bits,),
        deps=deps,
        cost=costs(0, 4 * 32 * rows * width),
        name="place",
    )
    return out.reshape(32 * rows, width)


def place_dot(pieces, start, width, bits, a, dtype, deps=()):
    rows, block = pieces[0].shape[1], 512
    whole = pl.BlockSpec(a.shape, lambda j, _: (0, 0))
    w, y = run(
        place_dot_kernel,
        (width // block,),
        piece_specs(pieces, start, block) + [(a, whole)],
        [
            place_out(rows, width, block),
            (
                shaped((a.shape[0], width), dtype),
                pl.BlockSpec((a.shape[0], block), lambda j, _: (0, j)),
            ),
        ],
        prefetch=(bits,),
        deps=deps,
        cost=costs(2 * a.shape[0] * 32 * rows * width, 4 * 32 * rows * width),
        name="place_dot",
    )
    return w.reshape(32 * rows, width), y


def store_rows(value, outs):
    near = outs[0].shape[0]
    half = outs[1].shape[0]
    columns = value.shape[1]
    outs[0][:, :columns] = value[:near]
    outs[1][:, :columns] = value[near : near + half]
    outs[2][:, :columns] = value[near + half :]


def row_outs(rows, columns, block):
    return [
        (shaped((r, columns), BF), pl.BlockSpec((r, block), lambda j, *_: (0, j)))
        for r in (rows * 3 // 4, rows // 8, rows // 8)
    ]


def wgrad_kernel(starts, extra, *refs):
    outs = refs[-3:]
    j = pl.program_id(0)
    for s in range(len(starts) - 1):
        a, a2, g, g2 = refs[4 * s : 4 * s + 4]

        @pl.when((j >= starts[s]) & (j < starts[s + 1]))
        def _(a=a, a2=a2, g=g, g2=g2):
            store_rows((dot(a[...], g[...]) + dot(a2[...], g2[...])).astype(BF), outs)

    if extra:

        @pl.when(j == starts[-1])
        def _():
            mine, theirs = refs[-5], refs[-4]
            store_rows((mine[...].astype(F32) + theirs[...].astype(F32)).astype(BF), outs)


def wgrad(segments, extra=(), deps=(), block=1024):
    starts, ins = [0], []
    for a, a2, g, g2, *span in segments:
        per = g.shape[2] // block
        first, end = span or (0, g.shape[0] * per)
        count, start = end - first, starts[-1]

        def at(j, start=start, count=count, per=per, first=first):
            k = first + jnp.clip(j - start, 0, count - 1)
            return (k // per, 0, k % per)

        whole = pl.BlockSpec(a.shape, lambda j: (0, 0))
        grads = pl.BlockSpec((None, g.shape[1], block), at)
        ins += [(a, whole), (a2, whole), (g, grads), (g2, grads)]
        starts.append(start + count)
    rows = segments[0][0].shape[0]
    columns = starts[-1] * block
    steps = starts[-1]
    if extra:
        ins += [(e, pl.BlockSpec(e.shape, lambda j: (0, 0))) for e in extra]
        columns += extra[0].shape[1]
        steps += 1
    return run(
        functools.partial(wgrad_kernel, tuple(starts), bool(extra)),
        (steps,),
        ins,
        row_outs(rows, columns, block),
        deps=deps,
        cost=costs(2 * rows * 1024 * columns, 4 * 512 * columns + 2 * rows * columns),
        name="wgrad",
    )


def wgrad_down_kernel(bits_ref, *refs):
    blocks, other, dy, dy2 = refs[:4], refs[4:8], refs[8], refs[9]
    mine = jnp.concatenate([r[...].T for r in blocks], axis=0)
    theirs = jnp.concatenate([r[...].T for r in other], axis=0)
    store_rows((dot(mine, dy[...]) + dot(theirs, dy2[...])).astype(BF), refs[10:])


def wgrad_down(bits, g, g_other, dy, dy_other, cuts):
    tokens, d = dy.shape

    def spec(rel, whole):
        def at(b, bits_ref):
            x = bits_ref[0] ^ (rel & 1)
            y = bits_ref[1] ^ (rel >> 1)
            block = b * 4 + y * 2 + x
            return (0, block * 2 + bits_ref[2] if whole else block)

        return pl.BlockSpec((tokens, 128), at)

    rows = pl.BlockSpec((tokens, d), lambda b, _: (0, 0))
    return run(
        wgrad_down_kernel,
        (cuts,),
        [(g, spec(r, True)) for r in range(4)]
        + [(g_other, spec(r, False)) for r in range(4)]
        + [(dy, rows), (dy_other, rows)],
        row_outs(512, cuts * d, d),
        prefetch=(bits,),
        cost=costs(2 * 512 * 1024 * cuts * d, 16 * tokens * d),
        name="wgrad_down",
    )


def up_kernel(bits_ref, *refs):
    h_ref, w_ref, g_ref, slope_ref, send_ref = refs[10:]
    put_pieces(bits_ref, refs[:10], w_ref)
    u = dot(h_ref[...], w_ref[...].reshape(h_ref.shape[1], w_ref.shape[3]))
    cdf = 0.5 * (1.0 + lax.erf(u * (0.5**0.5)))
    g = (u * cdf).astype(BF)
    g_ref[...] = g
    slope_ref[...] = (cdf + u * (jnp.exp(-0.5 * u * u) * 0.3989422804014327)).astype(BF)
    core = bits_ref[2]
    for k in range(0, g.shape[1], 256):
        send_ref[:, k // 2 : k // 2 + 128] = jnp.where(
            core == 0, g[:, k + 128 : k + 256], g[:, k : k + 128]
        )


def feed_up(bits, h, pieces, ff, deps=(), block=512):
    tokens, d = h.shape
    rows = pieces[0].shape[1]
    out = (shaped((tokens, ff), BF), pl.BlockSpec((tokens, block), lambda j, _: (0, j)))
    w, *rest = run(
        up_kernel,
        (ff // block,),
        piece_specs(pieces, 0, block) + [(h, pl.BlockSpec((tokens, d), lambda j, _: (0, 0)))],
        [
            place_out(rows, ff, block),
            out,
            out,
            (
                shaped((tokens, ff // 2), BF),
                pl.BlockSpec((tokens, block // 2), lambda j, _: (0, j)),
            ),
        ],
        prefetch=(bits,),
        deps=deps,
        cost=costs(2 * tokens * d * ff, 4 * d * ff + 4 * tokens * ff, 2 * tokens * ff),
        name="feed_up",
    )
    return w.reshape(d, ff), *rest


def down_kernel(g_ref, w_ref, x_ref, out_ref):
    @pl.when(pl.program_id(0) == 0)
    def _():
        out_ref[...] = x_ref[...]

    out_ref[...] += dot(g_ref[...], w_ref[...])


def feed_down(g, w, x, cuts, deps=()):
    tokens, d = x.shape
    block = d // 2
    whole = pl.BlockSpec((tokens, d), lambda j: (0, 0))
    return run(
        down_kernel,
        (2 * cuts,),
        [
            (g, pl.BlockSpec((tokens, block), lambda j: (0, j))),
            (w, pl.BlockSpec((block, d), lambda j: (j % 2, j // 2))),
            (x, whole),
        ],
        [(shaped((tokens, d), F32), whole)],
        deps=deps,
        cost=costs(2 * tokens * d * d * cuts, 2 * d * d * cuts + 10 * tokens * d),
        name="feed_down",
    )


def norm_back_store(acc, x_ref, gain_ref, res_ref, dx_ref, low_ref, sums_ref):
    gain_grad, bias_grad = 0.0, 0.0
    step = 128
    for r in range(0, x_ref.shape[0], step):
        part = slice(r, r + step)
        x, dh = x_ref[part, :], acc[part, :]
        center = x - jnp.mean(x, -1, keepdims=True)
        inverse = lax.rsqrt(jnp.mean(center * center, -1, keepdims=True) + 1e-05)
        unit = center * inverse
        gain_grad += jnp.sum(dh * unit, axis=0, keepdims=True)
        bias_grad += jnp.sum(dh, axis=0, keepdims=True)
        scaled = dh * gain_ref[...]
        mean_a = jnp.mean(scaled, -1, keepdims=True)
        mean_b = jnp.mean(scaled * unit, -1, keepdims=True)
        dx = res_ref[part, :] + inverse * (scaled - mean_a - unit * mean_b)
        dx_ref[part, :] = dx
        if low_ref is not None:
            low_ref[part, :] = dx.astype(BF)
    sums_ref[0:1, :] = gain_grad
    sums_ref[1:2, :] = bias_grad


def accumulate(acc, part):
    j = pl.program_id(0)

    @pl.when(j == 0)
    def _():
        acc[...] = part

    @pl.when(j > 0)
    def _():
        acc[...] += part


def feed_back_kernel(
    dy_ref, w2_ref, slope_ref, w1_ref, x_ref, gain_ref, res_ref, du_ref, dx_ref, low_ref, sums_ref, acc
):
    du = (dot_nt(dy_ref[...], w2_ref[...]) * slope_ref[...].astype(F32)).astype(BF)
    du_ref[...] = du
    accumulate(acc, dot_nt(du, w1_ref[...]))

    @pl.when(pl.program_id(0) == pl.num_programs(0) - 1)
    def _():
        norm_back_store(acc, x_ref, gain_ref, res_ref, dx_ref, low_ref, sums_ref)


def feed_back(dy, w2, slope, w1, x, gain, res, cuts, deps=()):
    tokens, d = x.shape
    block = d // 2
    ff = w1.shape[1]
    whole = pl.BlockSpec((tokens, d), lambda j: (0, 0), pipeline_mode=pl.Buffered(1))
    part = pl.BlockSpec((tokens, block), lambda j: (0, j))
    return run(
        feed_back_kernel,
        (2 * cuts,),
        [
            (dy, whole),
            (w2, pl.BlockSpec((block, d), lambda j: (j % 2, j // 2))),
            (slope, part),
            (w1, pl.BlockSpec((d, block), lambda j: (0, j))),
            (x, whole),
            (gain, pl.BlockSpec((1, d), lambda j: (0, 0))),
            (res, whole),
        ],
        [
            (shaped((tokens, ff), BF), part),
            (shaped((tokens, d), F32), whole),
            (shaped((tokens, d), BF), whole),
            (shaped((2, d), F32), pl.BlockSpec((2, d), lambda j: (0, 0))),
        ],
        scratch=[pltpu.VMEM((tokens, d), F32)],
        deps=deps,
        cost=costs(4 * tokens * d * ff, 4 * d * ff + 4 * tokens * ff + 16 * tokens * d),
        name="feed_back",
    )


def norm_back_kernel(g_ref, w_ref, x_ref, gain_ref, res_ref, *refs):
    dx_ref, sums_ref, acc = refs[0], refs[-2], refs[-1]
    low_ref = refs[1] if len(refs) == 4 else None
    accumulate(acc, dot_nt(g_ref[...], w_ref[...]))

    @pl.when(pl.program_id(0) == pl.num_programs(0) - 1)
    def _():
        norm_back_store(acc, x_ref, gain_ref, res_ref, dx_ref, low_ref, sums_ref)


def through_norm(g, w, x, gain, res, low=True, deps=()):
    tokens, d = x.shape
    block = 512
    per = g.shape[2] // block
    count = g.shape[0] * per
    whole = pl.BlockSpec((tokens, d), lambda j: (0, 0), pipeline_mode=pl.Buffered(1))
    outs = [(shaped((tokens, d), F32), whole)]
    if low:
        outs.append((shaped((tokens, d), BF), whole))
    outs.append((shaped((2, d), F32), pl.BlockSpec((2, d), lambda j: (0, 0))))
    return run(
        norm_back_kernel,
        (count,),
        [
            (g, pl.BlockSpec((None, tokens, block), lambda j: (j // per, 0, j % per))),
            (w, pl.BlockSpec((d, block), lambda j: (0, j))),
            (x, whole),
            (gain, pl.BlockSpec((1, d), lambda j: (0, 0))),
            (res, whole),
        ],
        outs,
        scratch=[pltpu.VMEM((tokens, d), F32)],
        deps=deps,
        cost=costs(2 * tokens * d * block * count, 2 * d * block * count + 16 * tokens * d),
        name="through_norm",
    )


def scatter_far(grads):
    return swap(grads[1], XBIT), swap(grads[2], YBIT)


def pass_on_kernel(x_ref, y_ref, from_x, from_y, to_x, to_y):
    half = from_x.shape[0]
    to_x[:half] = x_ref[:half]
    to_x[half:] = x_ref[half:] + from_y[...]
    to_y[:half] = y_ref[:half] + from_x[...]
    to_y[half:] = y_ref[half:]


def sum_kernel(own, got_x, got_y, out):
    total = own[...].astype(F32) + got_x[...].astype(F32) + got_y[...].astype(F32)
    out[...] = total.astype(out.dtype)


def column_blocks(columns):
    return columns if columns <= 2304 else next(b for b in (2048, 1024, 640) if columns % b == 0)


def rows_spec(rows, block, at=0):
    return pl.BlockSpec((rows, block), lambda j: (at, j))


def scatter_near(near, far):
    rows, columns = near.shape[0] // 3, near.shape[1]
    block = column_blocks(columns)
    far_spec, out = rows_spec(rows // 2, block), (shaped((rows, columns), BF), rows_spec(rows, block))
    to_x, to_y = run(
        pass_on_kernel,
        (columns // block,),
        [
            (near, rows_spec(rows, block, 1)),
            (near, rows_spec(rows, block, 2)),
            (far[0], far_spec),
            (far[1], far_spec),
        ],
        [out, out],
        cost=costs(rows * columns, 10 * rows * columns),
        name="pass_on",
    )
    return swap(to_x, XBIT), swap(to_y, YBIT)


def plane_sum(near, got, dtype):
    rows, columns = got[0].shape
    block = column_blocks(columns)
    return run(
        sum_kernel,
        (columns // block,),
        [(a, rows_spec(rows, block)) for a in (near, *got)],
        [(shaped((rows, columns), dtype), rows_spec(rows, block))],
        cost=costs(2 * rows * columns, 8 * rows * columns),
        name="plane_sum",
    )


def scatter_line(near, got):
    total = plane_sum(near, got, BF)
    return lax.psum_scatter(total, "gx", scatter_dimension=0, tiled=True)


def scatter_line_direct(near, got, z):
    total = plane_sum(near, got, F32)
    total = total.reshape(4, -1, total.shape[1])
    low = total.astype(BF)
    own = lax.dynamic_index_in_dim(total, z, 0, keepdims=False)
    for step in (1, 2, 3):
        part = lax.dynamic_index_in_dim(low, (z + step) % 4, 0, keepdims=False)
        came = lax.ppermute(part, ALL, [(i, (i + 8 * step) % 32) for i in range(32)])
        own = own + came.astype(F32)
    return own


def turn_kernel(select_ref, a_ref, mine, theirs):
    rows = dot_nt(select_ref[...], a_ref[...]).astype(BF)
    half = pl.num_programs(0) // 2

    @pl.when(pl.program_id(0) < half)
    def _():
        mine[...] = rows

    @pl.when(pl.program_id(0) >= half)
    def _():
        theirs[...] = rows


def turn(select, a):
    tokens, d = a.shape
    steps = 4
    block, half = d // steps, steps // 2
    out = shaped((d // 2, tokens), BF)
    return run(
        turn_kernel,
        (steps,),
        [
            (select, pl.BlockSpec((block, d), lambda j: (j, 0))),
            (a, pl.BlockSpec((tokens, d), lambda j: (0, 0))),
        ],
        [
            (out, pl.BlockSpec((block, tokens), lambda j: (jnp.minimum(j, half - 1), 0))),
            (out, pl.BlockSpec((block, tokens), lambda j: (jnp.maximum(j - half, 0), 0))),
        ],
        cost=costs(2 * d * d * tokens, 2 * d * d + 4 * d * tokens),
        name="turn",
    )


def hidden_order_kernel(to_hidden, rows, cuts, src, out):
    lines = 4
    width = lines * cuts * rows
    at = lax.broadcasted_iota(jnp.int32, (width, width), 0)
    to = lax.broadcasted_iota(jnp.int32, (width, width), 1)
    first, second = (lines, cuts) if to_hidden else (cuts, lines)
    moved = (at // rows % second * first + at // (rows * second)) * rows + at % rows
    swap_two = (moved == to).astype(F32).astype(BF)
    for place_at in range(8):
        if to_hidden:
            step, parts, wide = cuts * rows, lines, cuts * rows
        else:
            step, parts, wide = lines * rows, cuts, lines * rows
        pieces = [
            src[:, (k * 8 + place_at) * step : (k * 8 + place_at) * step + wide]
            for k in range(parts)
        ]
        done = dot(jnp.concatenate(pieces, axis=1), swap_two)
        out_step = lines * rows if to_hidden else cuts * rows
        for k in range(cuts if to_hidden else lines):
            at_column = (k * 8 + place_at) * out_step
            out[:, at_column : at_column + out_step] = done[
                :, k * out_step : (k + 1) * out_step
            ].astype(out.dtype)


def hidden_order(a, to_hidden, cuts, dtype):
    rows, ff = a.shape
    whole = pl.BlockSpec((rows, ff), lambda j: (0, 0))
    return run(
        functools.partial(hidden_order_kernel, to_hidden, ff // 32 // cuts, cuts),
        (1,),
        [(a, whole)],
        [(shaped((rows, ff), dtype), whole)],
        cost=costs(2 * rows * ff * 512, 6 * rows * ff),
        name="hidden_order",
    )


def memory_grad_kernel(g_ref, w_ref, out_ref):
    part = dot_nt(g_ref[...], w_ref[...])[: out_ref.shape[0]]

    @pl.when(pl.program_id(0) == 0)
    def _():
        out_ref[...] = part

    @pl.when(pl.program_id(0) > 0)
    def _():
        out_ref[...] += part


def memory_grad(g, w, rows):
    _, padded, d = g.shape
    block = d // 2
    return run(
        memory_grad_kernel,
        (4,),
        [
            (g, pl.BlockSpec((None, padded, block), lambda j: (j // 2, 0, j % 2))),
            (w, pl.BlockSpec((d, block), lambda j: (0, j))),
        ],
        [(shaped((rows, d), F32), pl.BlockSpec((rows, d), lambda j: (0, 0)))],
        cost=costs(4 * padded * d * d, 8 * d * d + 4 * rows * d),
        name="memory_grad",
    )


def shards_plane(
    hidden,
    memory,
    lengths,
    page_class,
    cotangent,
    w_self_qkv,
    w_self_out,
    w_cross_q,
    w_cross_kv,
    w_cross_out,
    w_fc1,
    w_fc2,
    norm_gains,
    norm_biases,
):
    tokens, d = hidden.shape
    rows, ff = w_fc1.shape
    cuts = w_fc2.shape[0] // rows
    mem_rows = -(-memory.shape[0] // 16) * 16
    slots_used = jnp.where(page_class == 0, MEM_BIG, MEM_BIG // 4).astype(jnp.int32)
    along = lax.axis_index("gy")
    x_at, y_at, core = (along // 2) % 2, along // 4, along % 2
    z_at = lax.axis_index("gx")
    bits = jnp.stack([x_at, y_at, core]).astype(jnp.int32)

    norm_cols = jnp.concatenate([norm_gains, norm_biases], axis=0).T
    norm_cols = jnp.pad(norm_cols, ((0, 0), (0, 128 - norm_cols.shape[1])))
    up_local = hidden_order(w_fc1, True, cuts, BF)
    down_local = jnp.concatenate(
        [w_fc2[c * rows : (c + 1) * rows] for c in range(cuts)], axis=1
    )
    place_at = jnp.arange(d)
    r = place_at % rows
    z = (place_at // rows) % 4
    rel = (place_at // (4 * rows)) % 4
    source_core = core ^ (place_at // (16 * rows))
    device = z * 8 + (y_at ^ (rel // 2)) * 4 + (x_at ^ (rel % 2)) * 2 + source_core
    select = ((device * rows + r)[:, None] == place_at[None, :]).astype(BF)

    def turned(a):
        mine, theirs = turn(select, a)
        return mine, swap(theirs, CORE)

    pack1 = jnp.concatenate([w_self_qkv, norm_cols], axis=1)
    pack2 = jnp.concatenate([w_cross_kv, w_self_out, w_cross_q, w_cross_out], axis=1)
    blocks = d // PAIR
    memory_pad = jnp.pad(memory, ((0, mem_rows - memory.shape[0]), (0, 0)))

    line1, pack2, memory_pad, hidden = fence(gather_line(pack1), pack2, memory_pad, hidden)

    line2 = gather_line(pack2)
    near1 = gather_near(line1)
    mem_t = turned(memory_pad)
    unit1, _ = norm_parts(hidden)
    near1, mem_t, unit1 = fence(near1, mem_t, unit1)

    near1, far1, cores1, line2, pack3 = fence(
        near1, gather_far(near1), swap_cores(near1), line2, up_local
    )

    line3 = gather_line(pack3)
    near2 = gather_near(line2)
    first = near1 + far1 + cores1 + swap_cores(far1)
    norms = place(first, 3 * d, 128, bits)[:, :6].T.astype(F32)
    gains, biases = norms[:3], norms[3:]
    h1 = (unit1 * gains[0] + biases[0]).astype(BF)
    wqkv, qkv = place_dot(first, 0, 3 * d, bits, h1, BF)
    o, lse = attn_fwd((qkv, 0), qkv, blocks, 2 * blocks, lengths, True)
    near2, o, h1, gains, biases = fence(near2, o, h1, gains, biases)

    near2, far2, cores2, h1, o, line3, pack4 = fence(
        near2, gather_far(near2), swap_cores(near2), h1, o, line3, down_local
    )

    wdown = lax.all_gather(pack4, ("gy", "gx"), axis=0, tiled=True)
    near3 = gather_near(line3)
    second = near2 + far2 + cores2 + swap_cores(far2)
    wso, y1 = place_dot(second, 2 * d, d, bits, o, F32)
    x1 = hidden + y1
    unit2, _ = norm_parts(x1)
    h2 = (unit2 * gains[1] + biases[1]).astype(BF)
    wcq, qc = place_dot(second, 3 * d, d, bits, h2, BF)
    wckv, kvc = place_dot(second, 0, 2 * d, bits, memory_pad, BF)
    h1_t, o_t = turned(h1), turned(o)
    near3, second, qc, kvc, h2, x1, h1_t, o_t = fence(
        near3, second, qc, kvc, h2, x1, h1_t, o_t
    )

    far3, cores3 = gather_far(near3), swap_cores(near3)
    o2, lse2 = attn_fwd((qc, 0), kvc, 0, blocks, slots_used, False)
    near3, far3, cores3, o2, h2, cotangent = fence(near3, far3, cores3, o2, h2, cotangent)

    third = near3 + far3 + cores3 + swap_cores(far3)
    wco, y2 = place_dot(second, 4 * d, d, bits, o2, F32)
    x2 = x1 + y2
    unit3, _ = norm_parts(x2)
    h3 = (unit3 * gains[2] + biases[2]).astype(BF)
    valid = (jnp.arange(tokens) < lengths[0])[:, None].astype(F32)
    dout = cotangent * valid
    dy3 = dout.astype(BF)
    dy3_other = swap(dy3, CORE)
    third, h3, x2, o2, dout, dy3, dy3_other = fence(third, h3, x2, o2, dout, dy3, dy3_other)

    wup, g, slope, g_send = feed_up(bits, h3, third, ff)
    wup, g, slope, g_send, h3, o2 = fence(wup, g, slope, g_send, h3, o2)

    h2_t, h3_t, o2_t = turned(h2), turned(h3), turned(o2)
    g_other, h2_t, h3_t, o2_t, g = fence(swap(g_send, CORE), h2_t, h3_t, o2_t, g)

    grad_down = wgrad_down(bits, g, g_other, dy3, dy3_other, cuts)
    grad_down, dy3, slope, wdown = fence(grad_down, dy3, slope, wdown)

    du, dx2, dy2, sums3 = feed_back(dy3, wdown, slope, wup, x2, gains[2:3], dout, cuts)
    far1, du, dx2, dy2, g = fence(scatter_far(grad_down), du, dx2, dy2, g)

    got1 = scatter_near(grad_down[0], far1)
    do2 = dot_nt(dy2, wco).astype(BF)
    du_other, do2, du = fence(swap(du, CORE), do2, du)

    grad_up = wgrad([h3_t + (du[None], du_other[None])])
    grad_up, do2, dy2 = fence(grad_up, do2, dy2)

    dqc, dkvc = attn_bwd((qc, 0), kvc, 0, blocks, o2, do2, lse2, slots_used, False)
    far2, got1, dqc, dkvc, dy2_other, dx2 = fence(
        scatter_far(grad_up), got1, dqc, dkvc, swap(dy2, CORE), dx2
    )

    own_down = scatter_line(grad_down[0], got1)
    got2 = scatter_near(grad_up[0], far2)
    dx1, dy1, sums2 = through_norm(dqc, wcq, x1, gains[1:2], dx2)
    do = dot_nt(dy1, wso).astype(BF)
    dqc_other, dkvc_other, dx1, dy1, do, dqc, dkvc = fence(
        swap(dqc, CORE), swap(dkvc, CORE), dx1, dy1, do, dqc, dkvc
    )

    grad_mid = wgrad(
        [
            o2_t + (dy2[None], dy2_other[None]),
            h2_t + (dqc, dqc_other),
            mem_t + (dkvc, dkvc_other),
        ]
    )
    grad_mid, do, dy1 = fence(grad_mid, do, dy1)

    dqkv = attn_bwd((qkv, 0), qkv, blocks, 2 * blocks, o, do, lse, lengths, True)
    far3, dy1_other, dqkv, got2, dx1 = fence(
        scatter_far(grad_mid), swap(dy1, CORE), dqkv, got2, dx1
    )

    own_up = scatter_line(grad_up[0], got2)
    got3 = scatter_near(grad_mid[0], far3)
    grad_hidden, sums1 = through_norm(dqkv, wqkv, hidden, gains[0:1], dx1, low=False)
    sums = jnp.concatenate([sums1, sums2, sums3], axis=0)
    sums = jnp.pad(sums, ((0, 122), (0, 0))).astype(BF)
    dqkv_other, grad_hidden, sums_t = fence(swap(dqkv, CORE), grad_hidden, turned(sums))

    grad_a = wgrad(
        [o_t + (dy1[None], dy1_other[None]), h1_t + (dqkv, dqkv_other, 0, 1)]
    )
    grad_a, dqkv, dqkv_other, sums_t = fence(grad_a, dqkv, dqkv_other, sums_t)

    grad_b = wgrad([h1_t + (dqkv, dqkv_other, 1, 3)], extra=sums_t)
    far_a, grad_b, got3, dkvc, own_down = fence(
        scatter_far(grad_a), grad_b, got3, dkvc, own_down
    )

    got_a = scatter_near(grad_a[0], far_a)
    own_mid = scatter_line(grad_mid[0], got3)
    grad_memory = memory_grad(dkvc, wckv, memory.shape[0])
    far_b, got_a, grad_memory, own_up, g = fence(
        scatter_far(grad_b), got_a, grad_memory, own_up, g
    )

    got_b = scatter_near(grad_b[0], far_b)
    own_a = scatter_line_direct(grad_a[0], got_a, z_at)
    own_up = hidden_order(own_up, False, cuts, F32)
    result = feed_down(g, wdown, x2, cuts)
    got_b, own_a, own_up, result = fence(got_b, own_a, own_up, result)

    own_b = scatter_line_direct(grad_b[0], got_b, z_at)
    own_qkv = jnp.concatenate([own_a[:, d:], own_b[:, : 2 * d]], axis=1)
    own_down = jnp.concatenate(
        [own_down[:, c * d : (c + 1) * d] for c in range(cuts)], axis=0
    )
    own_sums = own_b[:, 2 * d : 2 * d + 6].T
    return (
        result,
        grad_hidden,
        grad_memory,
        own_qkv,
        own_a[:, :d],
        own_mid[:, d : 2 * d].astype(F32),
        own_mid[:, 2 * d :].astype(F32),
        own_mid[:, :d].astype(F32),
        own_up,
        own_down.astype(F32),
        own_sums[0::2],
        own_sums[1::2],
    )


def solution(mesh):
    row = P(ALL, None)
    col = P(None, ALL)
    nx, ny = mesh.shape["gx"], mesh.shape["gy"]
    body = shards_plane if (nx, ny) == (4, 8) else functools.partial(shards_any, nx=nx, ny=ny)
    return jax.shard_map(
        body,
        mesh=mesh,
        in_specs=(row, row, P(ALL), P(ALL), row) + (row,) * 7 + (col, col),
        out_specs=(row,) * 10 + (col, col),
        check_vma=False,
    )
```

profile of v0, /device:TPU:0, one launch (start us, length us, event | category | flops | bytes accessed | tf_op | source)
XLA Modules:
  0.0 438.1 jit_solution(3477764176013636309)
XLA Ops:
  9.1 22.1 %all-gather = bf16[128,3200]{1,0:T(8,128)(2,1)} all-gather(bf16[32,3200]{1,0:T(8,128)(2,1)S(1)} %fusion.11), channel_id=2, replica_groups=mesh['gx'=4,'gy'=8] {'gx'}, dimensions={0}, use_global_device_ids=true | all-gather | bytes 1024000 | tf_op jit(solution)/shard_map/all_gather | solution.py:419
  35.8 2.6 turn.7
  42.1 1.6 subtract_multiply_fusion
  43.6 6.2 %collective-permute-done.refs_2_ = bf16[4,32,3200]{2,1,0:T(8,128)(2,1)} collective-permute-done((bf16[4,32,3200]{2,1,0:T(8,128)(2,1)}, bf16[4,32,3200]{2,1,0:T(8,128)(2,1)}, u32[]{:S(2)}, u32[]{:S(2)}) %collective-permute-start) | collective-permute-done | bytes 819232 | tf_op jit(solution)/shard_map/ppermute | solution.py:411
  51.6 1.8 slice.103
  58.1 8.5 %collective-permute-done.3.refs_4_ = bf16[2,32,3200]{2,1,0:T(8,128)(2,1)} collective-permute-done((bf16[2,32,3200]{2,1,0:T(8,128)(2,1)}, bf16[2,32,3200]{2,1,0:T(8,128)(2,1)}, u32[]{:S(2)}, u32[]{:S(2)}) %collective-permute-start.3) | collective-permute-done | bytes 409632 | tf_op jit(solution)/shard_map/ppermute | solution.py:411
  76.4 2.0 add_convert_fusion.2.refs_11_.refs_1_
  78.5 8.6 %place_dot.5 = (bf16[4,8,32,3072]{3,2,1,0:T(8,128)(2,1)}, bf16[512,3072]{1,0:T(8,128)(2,1)S(1)}) custom-call(s32[3]{0:T(128)S(1)} %pad_add_fusion.refs_0_, bf16[4,32,3200]{2,1,0:T(8,128)(2,1)} %bitcast.1.refs_1_, bf16[4,32,3200]{2,1,0:T(8,128)(2,1)} %collective-permute-done.refs_2_, bf16[4,32,3200]{2,1,0:T(8,128)(2,1)} %collective-permute-done.1.refs_3_, ...), custom_call_target="tpu_custom_call" | custom-call | flops 3221225472 | bytes 12582912 | tf_op jit(solution)/shard_map/place_dot/pallas_call | solution.py:41
  87.1 13.6 %attn_fwd.2 = (bf16[512,1024]{1,0:T(8,128)(2,1)S(1)}, f32[8,2,512]{2,1,0:T(2,128)S(1)}) custom-call(s32[1]{0:T(128)} %copy.58.refs_0_, bf16[512,3072]{1,0:T(8,128)(2,1)S(1)} %get-tuple-element.279.refs_1_.refs_2_.refs_3_, bf16[512,3072]{1,0:T(8,128)(2,1)S(1)} %get-tuple-element.279.refs_1_.refs_2_.refs_3_, ...), custom_call_target="tpu_custom_call" | custom-call | flops 4294967296 | bytes 4194304 | tf_op jit(solution)/shard_map/attn_fwd/pallas_call | solution.py:41
  102.4 2.0 slice.110
  107.4 15.3 %collective-permute-done.12.refs_4_ = bf16[2,32,5120]{2,1,0:T(8,128)(2,1)} collective-permute-done((bf16[2,32,5120]{2,1,0:T(8,128)(2,1)}, bf16[2,32,5120]{2,1,0:T(8,128)(2,1)}, u32[]{:S(2)}, u32[]{:S(2)}) %collective-permute-start.12) | collective-permute-done | bytes 655392 | tf_op jit(solution)/shard_map/ppermute | solution.py:411
  126.1 1.6 copy-done.9
  128.9 2.2 turn.8
  131.1 2.0 turn.9
  134.5 4.0 place_dot.6
  139.6 3.7 place_dot.7
  143.3 6.4 %place_dot.8 = (bf16[4,8,32,2048]{3,2,1,0:T(8,128)(2,1)}, bf16[592,2048]{1,0:T(8,128)(2,1)S(1)}) custom-call(s32[3]{0:T(128)S(1)} %pad_add_fusion.refs_0_, bf16[4,32,5120]{2,1,0:T(8,128)(2,1)} %bitcast.2.refs_1_, bf16[4,32,5120]{2,1,0:T(8,128)(2,1)S(1)} %collective-permute-done.8.refs_2_, bf16[4,32,5120]{2,1,0:T(8,128)(2,1)} %collective-permute-done.9.refs_3_, ...), custom_call_target="tpu_custom_call" | custom-call | flops 2483027968 | bytes 8388608 | tf_op jit(solution)/shard_map/place_dot/pallas_call | solution.py:41
  154.9 17.6 %attn_fwd.3 = (bf16[512,1024]{1,0:T(8,128)(2,1)S(1)}, f32[8,2,512]{2,1,0:T(2,128)S(1)}) custom-call(s32[1]{0:T(128)S(6)} %select_n.140.refs_0_, bf16[512,1024]{1,0:T(8,128)(2,1)S(1)} %get-tuple-element.312.refs_1_, bf16[592,2048]{1,0:T(8,128)(2,1)S(1)} %get-tuple-element.313.refs_2_.refs_3_, bf16[592,2048]{1,0:T(8,128)(2,1)S(1)} %get-tuple-element.313.refs_2_.refs_3_), custom_call_target="tpu_custom_call" | custom-call | flops 4966055936 | bytes 4194304 | tf_op jit(solution)/shard_map/attn_fwd/pallas_call | solution.py:41
  172.6 1.6 fusion.41
  174.8 4.4 place_dot.9
  180.8 12.1 %feed_up.1 = (bf16[4,8,32,4096]{3,2,1,0:T(8,128)(2,1)}, bf16[512,4096]{1,0:T(8,128)(2,1)}, bf16[512,4096]{1,0:T(8,128)(2,1)}, bf16[512,2048]{1,0:T(8,128)(2,1)S(1)}) custom-call(s32[3]{0:T(128)S(1)} %pad_add_fusion.refs_0_, bf16[4,32,4096]{2,1,0:T(8,128)(2,1)S(1)} %bitcast.79, bf16[4,32,4096]{2,1,0:T(8,128)(2,1)S(1)} %collective-permute-done.17.refs_2_, ...), custom_call_target="tpu_custom_call" | custom-call | flops 4294967296 | bytes 25165824 | tf_op jit(solution)/shard_map/feed_up/pallas_call | solution.py:41
  193.3 2.0 turn.10
  196.2 2.0 turn.12
  198.8 2.0 turn.11
  201.6 1.9 collective-permute-done.33.refs_1_
  204.3 8.3 %wgrad_down.1 = (bf16[384,4096]{1,0:T(8,128)(2,1)}, bf16[64,4096]{1,0:T(8,128)(2,1)}, bf16[64,4096]{1,0:T(8,128)(2,1)}) custom-call(s32[3]{0:T(128)S(1)} %pad_add_fusion.refs_0_, bf16[512,4096]{1,0:T(8,128)(2,1)S(1)} %copy-done, bf16[512,4096]{1,0:T(8,128)(2,1)S(1)} %copy-done, bf16[512,4096]{1,0:T(8,128)(2,1)S(1)} %copy-done, ...), custom_call_target="tpu_custom_call" | custom-call | flops 4294967296 | bytes 8388608 | tf_op jit(solution)/shard_map/wgrad_down/pallas_call | solution.py:41
  212.6 1.8 collective-permute-start.35
  216.1 20.1 %feed_back.1 = (bf16[512,4096]{1,0:T(8,128)(2,1)}, f32[512,1024]{1,0:T(8,128)}, bf16[512,1024]{1,0:T(8,128)(2,1)S(1)}, f32[2,1024]{1,0:T(2,128)S(1)}) custom-call(bf16[512,1024]{1,0:T(8,128)(2,1)S(1)} %copy-done.16, bf16[1024,4096]{1,0:T(8,128)(2,1)} %all-gather.7.cloned.1.call-done.refs_1_, bf16[512,4096]{1,0:T(8,128)(2,1)} %get-tuple-element.382.refs_2_, ...), custom_call_target="tpu_custom_call" | custom-call | flops 8589934592 | bytes 33554432 | tf_op jit(solution)/shard_map/feed_back/pallas_call | solution.py:41
  237.3 2.3 pass_on.5
  241.6 2.3 convolution_convert_fusion.1.refs_5_
  244.4 6.8 %wgrad.4 = (bf16[384,4096]{1,0:T(8,128)(2,1)}, bf16[64,4096]{1,0:T(8,128)(2,1)}, bf16[64,4096]{1,0:T(8,128)(2,1)}) custom-call(bf16[512,512]{1,0:T(8,128)(2,1)S(1)} %copy-done.67, bf16[512,512]{1,0:T(8,128)(2,1)S(1)} %copy-done.61, bf16[1,512,4096]{2,1,0:T(8,128)(2,1)S(1)} %bitcast.74, bf16[1,512,4096]{2,1,0:T(8,128)(2,1)S(1)} %bitcast.75), custom_call_target="tpu_custom_call" | custom-call | flops 4294967296 | bytes 12582912 | tf_op jit(solution)/shard_map/wgrad/pallas_call | solution.py:41
  251.3 1.8 collective-permute-start.38
  254.7 18.0 %attn_bwd.2 = (bf16[1,512,1024]{2,1,0:T(8,128)(2,1)S(1)}, bf16[2,592,1024]{2,1,0:T(8,128)(2,1)}) custom-call(s32[1]{0:T(128)S(6)} %select_n.140.refs_0_, bf16[512,1024]{1,0:T(8,128)(2,1)S(1)} %copy-done.51, bf16[592,2048]{1,0:T(8,128)(2,1)S(1)} %copy-done.48, bf16[592,2048]{1,0:T(8,128)(2,1)S(1)} %copy-done.48, bf16[512,1024]{1,0:T(8,128)(2,1)S(1)} %copy-done.25, ...), custom_call_target="tpu_custom_call" | custom-call | flops 12415139840 | bytes 8388608 | tf_op jit(solution)/shard_map/attn_bwd/pallas_call | solution.py:41
  272.8 2.8 collective-permute-done.38.refs_2_
  277.9 2.2 copy.53.refs_9_
  280.0 3.1 pass_on.6
  285.7 4.7 %through_norm.2 = (f32[512,1024]{1,0:T(8,128)S(1)}, bf16[512,1024]{1,0:T(8,128)(2,1)}, f32[2,1024]{1,0:T(2,128)S(1)}) custom-call(bf16[1,512,1024]{2,1,0:T(8,128)(2,1)S(1)} %get-tuple-element.421.refs_0_.refs_6_, bf16[1024,1024]{1,0:T(8,128)(2,1)S(1)} %bitcast.69, f32[512,1024]{1,0:T(8,128)S(1)} %copy-done.4, f32[1,1024]{1,0:T(1,128)S(1)} %get-tuple-element.574.refs_3_, ...), custom_call_target="tpu_custom_call" | custom-call | flops 1073741824 | bytes 10485760 | tf_op jit(solution)/shard_map/through_norm/pallas_call | solution.py:41
  290.5 4.3 convolution_convert_fusion.refs_5_
  294.9 9.5 %wgrad.5 = (bf16[384,4096]{1,0:T(8,128)(2,1)}, bf16[64,4096]{1,0:T(8,128)(2,1)}, bf16[64,4096]{1,0:T(8,128)(2,1)}) custom-call(bf16[512,512]{1,0:T(8,128)(2,1)S(1)} %copy-done.65, bf16[512,512]{1,0:T(8,128)(2,1)S(1)} %copy-done.59, bf16[1,512,1024]{2,1,0:T(8,128)(2,1)S(1)} %bitcast.80, bf16[1,512,1024]{2,1,0:T(8,128)(2,1)S(1)} %bitcast.81, ...), custom_call_target="tpu_custom_call" | custom-call | flops 4294967296 | bytes 12582912 | tf_op jit(solution)/shard_map/wgrad/pallas_call | solution.py:41
  304.4 3.0 plane_sum.5
  309.0 1.9 copy-done.71
  312.3 13.8 %attn_bwd.3.refs_0_.refs_6_.refs_2_ = bf16[3,512,1024]{2,1,0:T(8,128)(2,1)} custom-call(s32[1]{0:T(128)} %copy.58.refs_0_, bf16[512,3072]{1,0:T(8,128)(2,1)S(1)} %copy-done.71, bf16[512,3072]{1,0:T(8,128)(2,1)S(1)} %copy-done.71, bf16[512,3072]{1,0:T(8,128)(2,1)S(1)} %copy-done.71, bf16[512,1024]{1,0:T(8,128)(2,1)S(1)} %copy-done.23, ...), custom_call_target="tpu_custom_call" | custom-call | flops 10737418240 | bytes 8388608 | tf_op jit(solution)/shard_map/attn_bwd/pallas_call | solution.py:41
  326.1 2.9 plane_sum.6
  329.1 2.9 pass_on.7
  334.4 2.8 copy-done.12
  337.2 10.0 %through_norm.3 = (f32[512,1024]{1,0:T(8,128)}, f32[2,1024]{1,0:T(2,128)S(1)}) custom-call(bf16[3,512,1024]{2,1,0:T(8,128)(2,1)} %attn_bwd.3.refs_0_.refs_6_.refs_2_, bf16[1024,3072]{1,0:T(8,128)(2,1)S(1)} %bitcast.64, f32[512,1024]{1,0:T(8,128)S(1)} %copy-done.2, f32[1,1024]{1,0:T(1,128)S(1)} %get-tuple-element.572.refs_3_, f32[512,1024]{1,0:T(8,128)S(1)} %copy-done.19), custom_call_target="tpu_custom_call" | custom-call | flops 3221225472 | bytes 14680064 | tf_op jit(solution)/shard_map/through_norm/pallas_call | solution.py:41
  350.0 5.7 %wgrad.6 = (bf16[384,2048]{1,0:T(8,128)(2,1)}, bf16[64,2048]{1,0:T(8,128)(2,1)}, bf16[64,2048]{1,0:T(8,128)(2,1)}) custom-call(bf16[512,512]{1,0:T(8,128)(2,1)S(1)} %copy-done.40, bf16[512,512]{1,0:T(8,128)(2,1)S(1)} %copy-done.42, bf16[1,512,1024]{2,1,0:T(8,128)(2,1)} %bitcast.24.refs_2_, bf16[1,512,1024]{2,1,0:T(8,128)(2,1)} %bitcast.25.refs_3_, ...), custom_call_target="tpu_custom_call" | custom-call | flops 2147483648 | bytes 6291456 | tf_op jit(solution)/shard_map/wgrad/pallas_call | solution.py:41
  357.4 5.2 %wgrad.7 = (bf16[384,2176]{1,0:T(8,128)(2,1)}, bf16[64,2176]{1,0:T(8,128)(2,1)}, bf16[64,2176]{1,0:T(8,128)(2,1)}) custom-call(bf16[512,512]{1,0:T(8,128)(2,1)S(1)} %copy-done.36, bf16[512,512]{1,0:T(8,128)(2,1)S(1)} %copy-done.38, bf16[3,512,1024]{2,1,0:T(8,128)(2,1)} %attn_bwd.3.refs_0_.refs_6_.refs_2_, ...), custom_call_target="tpu_custom_call" | custom-call | flops 2281701376 | bytes 6684672 | tf_op jit(solution)/shard_map/wgrad/pallas_call | solution.py:41
  362.6 1.7 collective-permute-done.52.refs_2_
  366.6 1.7 collective-permute-start.58
  370.7 2.9 plane_sum.9
  375.4 2.2 copy-done.45
  377.6 6.8 %memory_grad.1 = f32[588,1024]{1,0:T(8,128)} custom-call(bf16[2,592,1024]{2,1,0:T(8,128)(2,1)} %get-tuple-element.485.refs_10_.refs_0_, bf16[1024,2048]{1,0:T(8,128)(2,1)S(1)} %bitcast.73), custom_call_target="tpu_custom_call" | custom-call | flops 2483027968 | bytes 10797056 | tf_op jit(solution)/shard_map/memory_grad/pallas_call | solution.py:41
  388.4 1.7 plane_sum.7
  390.3 2.2 collective-permute-start.63
  392.5 1.6 collective-permute-start.64
  397.6 3.4 copy-done.7
  401.0 8.2 %feed_down.1 = f32[512,1024]{1,0:T(8,128)} custom-call(bf16[512,4096]{1,0:T(8,128)(2,1)S(1)} %copy-done.1, bf16[1024,4096]{1,0:T(8,128)(2,1)S(1)} %copy-done.7, f32[512,1024]{1,0:T(8,128)S(1)} %copy-done.6), custom_call_target="tpu_custom_call" | custom-call | flops 4294967296 | bytes 13631488 | tf_op jit(solution)/shard_map/feed_down/pallas_call | solution.py:41
  409.2 1.7 hidden_order.3
  416.3 2.8 collective-permute-start.67
  419.8 1.8 collective-permute-done.65
  421.6 3.9 collective-permute-done.66
  427.8 1.6 slice_convert_fusion.1
  429.4 1.6 slice_convert_fusion
  (387 shorter events, 91.6 us)
Async XLA Ops:
  7.2 60.4 %all-gather.9.cloned.1.call-start = ((), (), s32[]{:S(2)}) async-start(), calls=%async_computation.7 | async-start | bytes 1638400 | tf_op jit(solution)/shard_map/all_gather | solution.py:419
  32.2 17.6 %collective-permute-start = (bf16[4,32,3200]{2,1,0:T(8,128)(2,1)}, bf16[4,32,3200]{2,1,0:T(8,128)(2,1)}, u32[]{:S(2)}, u32[]{:S(2)}) collective-permute-start(bf16[4,32,3200]{2,1,0:T(8,128)(2,1)} %bitcast.1.refs_1_), channel_id=1, source_target_pairs={{0,2},{1,3},{2,0},{3,1},{4,6},{5,7},{6,4},{7,5},{8,10},{9,11},{10,... | collective-permute-start | bytes 2457608 | tf_op jit(solution)/shard_map/ppermute | solution.py:411
  33.7 17.4 %collective-permute-start.1 = (bf16[4,32,3200]{2,1,0:T(8,128)(2,1)}, bf16[4,32,3200]{2,1,0:T(8,128)(2,1)}, u32[]{:S(2)}, u32[]{:S(2)}) collective-permute-start(bf16[4,32,3200]{2,1,0:T(8,128)(2,1)} %bitcast.1.refs_1_), channel_id=1, source_target_pairs={{0,4},{1,5},{2,6},{3,7},{4,0},{5,1},{6,2},{7,3},{8,12},{9,13},{10,... | collective-permute-start | bytes 2457608 | tf_op jit(solution)/shard_map/ppermute | solution.py:411
  35.2 72.2 %all-gather.11.cloned.1.call-start = ((), (), s32[]{:S(2)}) async-start(), calls=%async_computation.8 | async-start | bytes 1310720 | tf_op jit(solution)/shard_map/all_gather | solution.py:419
  51.0 15.6 %collective-permute-start.5 = (bf16[4,32,3200]{2,1,0:T(8,128)(2,1)}, bf16[4,32,3200]{2,1,0:T(8,128)(2,1)S(1)}, u32[]{:S(2)}, u32[]{:S(2)}) collective-permute-start(bf16[4,32,3200]{2,1,0:T(8,128)(2,1)} %bitcast.1.refs_1_), channel_id=1, source_target_pairs={{0,1},{1,0},{2,3},{3,2},{4,5},{5,4},{6,7},{7,6},{8,9},{9,8},{10,11... | collective-permute-start | bytes 2457608 | tf_op jit(solution)/shard_map/ppermute | solution.py:411
  51.0 16.5 %collective-permute-start.6 = (bf16[4,32,3200]{2,1,0:T(8,128)(2,1)}, bf16[4,32,3200]{2,1,0:T(8,128)(2,1)}, u32[]{:S(2)}, u32[]{:S(2)}) collective-permute-start(bf16[4,32,3200]{2,1,0:T(8,128)(2,1)} %collective-permute-done.refs_2_), channel_id=1, source_target_pairs={{0,1},{1,0},{2,3},{3,2},{4,5},{5,4},{6,7},{7,6},{8,9},{9,8},{10,11... | collective-permute-start | bytes 2457608 | tf_op jit(solution)/shard_map/ppermute | solution.py:411
  51.6 16.0 %collective-permute-start.7 = (bf16[4,32,3200]{2,1,0:T(8,128)(2,1)}, bf16[4,32,3200]{2,1,0:T(8,128)(2,1)}, u32[]{:S(2)}, u32[]{:S(2)}) collective-permute-start(bf16[4,32,3200]{2,1,0:T(8,128)(2,1)} %collective-permute-done.1.refs_3_), channel_id=1, source_target_pairs={{0,1},{1,0},{2,3},{3,2},{4,5},{5,4},{6,7},{7,6},{8,9},{9,8},{10,11... | collective-permute-start | bytes 2457608 | tf_op jit(solution)/shard_map/ppermute | solution.py:411
  54.4 12.3 %collective-permute-start.3 = (bf16[2,32,3200]{2,1,0:T(8,128)(2,1)}, bf16[2,32,3200]{2,1,0:T(8,128)(2,1)}, u32[]{:S(2)}, u32[]{:S(2)}) collective-permute-start(bf16[2,32,3200]{2,1,0:T(8,128)(2,1)} %slice.103), channel_id=1, source_target_pairs={{0,2},{1,3},{2,0},{3,1},{4,6},{5,7},{6,4},{7,5},{8,10},{9,11},{10,... | collective-permute-start | bytes 1228808 | tf_op jit(solution)/shard_map/ppermute | solution.py:411
  55.0 11.7 %collective-permute-start.4 = (bf16[2,32,3200]{2,1,0:T(8,128)(2,1)S(1)}, bf16[2,32,3200]{2,1,0:T(8,128)(2,1)}, u32[]{:S(2)}, u32[]{:S(2)}) collective-permute-start(bf16[2,32,3200]{2,1,0:T(8,128)(2,1)S(1)} %slice.104), channel_id=1, source_target_pairs={{0,4},{1,5},{2,6},{3,7},{4,0},{5,1},{6,2},{7,3},{8,12},{9,13},{10,... | collective-permute-start | bytes 1228808 | tf_op jit(solution)/shard_map/ppermute | solution.py:411
  68.9 32.8 %collective-permute-start.8 = (bf16[4,32,5120]{2,1,0:T(8,128)(2,1)}, bf16[4,32,5120]{2,1,0:T(8,128)(2,1)S(1)}, u32[]{:S(2)}, u32[]{:S(2)}) collective-permute-start(bf16[4,32,5120]{2,1,0:T(8,128)(2,1)} %bitcast.2.refs_1_), channel_id=1, source_target_pairs={{0,2},{1,3},{2,0},{3,1},{4,6},{5,7},{6,4},{7,5},{8,10},{9,11},{10,... | collective-permute-start | bytes 3932168 | tf_op jit(solution)/shard_map/ppermute | solution.py:411
  70.4 31.3 %collective-permute-start.9 = (bf16[4,32,5120]{2,1,0:T(8,128)(2,1)}, bf16[4,32,5120]{2,1,0:T(8,128)(2,1)}, u32[]{:S(2)}, u32[]{:S(2)}) collective-permute-start(bf16[4,32,5120]{2,1,0:T(8,128)(2,1)} %bitcast.2.refs_1_), channel_id=1, source_target_pairs={{0,4},{1,5},{2,6},{3,7},{4,0},{5,1},{6,2},{7,3},{8,12},{9,13},{10,... | collective-permute-start | bytes 3932168 | tf_op jit(solution)/shard_map/ppermute | solution.py:411
  71.9 140.7 %all-gather.7.cloned.1.call-start = ((), (), s32[]{:S(2)}) async-start(), calls=%async_computation.3 | async-start | bytes 8650752 | tf_op jit(solution)/shard_map/all_gather | solution.py:1041
  101.7 21.2 %collective-permute-start.14 = (bf16[4,32,5120]{2,1,0:T(8,128)(2,1)}, bf16[4,32,5120]{2,1,0:T(8,128)(2,1)}, u32[]{:S(2)}, u32[]{:S(2)}) collective-permute-start(bf16[4,32,5120]{2,1,0:T(8,128)(2,1)} %bitcast.2.refs_1_), channel_id=1, source_target_pairs={{0,1},{1,0},{2,3},{3,2},{4,5},{5,4},{6,7},{7,6},{8,9},{9,8},{10,11... | collective-permute-start | bytes 3932168 | tf_op jit(solution)/shard_map/ppermute | solution.py:411
  101.8 21.1 %collective-permute-start.15 = (bf16[4,32,5120]{2,1,0:T(8,128)(2,1)S(1)}, bf16[4,32,5120]{2,1,0:T(8,128)(2,1)}, u32[]{:S(2)}, u32[]{:S(2)}) collective-permute-start(bf16[4,32,5120]{2,1,0:T(8,128)(2,1)S(1)} %collective-permute-done.8.refs_2_), channel_id=1, source_target_pairs={{0,1},{1,0},{2,3},{3,2},{4,5},{5,4},{6,7},{7,6},{8,9},{9,8},{10,11... | collective-permute-start | bytes 3932168 | tf_op jit(solution)/shard_map/ppermute | solution.py:411
  102.3 20.6 %collective-permute-start.16 = (bf16[4,32,5120]{2,1,0:T(8,128)(2,1)}, bf16[4,32,5120]{2,1,0:T(8,128)(2,1)}, u32[]{:S(2)}, u32[]{:S(2)}) collective-permute-start(bf16[4,32,5120]{2,1,0:T(8,128)(2,1)} %collective-permute-done.9.refs_3_), channel_id=1, source_target_pairs={{0,1},{1,0},{2,3},{3,2},{4,5},{5,4},{6,7},{7,6},{8,9},{9,8},{10,11... | collective-permute-start | bytes 3932168 | tf_op jit(solution)/shard_map/ppermute | solution.py:411
  105.3 17.4 %collective-permute-start.12 = (bf16[2,32,5120]{2,1,0:T(8,128)(2,1)}, bf16[2,32,5120]{2,1,0:T(8,128)(2,1)}, u32[]{:S(2)}, u32[]{:S(2)}) collective-permute-start(bf16[2,32,5120]{2,1,0:T(8,128)(2,1)} %slice.110), channel_id=1, source_target_pairs={{0,2},{1,3},{2,0},{3,1},{4,6},{5,7},{6,4},{7,5},{8,10},{9,11},{10,... | collective-permute-start | bytes 1966088 | tf_op jit(solution)/shard_map/ppermute | solution.py:411
  105.8 17.1 %collective-permute-start.13 = (bf16[2,32,5120]{2,1,0:T(8,128)(2,1)}, bf16[2,32,5120]{2,1,0:T(8,128)(2,1)}, u32[]{:S(2)}, u32[]{:S(2)}) collective-permute-start(bf16[2,32,5120]{2,1,0:T(8,128)(2,1)} %slice.111), channel_id=1, source_target_pairs={{0,4},{1,5},{2,6},{3,7},{4,0},{5,1},{6,2},{7,3},{8,12},{9,13},{10,... | collective-permute-start | bytes 1966088 | tf_op jit(solution)/shard_map/ppermute | solution.py:411
  122.9 239.6 %reduce-scatter.4.cloned.1.call-start = ((), (), s32[]{:S(2)}) async-start(), calls=%async_computation.4 | async-start | bytes 1310720 | tf_op jit(solution)/shard_map/reduce_scatter | solution.py:850
  123.0 11.0 %collective-permute-start.19 = (bf16[2,32,5120]{2,1,0:T(8,128)(2,1)}, bf16[2,32,5120]{2,1,0:T(8,128)(2,1)S(1)}, u32[]{:S(2)}, u32[]{:S(2)}) collective-permute-start(bf16[2,32,5120]{2,1,0:T(8,128)(2,1)} %collective-permute-done.12.refs_4_), channel_id=1, source_target_pairs={{0,1},{1,0},{2,3},{3,2},{4,5},{5,4},{6,7},{7,6},{8,9},{9,8},{10,11... | collective-permute-start | bytes 1966088 | tf_op jit(solution)/shard_map/ppermute | solution.py:411
  123.1 11.4 %collective-permute-start.20 = (bf16[2,32,5120]{2,1,0:T(8,128)(2,1)}, bf16[2,32,5120]{2,1,0:T(8,128)(2,1)S(1)}, u32[]{:S(2)}, u32[]{:S(2)}) collective-permute-start(bf16[2,32,5120]{2,1,0:T(8,128)(2,1)} %collective-permute-done.13.refs_5_), channel_id=1, source_target_pairs={{0,1},{1,0},{2,3},{3,2},{4,5},{5,4},{6,7},{7,6},{8,9},{9,8},{10,11... | collective-permute-start | bytes 1966088 | tf_op jit(solution)/shard_map/ppermute | solution.py:411
  123.6 27.3 %collective-permute-start.17 = (bf16[4,32,4096]{2,1,0:T(8,128)(2,1)}, bf16[4,32,4096]{2,1,0:T(8,128)(2,1)S(1)}, u32[]{:S(2)}, u32[]{:S(2)}) collective-permute-start(bf16[4,32,4096]{2,1,0:T(8,128)(2,1)} %bitcast.76), channel_id=1, source_target_pairs={{0,2},{1,3},{2,0},{3,1},{4,6},{5,7},{6,4},{7,5},{8,10},{9,11},{10,... | collective-permute-start | bytes 3145736 | tf_op jit(solution)/shard_map/ppermute | solution.py:411
  125.2 26.9 %collective-permute-start.18 = (bf16[4,32,4096]{2,1,0:T(8,128)(2,1)}, bf16[4,32,4096]{2,1,0:T(8,128)(2,1)S(1)}, u32[]{:S(2)}, u32[]{:S(2)}) collective-permute-start(bf16[4,32,4096]{2,1,0:T(8,128)(2,1)} %bitcast.77), channel_id=1, source_target_pairs={{0,4},{1,5},{2,6},{3,7},{4,0},{5,1},{6,2},{7,3},{8,12},{9,13},{10,... | collective-permute-start | bytes 3145736 | tf_op jit(solution)/shard_map/ppermute | solution.py:411
  131.1 18.6 %collective-permute-start.21 = (bf16[512,512]{1,0:T(8,128)(2,1)S(1)}, bf16[512,512]{1,0:T(8,128)(2,1)S(1)}, u32[]{:S(2)}, u32[]{:S(2)}) collective-permute-start(bf16[512,512]{1,0:T(8,128)(2,1)S(1)} %get-tuple-element.304), channel_id=1, source_target_pairs={{0,1},{1,0},{2,3},{3,2},{4,5},{5,4},{6,7},{7,6},{8,9},{9,8},{10,11... | collective-permute-start | bytes 1572872 | tf_op jit(solution)/shard_map/ppermute | solution.py:411
  134.0 15.7 %collective-permute-start.22 = (bf16[512,512]{1,0:T(8,128)(2,1)S(1)}, bf16[512,512]{1,0:T(8,128)(2,1)S(1)}, u32[]{:S(2)}, u32[]{:S(2)}) collective-permute-start(bf16[512,512]{1,0:T(8,128)(2,1)S(1)} %get-tuple-element.306), channel_id=1, source_target_pairs={{0,1},{1,0},{2,3},{3,2},{4,5},{5,4},{6,7},{7,6},{8,9},{9,8},{10,11... | collective-permute-start | bytes 1572872 | tf_op jit(solution)/shard_map/ppermute | solution.py:411
  152.1 20.5 %collective-permute-start.25 = (bf16[4,32,4096]{2,1,0:T(8,128)(2,1)S(1)}, bf16[4,32,4096]{2,1,0:T(8,128)(2,1)S(1)}, u32[]{:S(2)}, u32[]{:S(2)}) collective-permute-start(bf16[4,32,4096]{2,1,0:T(8,128)(2,1)S(1)} %bitcast.78), channel_id=1, source_target_pairs={{0,1},{1,0},{2,3},{3,2},{4,5},{5,4},{6,7},{7,6},{8,9},{9,8},{10,11... | collective-permute-start | bytes 3145736 | tf_op jit(solution)/shard_map/ppermute | solution.py:411
  152.1 20.5 %collective-permute-start.26 = (bf16[4,32,4096]{2,1,0:T(8,128)(2,1)S(1)}, bf16[4,32,4096]{2,1,0:T(8,128)(2,1)S(1)}, u32[]{:S(2)}, u32[]{:S(2)}) collective-permute-start(bf16[4,32,4096]{2,1,0:T(8,128)(2,1)S(1)} %collective-permute-done.17.refs_2_), channel_id=1, source_target_pairs={{0,1},{1,0},{2,3},{3,2},{4,5},{5,4},{6,7},{7,6},{8,9},{9,8},{10,11... | collective-permute-start | bytes 3145736 | tf_op jit(solution)/shard_map/ppermute | solution.py:411
  152.6 20.0 %collective-permute-start.27 = (bf16[4,32,4096]{2,1,0:T(8,128)(2,1)S(1)}, bf16[4,32,4096]{2,1,0:T(8,128)(2,1)S(1)}, u32[]{:S(2)}, u32[]{:S(2)}) collective-permute-start(bf16[4,32,4096]{2,1,0:T(8,128)(2,1)S(1)} %collective-permute-done.18.refs_3_), channel_id=1, source_target_pairs={{0,1},{1,0},{2,3},{3,2},{4,5},{5,4},{6,7},{7,6},{8,9},{9,8},{10,11... | collective-permute-start | bytes 3145736 | tf_op jit(solution)/shard_map/ppermute | solution.py:411
  153.4 19.2 %collective-permute-start.23 = (bf16[2,32,4096]{2,1,0:T(8,128)(2,1)S(1)}, bf16[2,32,4096]{2,1,0:T(8,128)(2,1)S(1)}, u32[]{:S(2)}, u32[]{:S(2)}) collective-permute-start(bf16[2,32,4096]{2,1,0:T(8,128)(2,1)S(1)} %slice.118), channel_id=1, source_target_pairs={{0,2},{1,3},{2,0},{3,1},{4,6},{5,7},{6,4},{7,5},{8,10},{9,11},{10,... | collective-permute-start | bytes 1572872 | tf_op jit(solution)/shard_map/ppermute | solution.py:411
  154.0 18.6 %collective-permute-start.24 = (bf16[2,32,4096]{2,1,0:T(8,128)(2,1)S(1)}, bf16[2,32,4096]{2,1,0:T(8,128)(2,1)S(1)}, u32[]{:S(2)}, u32[]{:S(2)}) collective-permute-start(bf16[2,32,4096]{2,1,0:T(8,128)(2,1)S(1)} %slice.119), channel_id=1, source_target_pairs={{0,4},{1,5},{2,6},{3,7},{4,0},{5,1},{6,2},{7,3},{8,12},{9,13},{10,... | collective-permute-start | bytes 1572872 | tf_op jit(solution)/shard_map/ppermute | solution.py:411
  192.9 11.4 %collective-permute-start.31 = (bf16[512,2048]{1,0:T(8,128)(2,1)S(1)}, bf16[512,2048]{1,0:T(8,128)(2,1)S(1)}, u32[]{:S(2)}, u32[]{:S(2)}) collective-permute-start(bf16[512,2048]{1,0:T(8,128)(2,1)S(1)} %get-tuple-element.354), channel_id=1, source_target_pairs={{0,1},{1,0},{2,3},{3,2},{4,5},{5,4},{6,7},{7,6},{8,9},{9,8},{10,11... | collective-permute-start | bytes 6291464 | tf_op jit(solution)/shard_map/ppermute | solution.py:411
  212.6 23.6 %collective-permute-start.35 = (bf16[64,4096]{1,0:T(8,128)(2,1)}, bf16[64,4096]{1,0:T(8,128)(2,1)S(1)}, u32[]{:S(2)}, u32[]{:S(2)}) collective-permute-start(bf16[64,4096]{1,0:T(8,128)(2,1)} %get-tuple-element.378), channel_id=1, source_target_pairs={{0,2},{1,3},{2,0},{3,1},{4,6},{5,7},{6,4},{7,5},{8,10},{9,11},{10,... | collective-permute-start | bytes 1572872 | tf_op jit(solution)/shard_map/ppermute | solution.py:411
  214.4 21.9 %collective-permute-start.36 = (bf16[64,4096]{1,0:T(8,128)(2,1)}, bf16[64,4096]{1,0:T(8,128)(2,1)S(1)}, u32[]{:S(2)}, u32[]{:S(2)}) collective-permute-start(bf16[64,4096]{1,0:T(8,128)(2,1)} %get-tuple-element.379), channel_id=1, source_target_pairs={{0,4},{1,5},{2,6},{3,7},{4,0},{5,1},{6,2},{7,3},{8,12},{9,13},{10,... | collective-permute-start | bytes 1572872 | tf_op jit(solution)/shard_map/ppermute | solution.py:411
  236.3 7.6 %collective-permute-start.37 = (bf16[512,4096]{1,0:T(8,128)(2,1)}, bf16[512,4096]{1,0:T(8,128)(2,1)S(1)}, u32[]{:S(2)}, u32[]{:S(2)}) collective-permute-start(bf16[512,4096]{1,0:T(8,128)(2,1)} %get-tuple-element.392), channel_id=1, source_target_pairs={{0,1},{1,0},{2,3},{3,2},{4,5},{5,4},{6,7},{7,6},{8,9},{9,8},{10,11... | collective-permute-start | bytes 12582920 | tf_op jit(solution)/shard_map/ppermute | solution.py:411
  239.7 33.1 %collective-permute-start.40 = (bf16[128,4096]{1,0:T(8,128)(2,1)S(1)}, bf16[128,4096]{1,0:T(8,128)(2,1)}, u32[]{:S(2)}, u32[]{:S(2)}) collective-permute-start(bf16[128,4096]{1,0:T(8,128)(2,1)S(1)} %get-tuple-element.404), channel_id=1, source_target_pairs={{0,2},{1,3},{2,0},{3,1},{4,6},{5,7},{6,4},{7,5},{8,10},{9,11},{10,... | collective-permute-start | bytes 3145736 | tf_op jit(solution)/shard_map/ppermute | solution.py:411
  240.7 32.1 %collective-permute-start.41 = (bf16[128,4096]{1,0:T(8,128)(2,1)S(1)}, bf16[128,4096]{1,0:T(8,128)(2,1)}, u32[]{:S(2)}, u32[]{:S(2)}) collective-permute-start(bf16[128,4096]{1,0:T(8,128)(2,1)S(1)} %get-tuple-element.405), channel_id=1, source_target_pairs={{0,4},{1,5},{2,6},{3,7},{4,0},{5,1},{6,2},{7,3},{8,12},{9,13},{10,... | collective-permute-start | bytes 3145736 | tf_op jit(solution)/shard_map/ppermute | solution.py:411
  251.3 25.1 %collective-permute-start.42 = (bf16[512,1024]{1,0:T(8,128)(2,1)S(1)}, bf16[512,1024]{1,0:T(8,128)(2,1)S(1)}, u32[]{:S(2)}, u32[]{:S(2)}) collective-permute-start(bf16[512,1024]{1,0:T(8,128)(2,1)S(1)} %get-tuple-element.398), channel_id=1, source_target_pairs={{0,1},{1,0},{2,3},{3,2},{4,5},{5,4},{6,7},{7,6},{8,9},{9,8},{10,11... | collective-permute-start | bytes 3145736 | tf_op jit(solution)/shard_map/ppermute | solution.py:411
  251.3 24.4 %collective-permute-start.38 = (bf16[64,4096]{1,0:T(8,128)(2,1)}, bf16[64,4096]{1,0:T(8,128)(2,1)S(1)}, u32[]{:S(2)}, u32[]{:S(2)}) collective-permute-start(bf16[64,4096]{1,0:T(8,128)(2,1)} %get-tuple-element.399), channel_id=1, source_target_pairs={{0,2},{1,3},{2,0},{3,1},{4,6},{5,7},{6,4},{7,5},{8,10},{9,11},{10,... | collective-permute-start | bytes 1572872 | tf_op jit(solution)/shard_map/ppermute | solution.py:411
  253.0 23.3 %collective-permute-start.39 = (bf16[64,4096]{1,0:T(8,128)(2,1)}, bf16[64,4096]{1,0:T(8,128)(2,1)S(1)}, u32[]{:S(2)}, u32[]{:S(2)}) collective-permute-start(bf16[64,4096]{1,0:T(8,128)(2,1)} %get-tuple-element.400), channel_id=1, source_target_pairs={{0,4},{1,5},{2,6},{3,7},{4,0},{5,1},{6,2},{7,3},{8,12},{9,13},{10,... | collective-permute-start | bytes 1572872 | tf_op jit(solution)/shard_map/ppermute | solution.py:411
  277.3 17.5 %collective-permute-start.44 = (bf16[2,592,1024]{2,1,0:T(8,128)(2,1)}, bf16[2,592,1024]{2,1,0:T(8,128)(2,1)}, u32[]{:S(2)}, u32[]{:S(2)}) collective-permute-start(bf16[2,592,1024]{2,1,0:T(8,128)(2,1)} %get-tuple-element.485.refs_10_.refs_0_), channel_id=1, source_target_pairs={{0,1},{1,0},{2,3},{3,2},{4,5},{5,4},{6,7},{7,6},{8,9},{9,8},{10,11... | collective-permute-start | bytes 7274504 | tf_op jit(solution)/shard_map/ppermute | solution.py:411
  277.5 17.3 %collective-permute-start.43 = (bf16[1,512,1024]{2,1,0:T(8,128)(2,1)S(1)}, bf16[1,512,1024]{2,1,0:T(8,128)(2,1)}, u32[]{:S(2)}, u32[]{:S(2)}) collective-permute-start(bf16[1,512,1024]{2,1,0:T(8,128)(2,1)S(1)} %get-tuple-element.421.refs_0_.refs_6_), channel_id=1, source_target_pairs={{0,1},{1,0},{2,3},{3,2},{4,5},{5,4},{6,7},{7,6},{8,9},{9,8},{10,11... | collective-permute-start | bytes 3145736 | tf_op jit(solution)/shard_map/ppermute | solution.py:411
  283.1 42.9 %collective-permute-start.48 = (bf16[128,4096]{1,0:T(8,128)(2,1)}, bf16[128,4096]{1,0:T(8,128)(2,1)}, u32[]{:S(2)}, u32[]{:S(2)}) collective-permute-start(bf16[128,4096]{1,0:T(8,128)(2,1)} %get-tuple-element.440), channel_id=1, source_target_pairs={{0,2},{1,3},{2,0},{3,1},{4,6},{5,7},{6,4},{7,5},{8,10},{9,11},{10,... | collective-permute-start | bytes 3145736 | tf_op jit(solution)/shard_map/ppermute | solution.py:411
  284.2 41.9 %collective-permute-start.49 = (bf16[128,4096]{1,0:T(8,128)(2,1)}, bf16[128,4096]{1,0:T(8,128)(2,1)}, u32[]{:S(2)}, u32[]{:S(2)}) collective-permute-start(bf16[128,4096]{1,0:T(8,128)(2,1)} %get-tuple-element.441), channel_id=1, source_target_pairs={{0,4},{1,5},{2,6},{3,7},{4,0},{5,1},{6,2},{7,3},{8,12},{9,13},{10,... | collective-permute-start | bytes 3145736 | tf_op jit(solution)/shard_map/ppermute | solution.py:411
  304.4 21.7 %collective-permute-start.47 = (bf16[512,1024]{1,0:T(8,128)(2,1)}, bf16[512,1024]{1,0:T(8,128)(2,1)}, u32[]{:S(2)}, u32[]{:S(2)}) collective-permute-start(bf16[512,1024]{1,0:T(8,128)(2,1)} %get-tuple-element.432), channel_id=1, source_target_pairs={{0,1},{1,0},{2,3},{3,2},{4,5},{5,4},{6,7},{7,6},{8,9},{9,8},{10,11... | collective-permute-start | bytes 3145736 | tf_op jit(solution)/shard_map/ppermute | solution.py:411
  307.4 77.0 %reduce-scatter.6.cloned.1.call-start = ((), (), s32[]{:S(2)}) async-start(), calls=%async_computation.5 | async-start | bytes 1310720 | tf_op jit(solution)/shard_map/reduce_scatter | solution.py:850
  307.4 18.6 %collective-permute-start.45 = (bf16[64,4096]{1,0:T(8,128)(2,1)}, bf16[64,4096]{1,0:T(8,128)(2,1)}, u32[]{:S(2)}, u32[]{:S(2)}) collective-permute-start(bf16[64,4096]{1,0:T(8,128)(2,1)} %get-tuple-element.433), channel_id=1, source_target_pairs={{0,2},{1,3},{2,0},{3,1},{4,6},{5,7},{6,4},{7,5},{8,10},{9,11},{10,... | collective-permute-start | bytes 1572872 | tf_op jit(solution)/shard_map/ppermute | solution.py:411
  307.9 18.1 %collective-permute-start.46 = (bf16[64,4096]{1,0:T(8,128)(2,1)}, bf16[64,4096]{1,0:T(8,128)(2,1)}, u32[]{:S(2)}, u32[]{:S(2)}) collective-permute-start(bf16[64,4096]{1,0:T(8,128)(2,1)} %get-tuple-element.434), channel_id=1, source_target_pairs={{0,4},{1,5},{2,6},{3,7},{4,0},{5,1},{6,2},{7,3},{8,12},{9,13},{10,... | collective-permute-start | bytes 1572872 | tf_op jit(solution)/shard_map/ppermute | solution.py:411
  326.0 23.9 %collective-permute-start.50 = (bf16[3,512,1024]{2,1,0:T(8,128)(2,1)}, bf16[3,512,1024]{2,1,0:T(8,128)(2,1)}, u32[]{:S(2)}, u32[]{:S(2)}) collective-permute-start(bf16[3,512,1024]{2,1,0:T(8,128)(2,1)} %attn_bwd.3.refs_0_.refs_6_.refs_2_), channel_id=1, source_target_pairs={{0,1},{1,0},{2,3},{3,2},{4,5},{5,4},{6,7},{7,6},{8,9},{9,8},{10,11... | collective-permute-start | bytes 9437192 | tf_op jit(solution)/shard_map/ppermute | solution.py:411
  329.0 98.8 %reduce-scatter.8.cloned.1.call-start = ((), (), s32[]{:S(2)}) async-start(), calls=%async_computation.6 | async-start | bytes 1310720 | tf_op jit(solution)/shard_map/reduce_scatter | solution.py:850
  332.0 30.5 %collective-permute-start.54 = (bf16[128,4096]{1,0:T(8,128)(2,1)}, bf16[128,4096]{1,0:T(8,128)(2,1)}, u32[]{:S(2)}, u32[]{:S(2)}) collective-permute-start(bf16[128,4096]{1,0:T(8,128)(2,1)} %get-tuple-element.473), channel_id=1, source_target_pairs={{0,2},{1,3},{2,0},{3,1},{4,6},{5,7},{6,4},{7,5},{8,10},{9,11},{10,... | collective-permute-start | bytes 3145736 | tf_op jit(solution)/shard_map/ppermute | solution.py:411
  332.9 29.7 %collective-permute-start.55 = (bf16[128,4096]{1,0:T(8,128)(2,1)S(1)}, bf16[128,4096]{1,0:T(8,128)(2,1)}, u32[]{:S(2)}, u32[]{:S(2)}) collective-permute-start(bf16[128,4096]{1,0:T(8,128)(2,1)S(1)} %get-tuple-element.474), channel_id=1, source_target_pairs={{0,4},{1,5},{2,6},{3,7},{4,0},{5,1},{6,2},{7,3},{8,12},{9,13},{10,... | collective-permute-start | bytes 3145736 | tf_op jit(solution)/shard_map/ppermute | solution.py:411
  355.7 8.6 %collective-permute-start.52 = (bf16[64,2048]{1,0:T(8,128)(2,1)}, bf16[64,2048]{1,0:T(8,128)(2,1)S(1)}, u32[]{:S(2)}, u32[]{:S(2)}) collective-permute-start(bf16[64,2048]{1,0:T(8,128)(2,1)} %get-tuple-element.461), channel_id=1, source_target_pairs={{0,2},{1,3},{2,0},{3,1},{4,6},{5,7},{6,4},{7,5},{8,10},{9,11},{10,... | collective-permute-start | bytes 786440 | tf_op jit(solution)/shard_map/ppermute | solution.py:411
  356.1 8.3 %collective-permute-start.53 = (bf16[64,2048]{1,0:T(8,128)(2,1)}, bf16[64,2048]{1,0:T(8,128)(2,1)S(1)}, u32[]{:S(2)}, u32[]{:S(2)}) collective-permute-start(bf16[64,2048]{1,0:T(8,128)(2,1)} %get-tuple-element.462), channel_id=1, source_target_pairs={{0,4},{1,5},{2,6},{3,7},{4,0},{5,1},{6,2},{7,3},{8,12},{9,13},{10,... | collective-permute-start | bytes 786440 | tf_op jit(solution)/shard_map/ppermute | solution.py:411
  366.6 20.3 %collective-permute-start.58 = (bf16[128,2048]{1,0:T(8,128)(2,1)S(1)}, bf16[128,2048]{1,0:T(8,128)(2,1)S(1)}, u32[]{:S(2)}, u32[]{:S(2)}) collective-permute-start(bf16[128,2048]{1,0:T(8,128)(2,1)S(1)} %get-tuple-element.483), channel_id=1, source_target_pairs={{0,2},{1,3},{2,0},{3,1},{4,6},{5,7},{6,4},{7,5},{8,10},{9,11},{10,... | collective-permute-start | bytes 1572872 | tf_op jit(solution)/shard_map/ppermute | solution.py:411
  368.2 18.6 %collective-permute-start.59 = (bf16[128,2048]{1,0:T(8,128)(2,1)S(1)}, bf16[128,2048]{1,0:T(8,128)(2,1)S(1)}, u32[]{:S(2)}, u32[]{:S(2)}) collective-permute-start(bf16[128,2048]{1,0:T(8,128)(2,1)S(1)} %get-tuple-element.484), channel_id=1, source_target_pairs={{0,4},{1,5},{2,6},{3,7},{4,0},{5,1},{6,2},{7,3},{8,12},{9,13},{10,... | collective-permute-start | bytes 1572872 | tf_op jit(solution)/shard_map/ppermute | solution.py:411
  368.7 16.9 %collective-permute-start.56 = (bf16[64,2176]{1,0:T(8,128)(2,1)}, bf16[64,2176]{1,0:T(8,128)(2,1)S(1)}, u32[]{:S(2)}, u32[]{:S(2)}) collective-permute-start(bf16[64,2176]{1,0:T(8,128)(2,1)} %get-tuple-element.478), channel_id=1, source_target_pairs={{0,2},{1,3},{2,0},{3,1},{4,6},{5,7},{6,4},{7,5},{8,10},{9,11},{10,... | collective-permute-start | bytes 835592 | tf_op jit(solution)/shard_map/ppermute | solution.py:411
  369.9 16.9 %collective-permute-start.57 = (bf16[64,2176]{1,0:T(8,128)(2,1)}, bf16[64,2176]{1,0:T(8,128)(2,1)}, u32[]{:S(2)}, u32[]{:S(2)}) collective-permute-start(bf16[64,2176]{1,0:T(8,128)(2,1)} %get-tuple-element.479), channel_id=1, source_target_pairs={{0,4},{1,5},{2,6},{3,7},{4,0},{5,1},{6,2},{7,3},{8,12},{9,13},{10,... | collective-permute-start | bytes 835592 | tf_op jit(solution)/shard_map/ppermute | solution.py:411
  390.2 20.7 %collective-permute-start.62 = (bf16[32,2048]{1,0:T(8,128)(2,1)S(1)}, bf16[32,2048]{1,0:T(8,128)(2,1)S(1)}, u32[]{:S(2)}, u32[]{:S(2)}) collective-permute-start(bf16[32,2048]{1,0:T(8,128)(2,1)S(1)} %get-tuple-element.553), channel_id=1, source_target_pairs={{0,8},{1,9},{2,10},{3,11},{4,12},{5,13},{6,14},{7,15},{8,16},{9,17... | collective-permute-start | bytes 393224 | tf_op jit(solution)/shard_map/ppermute | solution.py:860
  390.3 20.6 %collective-permute-start.63 = (bf16[32,2048]{1,0:T(8,128)(2,1)S(1)}, bf16[32,2048]{1,0:T(8,128)(2,1)S(1)}, u32[]{:S(2)}, u32[]{:S(2)}) collective-permute-start(bf16[32,2048]{1,0:T(8,128)(2,1)S(1)} %get-tuple-element.555), channel_id=1, source_target_pairs={{0,16},{1,17},{2,18},{3,19},{4,20},{5,21},{6,22},{7,23},{8,24},{9,... | collective-permute-start | bytes 393224 | tf_op jit(solution)/shard_map/ppermute | solution.py:860
  392.5 18.4 %collective-permute-start.64 = (bf16[32,2048]{1,0:T(8,128)(2,1)S(1)}, bf16[32,2048]{1,0:T(8,128)(2,1)S(1)}, u32[]{:S(2)}, u32[]{:S(2)}) collective-permute-start(bf16[32,2048]{1,0:T(8,128)(2,1)S(1)} %get-tuple-element.554), channel_id=1, source_target_pairs={{0,24},{1,25},{2,26},{3,27},{4,28},{5,29},{6,30},{7,31},{8,0},{9,1... | collective-permute-start | bytes 393224 | tf_op jit(solution)/shard_map/ppermute | solution.py:860
  395.6 15.4 %collective-permute-start.60 = (bf16[128,2176]{1,0:T(8,128)(2,1)S(1)}, bf16[128,2176]{1,0:T(8,128)(2,1)S(1)}, u32[]{:S(2)}, u32[]{:S(2)}) collective-permute-start(bf16[128,2176]{1,0:T(8,128)(2,1)S(1)} %get-tuple-element.492), channel_id=1, source_target_pairs={{0,2},{1,3},{2,0},{3,1},{4,6},{5,7},{6,4},{7,5},{8,10},{9,11},{10,... | collective-permute-start | bytes 1671176 | tf_op jit(solution)/shard_map/ppermute | solution.py:411
  396.4 14.7 %collective-permute-start.61 = (bf16[128,2176]{1,0:T(8,128)(2,1)S(1)}, bf16[128,2176]{1,0:T(8,128)(2,1)S(1)}, u32[]{:S(2)}, u32[]{:S(2)}) collective-permute-start(bf16[128,2176]{1,0:T(8,128)(2,1)S(1)} %get-tuple-element.493), channel_id=1, source_target_pairs={{0,4},{1,5},{2,6},{3,7},{4,0},{5,1},{6,2},{7,3},{8,12},{9,13},{10,... | collective-permute-start | bytes 1671176 | tf_op jit(solution)/shard_map/ppermute | solution.py:411
  414.3 7.2 %collective-permute-start.65 = (bf16[32,2176]{1,0:T(8,128)(2,1)S(1)}, bf16[32,2176]{1,0:T(8,128)(2,1)S(1)}, u32[]{:S(2)}, u32[]{:S(2)}) collective-permute-start(bf16[32,2176]{1,0:T(8,128)(2,1)S(1)} %get-tuple-element.550), channel_id=1, source_target_pairs={{0,8},{1,9},{2,10},{3,11},{4,12},{5,13},{6,14},{7,15},{8,16},{9,17... | collective-permute-start | bytes 417800 | tf_op jit(solution)/shard_map/ppermute | solution.py:860
  415.0 10.5 %collective-permute-start.66 = (bf16[32,2176]{1,0:T(8,128)(2,1)S(1)}, bf16[32,2176]{1,0:T(8,128)(2,1)S(1)}, u32[]{:S(2)}, u32[]{:S(2)}) collective-permute-start(bf16[32,2176]{1,0:T(8,128)(2,1)S(1)} %get-tuple-element.552), channel_id=1, source_target_pairs={{0,16},{1,17},{2,18},{3,19},{4,20},{5,21},{6,22},{7,23},{8,24},{9,... | collective-permute-start | bytes 417800 | tf_op jit(solution)/shard_map/ppermute | solution.py:860
  416.3 9.2 %collective-permute-start.67 = (bf16[32,2176]{1,0:T(8,128)(2,1)S(1)}, bf16[32,2176]{1,0:T(8,128)(2,1)S(1)}, u32[]{:S(2)}, u32[]{:S(2)}) collective-permute-start(bf16[32,2176]{1,0:T(8,128)(2,1)S(1)} %get-tuple-element.551), channel_id=1, source_target_pairs={{0,24},{1,25},{2,26},{3,27},{4,28},{5,29},{6,30},{7,31},{8,0},{9,1... | collective-permute-start | bytes 417800 | tf_op jit(solution)/shard_map/ppermute | solution.py:860
  (105 other events, 703.4 us)
Sparse Core Ops, SparseCore 0:
  35.3 30.4 all-gather.8
  72.0 25.9 all-gather.10
  123.1 82.9 all-gather.6
  307.5 25.5 reduce-scatter.3
  335.3 25.7 reduce-scatter.5
  373.7 31.3 reduce-scatter.7
where the time goes:
time: 446 us; the launch traced here: 438 us
  Pallas kernels  229 us (51%)
  waiting for transfers between devices  50.9 us (11%)
  starting transfers between devices  48.8 us (11%)
  local copies, waits for them, and re-layouts  47.2 us (11%)
  blocking collectives  22.1 us (5%)
  between operations  17 us (4%)
  other arithmetic  16.8 us (4%)
  matrix products  6.59 us (1%)
    pallas_call x40, Pallas kernels, run(): pl.pallas_call(body, grid_spec=pltpu.PrefetchScalarGridSpec(num_scalar_pr...  229 us
    ppermute x62, waiting for transfers between devices, swap(): return lax.ppermute(a, ALL, [(i, i ^ bit) for i in range(32)])  45 us
    ppermute x62, starting transfers between devices, swap(): return lax.ppermute(a, ALL, [(i, i ^ bit) for i in range(32)])  39.9 us
    unnamed x194, local copies, waits for them, and re-layouts  35.9 us
    all_gather x1, blocking collectives, gather_line(): return lax.all_gather(w, 'gx', axis=0)  22.1 us
  transfers between devices with their start and end apart: 74, of which 18 were waited for; matrix products, arithmetic and copies ran while one was open for 7% of the time, Pallas kernels for 52%

commit v1 on v0

--- a/solution.py
+++ b/solution.py
@@ -13,9 +13,9 @@
 BF = jnp.bfloat16
 F32 = jnp.float32
 PAIR = 128
-LIMITS = {'feed_back': 50, 'pass_on': 8, 'plane_sum': 8, 'place': 8, 'hidden_order': 8, 'memory_grad': 12, 'turn': 12, 'wgrad': 44, 'wgrad_down': 44}
-FAR_OUTS = {'wgrad': (0, 1, 2), 'wgrad_down': (0, 1, 2), 'feed_up': (0, 1, 2), 'place_dot': (0,), 'feed_back': (0, 1)}
-FAR_INS = {'pass_on': (0, 1, 2, 3), 'plane_sum': (0, 1, 2)}
+LIMITS = {'feed_back': 50, 'pass_on': 8, 'plane_sum': 8, 'place': 8, 'hidden_order': 8, 'memory_grad': 12, 'turn': 12, 'wgrad': 44, 'wgrad_down': 44, 'wgrad_mid': 44, 'finish': 12, 'line_parts': 12}
+FAR_OUTS = {'wgrad': (0, 1, 2), 'wgrad_down': (0, 1, 2, 3, 4, 5, 6), 'feed_up': (0, 1, 2), 'place_dot': (0,), 'feed_back': (0, 1), 'turn': (0, 1), 'wgrad_mid': (0, 1, 2)}
+FAR_INS = {'pass_on': (0, 1, 2, 3), 'plane_sum': (0, 1, 2), 'wgrad_mid': (0, 1, 2, 3, 4, 5, 6, 7, 8, 9, 10, 11), 'attn_bwd': (0, 1, 2, 3, 4)}
 
 
 def dot(a, b):
@@ -99,19 +99,21 @@
     limit = limit_ref[0]
     scale = BF(half**-0.5)
     v_t = v_ref[...].T
-    for q0, q1, keys in spans:
-        query = q_ref[q0:q1, :] * scale
-        ok = allowed_t(keys, q0, q1, limit, causal)
-        outs = []
-        for h in range(2):
-            s = dot_nt(k_ref[:keys, :], query * half_mask(width, h))
-            s = jnp.where(ok, s, -1e30)
-            top = jnp.max(s, axis=0, keepdims=True)
-            e = jnp.exp(s - top)
-            total = jnp.sum(e, axis=0, keepdims=True)
-            outs.append(dot(v_t[h * half : (h + 1) * half, :keys], e.astype(BF)) / total)
-            lse_ref[0, h : h + 1, q0:q1] = top + jnp.log(total)
-        o_ref[q0:q1, :] = jnp.concatenate(outs, axis=0).T.astype(BF)
+    work = [(q0, q1, keys, h) for q0, q1, keys in spans for h in range(2)]
+    scores = [
+        dot_nt(k_ref[:keys, :], q_ref[q0:q1, :] * scale * half_mask(width, h))
+        for q0, q1, keys, h in work
+    ]
+    outs = {}
+    for (q0, q1, keys, h), s in zip(work, scores, strict=True):
+        s = jnp.where(allowed_t(keys, q0, q1, limit, causal), s, -1e30)
+        top = jnp.max(s, axis=0, keepdims=True)
+        e = jnp.exp(s - top)
+        total = jnp.sum(e, axis=0, keepdims=True)
+        outs[q0, h] = dot(v_t[h * half : (h + 1) * half, :keys], e.astype(BF)) / total
+        lse_ref[0, h : h + 1, q0:q1] = top + jnp.log(total)
+    for q0, q1, _ in spans:
+        o_ref[q0:q1, :] = jnp.concatenate([outs[q0, 0], outs[q0, 1]], axis=0).T.astype(BF)
 
 
 def attn_bwd_kernel(
@@ -125,6 +127,7 @@
     scale = BF(half**-0.5)
     k_t = k_ref[...].T * scale
     total_k = k_ref.shape[0]
+    masks = [half_mask(width, h) for h in range(2)]
     dk = jnp.zeros((total_k, width), F32)
     dv = jnp.zeros((total_k, width), F32)
     for q0, q1, keys in spans:
@@ -132,21 +135,19 @@
         grad_o = do_ref[q0:q1, :]
         ok = allowed_t(keys, q0, q1, limit, causal)
         both = (grad_o.astype(F32) * o_ref[q0:q1, :].astype(F32)).T
-        outs = []
-        dk_part = jnp.zeros((keys, width), F32)
-        dv_part = jnp.zeros((keys, width), F32)
+        query_h = [query * m for m in masks]
+        grad_h = [grad_o * m for m in masks]
+        scores = [dot_nt(k_ref[:keys, :], a) for a in query_h]
+        dps = [dot_nt(v_ref[:keys, :], a) for a in grad_h]
+        probs, dss = [], []
         for h in range(2):
-            mask = half_mask(width, h)
-            query_h = query * mask
-            grad_h = grad_o * mask
             inner = jnp.sum(both[h * half : (h + 1) * half], axis=0, keepdims=True)
-            s = dot_nt(k_ref[:keys, :], query_h)
-            p = jnp.where(ok, jnp.exp(s - lse_ref[0, h : h + 1, q0:q1]), 0.0)
-            dv_part += dot(p.astype(BF), grad_h)
-            dp = dot_nt(v_ref[:keys, :], grad_h)
-            ds = (p * (dp - inner)).astype(BF)
-            dk_part += dot(ds, query_h)
-            outs.append(dot(k_t[h * half : (h + 1) * half, :keys], ds))
+            p = jnp.where(ok, jnp.exp(scores[h] - lse_ref[0, h : h + 1, q0:q1]), 0.0)
+            probs.append(p.astype(BF))
+            dss.append((p * (dps[h] - inner)).astype(BF))
+        dv_part = dot(probs[0], grad_h[0]) + dot(probs[1], grad_h[1])
+        dk_part = dot(dss[0], query_h[0]) + dot(dss[1], query_h[1])
+        outs = [dot(k_t[h * half : (h + 1) * half, :keys], dss[h]) for h in range(2)]
         dq_ref[q0:q1, :] = jnp.concatenate(outs, axis=0).T.astype(BF)
         if keys < total_k:
             pad = jnp.zeros((total_k - keys, width), F32)
@@ -506,12 +507,10 @@
 
 
 def store_rows(value, outs):
-    near = outs[0].shape[0]
-    half = outs[1].shape[0]
-    columns = value.shape[1]
-    outs[0][:, :columns] = value[:near]
-    outs[1][:, :columns] = value[near : near + half]
-    outs[2][:, :columns] = value[near + half :]
+    at = 0
+    for out in outs:
+        out[:, : value.shape[1]] = value[at : at + out.shape[0]]
+        at += out.shape[0]
 
 
 def row_outs(rows, columns, block):
@@ -521,6 +520,13 @@
     ]
 
 
+def half_outs(rows, columns, block):
+    return [
+        (shaped((r, columns), BF), pl.BlockSpec((r, block), lambda j, *_: (0, j)))
+        for r in (rows // 4,) + (rows // 8,) * 6
+    ]
+
+
 def wgrad_kernel(starts, extra, *refs):
     outs = refs[-3:]
     j = pl.program_id(0)
@@ -529,7 +535,9 @@
 
         @pl.when((j >= starts[s]) & (j < starts[s + 1]))
         def _(a=a, a2=a2, g=g, g2=g2):
-            store_rows((dot(a[...], g[...]) + dot(a2[...], g2[...])).astype(BF), outs)
+            tokens = g.shape[0]
+            part = dot(a[...][:, :tokens], g[...]) + dot(a2[...][:, :tokens], g2[...])
+            store_rows(part.astype(BF), outs)
 
     if extra:
 
@@ -539,7 +547,7 @@
             store_rows((mine[...].astype(F32) + theirs[...].astype(F32)).astype(BF), outs)
 
 
-def wgrad(segments, extra=(), deps=(), block=1024):
+def wgrad(segments, extra=(), deps=(), block=1024, name="wgrad"):
     starts, ins = [0], []
     for a, a2, g, g2, *span in segments:
         per = g.shape[2] // block
@@ -568,7 +576,7 @@
         row_outs(rows, columns, block),
         deps=deps,
         cost=costs(2 * rows * 1024 * columns, 4 * 512 * columns + 2 * rows * columns),
-        name="wgrad",
+        name=name,
     )
 
 
@@ -598,7 +606,7 @@
         [(g, spec(r, True)) for r in range(4)]
         + [(g_other, spec(r, False)) for r in range(4)]
         + [(dy, rows), (dy_other, rows)],
-        row_outs(512, cuts * d, d),
+        half_outs(512, cuts * d, d),
         prefetch=(bits,),
         cost=costs(2 * 512 * 1024 * cuts * d, 16 * tokens * d),
         name="wgrad_down",
@@ -749,28 +757,33 @@
     )
 
 
-def norm_back_kernel(g_ref, w_ref, x_ref, gain_ref, res_ref, *refs):
+def norm_back_kernel(further, g_ref, w_ref, x_ref, gain_ref, res_ref, *refs):
+    w2_ref = refs[0] if further else None
+    refs = refs[1:] if further else refs
     dx_ref, sums_ref, acc = refs[0], refs[-2], refs[-1]
-    low_ref = refs[1] if len(refs) == 4 else None
+    low_ref = refs[1] if further else None
     accumulate(acc, dot_nt(g_ref[...], w_ref[...]))
 
     @pl.when(pl.program_id(0) == pl.num_programs(0) - 1)
     def _():
         norm_back_store(acc, x_ref, gain_ref, res_ref, dx_ref, low_ref, sums_ref)
-
-
-def through_norm(g, w, x, gain, res, low=True, deps=()):
+        if further:
+            refs[2][...] = dot_nt(low_ref[...], w2_ref[...]).astype(BF)
+
+
+def through_norm(g, w, x, gain, res, further=None, deps=()):
     tokens, d = x.shape
     block = 512
     per = g.shape[2] // block
     count = g.shape[0] * per
     whole = pl.BlockSpec((tokens, d), lambda j: (0, 0), pipeline_mode=pl.Buffered(1))
+    whole_weight = pl.BlockSpec((d, d), lambda j: (0, 0), pipeline_mode=pl.Buffered(1))
     outs = [(shaped((tokens, d), F32), whole)]
-    if low:
-        outs.append((shaped((tokens, d), BF), whole))
+    if further is not None:
+        outs += [(shaped((tokens, d), BF), whole)] * 2
     outs.append((shaped((2, d), F32), pl.BlockSpec((2, d), lambda j: (0, 0))))
     return run(
-        norm_back_kernel,
+        functools.partial(norm_back_kernel, further is not None),
         (count,),
         [
             (g, pl.BlockSpec((None, tokens, block), lambda j: (j // per, 0, j % per))),
@@ -778,7 +791,8 @@
             (x, whole),
             (gain, pl.BlockSpec((1, d), lambda j: (0, 0))),
             (res, whole),
-        ],
+        ]
+        + ([] if further is None else [(further, whole_weight)]),
         outs,
         scratch=[pltpu.VMEM((tokens, d), F32)],
         deps=deps,
@@ -830,6 +844,55 @@
         name="pass_on",
     )
     return swap(to_x, XBIT), swap(to_y, YBIT)
+
+
+def add_pairs_kernel(a, b, c, d, first, second):
+    first[...] = a[...] + b[...]
+    second[...] = c[...] + d[...]
+
+
+def sum_halves_kernel(own, x_low, x_high, y_low, y_high, out):
+    half = x_low.shape[0]
+    for k, (x, y) in enumerate(((x_low, y_low), (x_high, y_high))):
+        part = own[k * half : (k + 1) * half].astype(F32) + x[...].astype(F32)
+        out[k * half : (k + 1) * half] = (part + y[...].astype(F32)).astype(BF)
+
+
+def early_first(grads):
+    _, x_low, _, _, y_high, low, high = grads
+    return swap(low, XBIT), swap(high, YBIT), swap(x_low, XBIT), swap(y_high, YBIT)
+
+
+def early_second(grads, came):
+    rows, columns = came[0].shape
+    block = column_blocks(columns)
+    spec = rows_spec(rows, block)
+    out = (shaped((rows, columns), BF), spec)
+    to_x, to_y = run(
+        add_pairs_kernel,
+        (columns // block,),
+        [(a, spec) for a in (grads[2], came[1], grads[3], came[0])],
+        [out, out],
+        cost=costs(2 * rows * columns, 12 * rows * columns),
+        name="pass_on",
+    )
+    return swap(to_x, XBIT), swap(to_y, YBIT)
+
+
+def early_line(grads, came, last):
+    rows, columns = grads[0].shape
+    block = column_blocks(columns)
+    half = rows_spec(rows // 2, block)
+    total = run(
+        sum_halves_kernel,
+        (columns // block,),
+        [(grads[0], rows_spec(rows, block))]
+        + [(a, half) for a in (came[2], last[0], last[1], came[3])],
+        [(shaped((rows, columns), BF), rows_spec(rows, block))],
+        cost=costs(2 * rows * columns, 8 * rows * columns),
+        name="plane_sum",
+    )
+    return lax.psum_scatter(total, "gx", scatter_dimension=0, tiled=True)
 
 
 def plane_sum(near, got, dtype):
@@ -850,16 +913,72 @@
     return lax.psum_scatter(total, "gx", scatter_dimension=0, tiled=True)
 
 
-def scatter_line_direct(near, got, z):
-    total = plane_sum(near, got, F32)
-    total = total.reshape(4, -1, total.shape[1])
-    low = total.astype(BF)
-    own = lax.dynamic_index_in_dim(total, z, 0, keepdims=False)
-    for step in (1, 2, 3):
-        part = lax.dynamic_index_in_dim(low, (z + step) % 4, 0, keepdims=False)
-        came = lax.ppermute(part, ALL, [(i, (i + 8 * step) % 32) for i in range(32)])
-        own = own + came.astype(F32)
-    return own
+def line_kernel(bits_ref, own, got_x, got_y, mine, *sends):
+    rows = mine.shape[0]
+    for step in range(4):
+        at = pl.ds(lax.rem(bits_ref[3] + step, 4) * rows, rows)
+        total = own[at, :].astype(F32) + got_x[at, :].astype(F32) + got_y[at, :].astype(F32)
+        if step == 0:
+            mine[...] = total
+        else:
+            sends[step - 1][...] = total.astype(BF)
+
+
+def line_parts(near, got, bits):
+    rows, columns = got[0].shape
+    spec = pl.BlockSpec((rows, columns), lambda j, _: (0, 0))
+    out = pl.BlockSpec((rows // 4, columns), lambda j, _: (0, 0))
+    mine, *sends = run(
+        line_kernel,
+        (1,),
+        [(a, spec) for a in (near, *got)],
+        [(shaped((rows // 4, columns), F32), out)] + [(shaped((rows // 4, columns), BF), out)] * 3,
+        prefetch=(bits,),
+        cost=costs(3 * rows * columns, 8 * rows * columns),
+        name="line_parts",
+    )
+    came = [
+        lax.ppermute(part, ALL, [(i, (i + 8 * step) % 32) for i in range(32)])
+        for step, part in zip((1, 2, 3), sends, strict=True)
+    ]
+    return [mine] + came
+
+
+def four_sum(refs, columns):
+    total = refs[0][:, columns]
+    for ref in refs[1:]:
+        total = total + ref[:, columns].astype(F32)
+    return total
+
+
+def finish_first_kernel(*refs):
+    d = refs[4].shape[1]
+    refs[4][...] = four_sum(refs[:4], slice(0, d))
+    refs[5][...] = four_sum(refs[:4], slice(d, 2 * d))
+
+
+def finish_last_kernel(*refs):
+    q, qkv, gains, biases = refs[4:]
+    d = q.shape[1]
+    qkv[:, :d] = q[...]
+    qkv[:, d:] = four_sum(refs[:4], slice(0, 2 * d))
+    sums = four_sum(refs[:4], slice(2 * d, 2 * d + 128)).T
+    gains[...] = sums[0:3]
+    biases[...] = sums[3:6]
+
+
+def finish(kernel, ins, outs):
+    def whole(shape):
+        return pl.BlockSpec(shape, lambda j: (0,) * len(shape))
+
+    return run(
+        kernel,
+        (1,),
+        [(a, whole(a.shape)) for a in ins],
+        [(shaped(s, F32), whole(s)) for s in outs],
+        cost=costs(4 * ins[0].size, 16 * ins[0].size),
+        name="finish",
+    )
 
 
 def turn_kernel(select_ref, a_ref, mine, theirs):
@@ -987,7 +1106,7 @@
     along = lax.axis_index("gy")
     x_at, y_at, core = (along // 2) % 2, along // 4, along % 2
     z_at = lax.axis_index("gx")
-    bits = jnp.stack([x_at, y_at, core]).astype(jnp.int32)
+    bits = jnp.stack([x_at, y_at, core, z_at]).astype(jnp.int32)
 
     norm_cols = jnp.concatenate([norm_gains, norm_biases], axis=0).T
     norm_cols = jnp.pad(norm_cols, ((0, 0), (0, 128 - norm_cols.shape[1])))
@@ -1016,7 +1135,7 @@
 
     line2 = gather_line(pack2)
     near1 = gather_near(line1)
-    mem_t = turned(memory_pad)
+    mem_t = turned(jnp.pad(memory_pad, ((0, -mem_rows % 128), (0, 0))))
     unit1, _ = norm_parts(hidden)
     near1, mem_t, unit1 = fence(near1, mem_t, unit1)
 
@@ -1034,8 +1153,10 @@
     o, lse = attn_fwd((qkv, 0), qkv, blocks, 2 * blocks, lengths, True)
     near2, o, h1, gains, biases = fence(near2, o, h1, gains, biases)
 
-    near2, far2, cores2, h1, o, line3, pack4 = fence(
-        near2, gather_far(near2), swap_cores(near2), h1, o, line3, down_local
+    far2, cores2 = gather_far(near2), swap_cores(near2)
+    h1_turn, o_turn = turn(select, h1), turn(select, o)
+    near2, far2, cores2, h1_turn, o_turn, o, line3, pack4 = fence(
+        near2, far2, cores2, h1_turn, o_turn, o, line3, down_local
     )
 
     wdown = lax.all_gather(pack4, ("gy", "gx"), axis=0, tiled=True)
@@ -1047,16 +1168,15 @@
     h2 = (unit2 * gains[1] + biases[1]).astype(BF)
     wcq, qc = place_dot(second, 3 * d, d, bits, h2, BF)
     wckv, kvc = place_dot(second, 0, 2 * d, bits, memory_pad, BF)
-    h1_t, o_t = turned(h1), turned(o)
+    h1_t, o_t = ((mine, swap(theirs, CORE)) for mine, theirs in (h1_turn, o_turn))
     near3, second, qc, kvc, h2, x1, h1_t, o_t = fence(
         near3, second, qc, kvc, h2, x1, h1_t, o_t
     )
 
     far3, cores3 = gather_far(near3), swap_cores(near3)
     o2, lse2 = attn_fwd((qc, 0), kvc, 0, blocks, slots_used, False)
-    near3, far3, cores3, o2, h2, cotangent = fence(near3, far3, cores3, o2, h2, cotangent)
-
-    third = near3 + far3 + cores3 + swap_cores(far3)
+    near3, cores3, o2, h2, cotangent = fence(near3, cores3, o2, h2, cotangent)
+
     wco, y2 = place_dot(second, 4 * d, d, bits, o2, F32)
     x2 = x1 + y2
     unit3, _ = norm_parts(x2)
@@ -1065,8 +1185,9 @@
     dout = cotangent * valid
     dy3 = dout.astype(BF)
     dy3_other = swap(dy3, CORE)
-    third, h3, x2, o2, dout, dy3, dy3_other = fence(third, h3, x2, o2, dout, dy3, dy3_other)
-
+    far3, h3, x2, o2, dout, dy3, dy3_other = fence(far3, h3, x2, o2, dout, dy3, dy3_other)
+
+    third = near3 + far3 + cores3 + swap_cores(far3)
     wup, g, slope, g_send = feed_up(bits, h3, third, ff)
     wup, g, slope, g_send, h3, o2 = fence(wup, g, slope, g_send, h3, o2)
 
@@ -1077,9 +1198,9 @@
     grad_down, dy3, slope, wdown = fence(grad_down, dy3, slope, wdown)
 
     du, dx2, dy2, sums3 = feed_back(dy3, wdown, slope, wup, x2, gains[2:3], dout, cuts)
-    far1, du, dx2, dy2, g = fence(scatter_far(grad_down), du, dx2, dy2, g)
-
-    got1 = scatter_near(grad_down[0], far1)
+    far1, du, dx2, dy2, g = fence(early_first(grad_down), du, dx2, dy2, g)
+
+    got1 = early_second(grad_down, far1)
     do2 = dot_nt(dy2, wco).astype(BF)
     du_other, do2, du = fence(swap(du, CORE), do2, du)
 
@@ -1091,10 +1212,9 @@
         scatter_far(grad_up), got1, dqc, dkvc, swap(dy2, CORE), dx2
     )
 
-    own_down = scatter_line(grad_down[0], got1)
+    own_down = early_line(grad_down, far1, got1)
     got2 = scatter_near(grad_up[0], far2)
-    dx1, dy1, sums2 = through_norm(dqc, wcq, x1, gains[1:2], dx2)
-    do = dot_nt(dy1, wso).astype(BF)
+    dx1, dy1, do, sums2 = through_norm(dqc, wcq, x1, gains[1:2], dx2, further=wso)
     dqc_other, dkvc_other, dx1, dy1, do, dqc, dkvc = fence(
         swap(dqc, CORE), swap(dkvc, CORE), dx1, dy1, do, dqc, dkvc
     )
@@ -1104,7 +1224,8 @@
             o2_t + (dy2[None], dy2_other[None]),
             h2_t + (dqc, dqc_other),
             mem_t + (dkvc, dkvc_other),
-        ]
+        ],
+        name="wgrad_mid",
     )
     grad_mid, do, dy1 = fence(grad_mid, do, dy1)
 
@@ -1115,8 +1236,8 @@
 
     own_up = scatter_line(grad_up[0], got2)
     got3 = scatter_near(grad_mid[0], far3)
-    grad_hidden, sums1 = through_norm(dqkv, wqkv, hidden, gains[0:1], dx1, low=False)
-    sums = jnp.concatenate([sums1, sums2, sums3], axis=0)
+    grad_hidden, sums1 = through_norm(dqkv, wqkv, hidden, gains[0:1], dx1)
+    sums = jnp.stack([sums1, sums2, sums3], axis=1).reshape(6, d)
     sums = jnp.pad(sums, ((0, 122), (0, 0))).astype(BF)
     dqkv_other, grad_hidden, sums_t = fence(swap(dqkv, CORE), grad_hidden, turned(sums))
 
@@ -1126,42 +1247,48 @@
     grad_a, dqkv, dqkv_other, sums_t = fence(grad_a, dqkv, dqkv_other, sums_t)
 
     grad_b = wgrad([h1_t + (dqkv, dqkv_other, 1, 3)], extra=sums_t)
-    far_a, grad_b, got3, dkvc, own_down = fence(
-        scatter_far(grad_a), grad_b, got3, dkvc, own_down
+    far_a, grad_b, got3, dkvc, own_down, g = fence(
+        scatter_far(grad_a), grad_b, got3, dkvc, own_down, g
     )
 
     got_a = scatter_near(grad_a[0], far_a)
     own_mid = scatter_line(grad_mid[0], got3)
+    result = feed_down(g, wdown, x2, cuts)
+    far_b, got_a, result, own_up, dkvc = fence(
+        scatter_far(grad_b), got_a, result, own_up, dkvc
+    )
+
+    got_b = scatter_near(grad_b[0], far_b)
+    came_a = line_parts(grad_a[0], got_a, bits)
+    own_up = hidden_order(own_up, False, cuts, F32)
     grad_memory = memory_grad(dkvc, wckv, memory.shape[0])
-    far_b, got_a, grad_memory, own_up, g = fence(
-        scatter_far(grad_b), got_a, grad_memory, own_up, g
-    )
-
-    got_b = scatter_near(grad_b[0], far_b)
-    own_a = scatter_line_direct(grad_a[0], got_a, z_at)
-    own_up = hidden_order(own_up, False, cuts, F32)
-    result = feed_down(g, wdown, x2, cuts)
-    got_b, own_a, own_up, result = fence(got_b, own_a, own_up, result)
-
-    own_b = scatter_line_direct(grad_b[0], got_b, z_at)
-    own_qkv = jnp.concatenate([own_a[:, d:], own_b[:, : 2 * d]], axis=1)
+    got_b, own_up, grad_memory = fence(got_b, own_up, grad_memory)
+
+    came_b = line_parts(grad_b[0], got_b, bits)
+    own_mid = own_mid.astype(F32)
+    mids = [own_mid[:, k * d : k * d + w * d] for k, w in ((0, 1), (1, 1), (2, 2))]
+    grad_so, grad_q = finish(finish_first_kernel, came_a, [(rows, d)] * 2)
+    came_b[1], mids, grad_so, grad_q = fence(came_b[1], mids, grad_so, grad_q)
+
+    own_qkv, own_gains, own_biases = finish(
+        finish_last_kernel, came_b + [grad_q], [(rows, 3 * d), (3, rows), (3, rows)]
+    )
     own_down = jnp.concatenate(
         [own_down[:, c * d : (c + 1) * d] for c in range(cuts)], axis=0
     )
-    own_sums = own_b[:, 2 * d : 2 * d + 6].T
     return (
         result,
         grad_hidden,
         grad_memory,
         own_qkv,
-        own_a[:, :d],
-        own_mid[:, d : 2 * d].astype(F32),
-        own_mid[:, 2 * d :].astype(F32),
-        own_mid[:, :d].astype(F32),
+        grad_so,
+        mids[1],
+        mids[2],
+        mids[0],
         own_up,
         own_down.astype(F32),
-        own_sums[0::2],
-        own_sums[1::2],
+        own_gains,
+        own_biases,
     )
 
 

time: 446 us -> 431 us (0.966)
  local copies, waits for them, and re-layouts: 47.2 us -> 39.3 us
  Pallas kernels: 229 us -> 224 us
  waiting for transfers between devices: 50.9 us -> 55.6 us
    ppermute x62 -> x64, waiting for transfers between devices: 45 us -> 51.2 us  [swap(): return lax.ppermute(a, ALL, [(i, i ^ bit) for i in range(32)])]
    unnamed x194 -> x164, local copies, waits for them, and re-layouts: 35.9 us -> 30.1 us
    pallas_call x40 -> x42, Pallas kernels: 229 us -> 224 us  [run(): pl.pallas_call(body, grid_spec=pltpu.PrefetchScalarGridSpec(num_scalar_pr...]
    ppermute x62 -> x64, starting transfers between devices: 39.9 us -> 41.8 us  [swap(): return lax.ppermute(a, ALL, [(i, i ^ bit) for i in range(32)])]
  transfers between devices with their start and end apart: 74 -> 76, of which waited for: 18 -> 26; matrix products, arithmetic and copies ran while one was open for 7% -> 5% of each run, Pallas kernels for 52% -> 53%
where the time goes in v1:
time: 431 us; the launch traced here: 423 us
  Pallas kernels  224 us (52%)
  waiting for transfers between devices  55.6 us (13%)
  starting transfers between devices  51.1 us (12%)
  local copies, waits for them, and re-layouts  39.3 us (9%)
  blocking collectives  21.7 us (5%)
  between operations  16.7 us (4%)
  other arithmetic  12.6 us (3%)
    pallas_call x42, Pallas kernels, run(): pl.pallas_call(body, grid_spec=pltpu.PrefetchScalarGridSpec(num_scalar_pr...  224 us
    ppermute x64, waiting for transfers between devices, swap(): return lax.ppermute(a, ALL, [(i, i ^ bit) for i in range(32)])  51.2 us
    ppermute x64, starting transfers between devices, swap(): return lax.ppermute(a, ALL, [(i, i ^ bit) for i in range(32)])  41.8 us
    unnamed x164, local copies, waits for them, and re-layouts  30.1 us
    all_gather x1, blocking collectives, gather_line(): return lax.all_gather(w, 'gx', axis=0)  21.7 us
    ppermute x6, starting transfers between devices, line_parts(): lax.ppermute(part, ALL, [(i, (i + 8 * step) % 32) for i in range(32)])  8.88 us
  transfers between devices with their start and end apart: 76, of which 26 were waited for; matrix products, arithmetic and copies ran while one was open for 5% of the time, Pallas kernels for 53%

profile of v1, /device:TPU:0, one launch (start us, length us, event | category | flops | bytes accessed | tf_op | source)
XLA Modules:
  0.0 423.0 jit_solution(13099642478273224980)
XLA Ops:
  9.2 21.7 %all-gather = bf16[128,3200]{1,0:T(8,128)(2,1)S(1)} all-gather(bf16[32,3200]{1,0:T(8,128)(2,1)S(1)} %fusion.2), channel_id=2, replica_groups=mesh['gx'=4,'gy'=8] {'gx'}, dimensions={0}, use_global_device_ids=true | all-gather | bytes 1024000 | tf_op jit(solution)/shard_map/all_gather | solution.py:420
  31.9 1.5 collective-permute-start.1
  35.6 3.6 turn.7
  39.7 1.6 subtract_multiply_fusion
  41.6 7.7 %collective-permute-done.1.refs_3_ = bf16[4,32,3200]{2,1,0:T(8,128)(2,1)} collective-permute-done((bf16[4,32,3200]{2,1,0:T(8,128)(2,1)S(1)}, bf16[4,32,3200]{2,1,0:T(8,128)(2,1)}, u32[]{:S(2)}, u32[]{:S(2)}) %collective-permute-start.1) | collective-permute-done | bytes 819232 | tf_op jit(solution)/shard_map/ppermute | solution.py:412
  52.2 1.8 slice.85
  57.6 8.6 %collective-permute-done.3.refs_4_ = bf16[2,32,3200]{2,1,0:T(8,128)(2,1)} collective-permute-done((bf16[2,32,3200]{2,1,0:T(8,128)(2,1)}, bf16[2,32,3200]{2,1,0:T(8,128)(2,1)}, u32[]{:S(2)}, u32[]{:S(2)}) %collective-permute-start.3) | collective-permute-done | bytes 409632 | tf_op jit(solution)/shard_map/ppermute | solution.py:412
  74.3 1.9 add_convert_fusion.2.refs_11_.refs_1_
  76.3 8.8 %place_dot.5 = (bf16[4,8,32,3072]{3,2,1,0:T(8,128)(2,1)}, bf16[512,3072]{1,0:T(8,128)(2,1)S(1)}) custom-call(s32[4]{0:T(128)S(1)} %pad_add_fusion.refs_0_, bf16[4,32,3200]{2,1,0:T(8,128)(2,1)S(1)} %bitcast.46, bf16[4,32,3200]{2,1,0:T(8,128)(2,1)} %collective-permute-done.refs_2_, bf16[4,32,3200]{2,1,0:T(8,128)(2,1)} %collective-permute-done.1.refs_3_, ...), custom_call_target="tpu_custom_call" | custom-call | flops 3221225472 | bytes 12582912 | tf_op jit(solution)/shard_map/place_dot/pallas_call | solution.py:41
  85.1 7.8 %attn_fwd.2 = (bf16[512,1024]{1,0:T(8,128)(2,1)S(1)}, f32[8,2,512]{2,1,0:T(2,128)S(1)}) custom-call(s32[1]{0:T(128)} %copy.34.refs_0_, bf16[512,3072]{1,0:T(8,128)(2,1)S(1)} %get-tuple-element.302.refs_1_.refs_2_.refs_3_, bf16[512,3072]{1,0:T(8,128)(2,1)S(1)} %get-tuple-element.302.refs_1_.refs_2_.refs_3_, ...), custom_call_target="tpu_custom_call" | custom-call | flops 4294967296 | bytes 4194304 | tf_op jit(solution)/shard_map/attn_fwd/pallas_call | solution.py:41
  93.9 5.5 %collective-permute-done.9.refs_3_ = bf16[4,32,5120]{2,1,0:T(8,128)(2,1)S(1)} collective-permute-done((bf16[4,32,5120]{2,1,0:T(8,128)(2,1)}, bf16[4,32,5120]{2,1,0:T(8,128)(2,1)S(1)}, u32[]{:S(2)}, u32[]{:S(2)}) %collective-permute-start.9) | collective-permute-done | bytes 1310752 | tf_op jit(solution)/shard_map/ppermute | solution.py:412
  100.3 2.0 slice.93
  103.7 1.5 collective-permute-start.13
  105.9 1.6 copy-done.13
  108.8 3.0 turn.8
  111.8 3.0 turn.9
  114.8 5.8 %collective-permute-done.12.refs_4_ = bf16[2,32,5120]{2,1,0:T(8,128)(2,1)} collective-permute-done((bf16[2,32,5120]{2,1,0:T(8,128)(2,1)}, bf16[2,32,5120]{2,1,0:T(8,128)(2,1)}, u32[]{:S(2)}, u32[]{:S(2)}) %collective-permute-start.12) | collective-permute-done | bytes 655392 | tf_op jit(solution)/shard_map/ppermute | solution.py:412
  121.8 1.6 collective-permute-start.18
  126.6 4.0 place_dot.6
  131.7 3.7 place_dot.7
  135.4 6.4 %place_dot.8 = (bf16[4,8,32,2048]{3,2,1,0:T(8,128)(2,1)}, bf16[592,2048]{1,0:T(8,128)(2,1)S(1)}) custom-call(s32[4]{0:T(128)S(1)} %pad_add_fusion.refs_0_, bf16[4,32,5120]{2,1,0:T(8,128)(2,1)} %bitcast.2.refs_1_, bf16[4,32,5120]{2,1,0:T(8,128)(2,1)} %collective-permute-done.8.refs_2_, bf16[4,32,5120]{2,1,0:T(8,128)(2,1)S(1)} %collective-permute-done.9.refs_3_, ...), custom_call_target="tpu_custom_call" | custom-call | flops 2483027968 | bytes 8388608 | tf_op jit(solution)/shard_map/place_dot/pallas_call | solution.py:41
  141.8 7.2 %collective-permute-done.18.refs_3_ = bf16[4,32,4096]{2,1,0:T(8,128)(2,1)S(1)} collective-permute-done((bf16[4,32,4096]{2,1,0:T(8,128)(2,1)}, bf16[4,32,4096]{2,1,0:T(8,128)(2,1)S(1)}, u32[]{:S(2)}, u32[]{:S(2)}) %collective-permute-start.18) | collective-permute-done | bytes 1048608 | tf_op jit(solution)/shard_map/ppermute | solution.py:412
  151.6 1.6 collective-permute-start.26
  153.7 10.6 %attn_fwd.3 = (bf16[512,1024]{1,0:T(8,128)(2,1)S(1)}, f32[8,2,512]{2,1,0:T(2,128)S(1)}) custom-call(s32[1]{0:T(128)S(6)} %select_n.102.refs_0_, bf16[512,1024]{1,0:T(8,128)(2,1)S(1)} %get-tuple-element.338.refs_1_, bf16[592,2048]{1,0:T(8,128)(2,1)S(1)} %get-tuple-element.339.refs_2_.refs_3_, bf16[592,2048]{1,0:T(8,128)(2,1)S(1)} %get-tuple-element.339.refs_2_.refs_3_), custom_call_target="tpu_custom_call" | custom-call | flops 4966055936 | bytes 4194304 | tf_op jit(solution)/shard_map/attn_fwd/pallas_call | solution.py:41
  164.3 1.6 fusion.32
  165.9 4.1 place_dot.9
  174.5 12.0 %feed_up.1 = (bf16[4,8,32,4096]{3,2,1,0:T(8,128)(2,1)}, bf16[512,4096]{1,0:T(8,128)(2,1)}, bf16[512,4096]{1,0:T(8,128)(2,1)}, bf16[512,2048]{1,0:T(8,128)(2,1)S(1)}) custom-call(s32[4]{0:T(128)S(1)} %pad_add_fusion.refs_0_, bf16[4,32,4096]{2,1,0:T(8,128)(2,1)S(1)} %bitcast.59, bf16[4,32,4096]{2,1,0:T(8,128)(2,1)S(1)} %collective-permute-done.17.refs_2_, ...), custom_call_target="tpu_custom_call" | custom-call | flops 4294967296 | bytes 25165824 | tf_op jit(solution)/shard_map/feed_up/pallas_call | solution.py:41
  186.9 3.1 turn.10
  190.1 3.0 turn.11
  193.5 3.0 turn.12
  196.7 2.0 collective-permute-done.34.refs_1_
  199.5 8.3 %wgrad_down.1 = (bf16[128,4096]{1,0:T(8,128)(2,1)}, bf16[64,4096]{1,0:T(8,128)(2,1)}, bf16[64,4096]{1,0:T(8,128)(2,1)}, bf16[64,4096]{1,0:T(8,128)(2,1)}, bf16[6...) custom-call(s32[4]{0:T(128)S(1)} %pad_add_fusion.refs_0_, bf16[512,4096]{1,0:T(8,128)(2,1)S(1)} %copy-done, ...), custom_call_target="tpu_custom_call" | custom-call | flops 4294967296 | bytes 8388608 | tf_op jit(solution)/shard_map/wgrad_down/pallas_call | solution.py:41
  213.1 20.0 %feed_back.1 = (bf16[512,4096]{1,0:T(8,128)(2,1)}, f32[512,1024]{1,0:T(8,128)}, bf16[512,1024]{1,0:T(8,128)(2,1)S(1)}, f32[2,1024]{1,0:T(2,128)S(1)}) custom-call(bf16[512,1024]{1,0:T(8,128)(2,1)S(1)} %copy-done.18, bf16[1024,4096]{1,0:T(8,128)(2,1)} %all-gather.7.cloned.1.call-done.refs_1_, bf16[512,4096]{1,0:T(8,128)(2,1)} %get-tuple-element.404.refs_2_, ...), custom_call_target="tpu_custom_call" | custom-call | flops 8589934592 | bytes 33554432 | tf_op jit(solution)/shard_map/feed_back/pallas_call | solution.py:41
  234.1 2.2 pass_on.5
  238.4 2.3 convolution_convert_fusion.refs_5_
  241.3 6.8 %wgrad.3 = (bf16[384,4096]{1,0:T(8,128)(2,1)}, bf16[64,4096]{1,0:T(8,128)(2,1)}, bf16[64,4096]{1,0:T(8,128)(2,1)}) custom-call(bf16[512,512]{1,0:T(8,128)(2,1)S(1)} %copy-done.55, bf16[512,512]{1,0:T(8,128)(2,1)S(1)} %collective-permute-done.33.refs_1_, bf16[1,512,4096]{2,1,0:T(8,128)(2,1)S(1)} %bitcast.54, bf16[1,512,4096]{2,1,0:T(8,128)(2,1)S(1)} %bitcast.55), custom_call_target="tpu_custom_call" | custom-call | flops 4294967296 | bytes 12582912 | tf_op jit(solution)/shard_map/wgrad/pallas_call | solution.py:41
  250.7 16.8 %attn_bwd.2 = (bf16[1,512,1024]{2,1,0:T(8,128)(2,1)S(1)}, bf16[2,592,1024]{2,1,0:T(8,128)(2,1)S(1)}) custom-call(s32[1]{0:T(128)S(6)} %select_n.102.refs_0_, bf16[512,1024]{1,0:T(8,128)(2,1)} %copy-done.51, bf16[592,2048]{1,0:T(8,128)(2,1)} %copy-done.49, bf16[592,2048]{1,0:T(8,128)(2,1)} %copy-done.49, bf16[512,1024]{1,0:T(8,128)(2,1)} %copy-done.30, ...), custom_call_target="tpu_custom_call" | custom-call | flops 12415139840 | bytes 8388608 | tf_op jit(solution)/shard_map/attn_bwd/pallas_call | solution.py:41
  268.5 5.2 %pass_on.6 = (bf16[128,4096]{1,0:T(8,128)(2,1)}, bf16[128,4096]{1,0:T(8,128)(2,1)}) custom-call(bf16[384,4096]{1,0:T(8,128)(2,1)} %get-tuple-element.461.refs_0_.refs_1_, bf16[384,4096]{1,0:T(8,128)(2,1)} %get-tuple-element.461.refs_0_.refs_1_, bf16[64,4096]{1,0:T(8,128)(2,1)} %copy-done.61, bf16[64,4096]{1,0:T(8,128)(2,1)} %copy-done.62), custom_call_target="tpu_custom_call" | custom-call | flops 524288 | bytes 5242880 | tf_op jit(solution)/shard_map/pass_on/pallas_call | solution.py:41
  275.3 4.7 %through_norm.2 = (f32[512,1024]{1,0:T(8,128)S(1)}, bf16[512,1024]{1,0:T(8,128)(2,1)S(1)}, bf16[512,1024]{1,0:T(8,128)(2,1)S(1)}, f32[2,1024]{1,0:T(2,128)S(1)}) custom-call(bf16[1,512,1024]{2,1,0:T(8,128)(2,1)S(1)} %get-tuple-element.445.refs_0_.refs_6_, bf16[1024,1024]{1,0:T(8,128)(2,1)S(1)} %bitcast.48, f32[512,1024]{1,0:T(8,128)S(1)} %copy-done.4, ...), custom_call_target="tpu_custom_call" | custom-call | flops 1073741824 | bytes 10485760 | tf_op jit(solution)/shard_map/through_norm/pallas_call | solution.py:41
  283.2 11.5 %wgrad_mid.1 = (bf16[384,4096]{1,0:T(8,128)(2,1)}, bf16[64,4096]{1,0:T(8,128)(2,1)}, bf16[64,4096]{1,0:T(8,128)(2,1)}) custom-call(bf16[512,512]{1,0:T(8,128)(2,1)} %get-tuple-element.381.refs_0_, bf16[512,512]{1,0:T(8,128)(2,1)} %copy-done.80, bf16[1,512,1024]{2,1,0:T(8,128)(2,1)} %bitcast.60, bf16[1,512,1024]{2,1,0:T(8,128)(2,1)} %bitcast.66, ...), custom_call_target="tpu_custom_call" | custom-call | flops 4294967296 | bytes 12582912 | tf_op jit(solution)/shard_map/wgrad_mid/pallas_call | solution.py:41
  294.8 2.5 plane_sum.3
  300.0 12.5 %attn_bwd.3.refs_0_.refs_6_.refs_2_ = bf16[3,512,1024]{2,1,0:T(8,128)(2,1)} custom-call(s32[1]{0:T(128)} %copy.34.refs_0_, bf16[512,3072]{1,0:T(8,128)(2,1)} %copy-done.56, bf16[512,3072]{1,0:T(8,128)(2,1)} %copy-done.56, bf16[512,3072]{1,0:T(8,128)(2,1)} %copy-done.56, bf16[512,1024]{1,0:T(8,128)(2,1)} %copy-done.27, bf16[512,1024]{1,0:T(8,128)(2,1)} %copy-done.53, ...), custom_call_target="tpu_custom_call" | custom-call | flops 10737418240 | bytes 8388608 | tf_op jit(solution)/shard_map/attn_bwd/pallas_call | solution.py:41
  313.6 2.9 plane_sum.4
  316.5 3.1 pass_on.7
  321.7 2.8 copy-done.16
  324.5 9.8 %through_norm.3 = (f32[512,1024]{1,0:T(8,128)}, f32[2,1024]{1,0:T(2,128)S(1)}) custom-call(bf16[3,512,1024]{2,1,0:T(8,128)(2,1)} %attn_bwd.3.refs_0_.refs_6_.refs_2_, bf16[1024,3072]{1,0:T(8,128)(2,1)S(1)} %bitcast.41, f32[512,1024]{1,0:T(8,128)S(1)} %copy-done.2, f32[1,1024]{1,0:T(1,128)S(1)} %get-tuple-element.574.refs_3_, f32[512,1024]{1,0:T(8,128)S(1)} %copy-done.23), custom_call_target="tpu_custom_call" | custom-call | flops 3221225472 | bytes 14680064 | tf_op jit(solution)/shard_map/through_norm/pallas_call | solution.py:41
  334.5 1.6 copy-done.15
  336.1 2.2 turn.13
  338.3 1.6 collective-permute-done.53.refs_5_
  344.0 5.5 %wgrad.4 = (bf16[384,2048]{1,0:T(8,128)(2,1)}, bf16[64,2048]{1,0:T(8,128)(2,1)}, bf16[64,2048]{1,0:T(8,128)(2,1)}) custom-call(bf16[512,512]{1,0:T(8,128)(2,1)S(1)} %copy-done.38, bf16[512,512]{1,0:T(8,128)(2,1)S(1)} %copy-done.42, bf16[1,512,1024]{2,1,0:T(8,128)(2,1)S(1)} %bitcast.49, bf16[1,512,1024]{2,1,0:T(8,128)(2,1)} %bitcast.26.refs_3_, ...), custom_call_target="tpu_custom_call" | custom-call | flops 2147483648 | bytes 6291456 | tf_op jit(solution)/shard_map/wgrad/pallas_call | solution.py:41
  351.5 5.2 %wgrad.5 = (bf16[384,2176]{1,0:T(8,128)(2,1)}, bf16[64,2176]{1,0:T(8,128)(2,1)}, bf16[64,2176]{1,0:T(8,128)(2,1)}) custom-call(bf16[512,512]{1,0:T(8,128)(2,1)S(1)} %copy-done.37, bf16[512,512]{1,0:T(8,128)(2,1)S(1)} %copy-done.40, bf16[3,512,1024]{2,1,0:T(8,128)(2,1)} %attn_bwd.3.refs_0_.refs_6_.refs_2_, ...), custom_call_target="tpu_custom_call" | custom-call | flops 2281701376 | bytes 6684672 | tf_op jit(solution)/shard_map/wgrad/pallas_call | solution.py:41
  359.3 2.9 plane_sum.5
  362.3 2.5 pass_on.8
  368.8 2.2 copy-done.1
  371.0 3.5 copy-done.11
  374.5 8.2 %feed_down.1 = f32[512,1024]{1,0:T(8,128)} custom-call(bf16[512,4096]{1,0:T(8,128)(2,1)S(1)} %copy-done.1, bf16[1024,4096]{1,0:T(8,128)(2,1)S(1)} %copy-done.11, f32[512,1024]{1,0:T(8,128)S(1)} %copy-done.6), custom_call_target="tpu_custom_call" | custom-call | flops 4294967296 | bytes 13631488 | tf_op jit(solution)/shard_map/feed_down/pallas_call | solution.py:41
  384.3 1.6 pass_on.9
  390.7 2.7 collective-permute-start.66
  394.0 1.7 hidden_order.3
  395.7 6.1 %memory_grad.1 = f32[588,1024]{1,0:T(8,128)} custom-call(bf16[2,592,1024]{2,1,0:T(8,128)(2,1)S(1)} %copy-done.48, bf16[1024,2048]{1,0:T(8,128)(2,1)S(1)} %bitcast.53), custom_call_target="tpu_custom_call" | custom-call | flops 2483027968 | bytes 10797056 | tf_op jit(solution)/shard_map/memory_grad/pallas_call | solution.py:41
  405.7 1.9 collective-permute-start.69
  407.7 1.6 slice.119
  409.3 1.6 fusion.36
  411.1 4.0 collective-permute-done.68.refs_2_
  (351 shorter events, 87.0 us)
Async XLA Ops:
  7.2 60.0 %all-gather.9.cloned.1.call-start = ((), (), s32[]{:S(2)}) async-start(), calls=%async_computation.7 | async-start | bytes 1638400 | tf_op jit(solution)/shard_map/all_gather | solution.py:420
  31.9 17.5 %collective-permute-start.1 = (bf16[4,32,3200]{2,1,0:T(8,128)(2,1)S(1)}, bf16[4,32,3200]{2,1,0:T(8,128)(2,1)}, u32[]{:S(2)}, u32[]{:S(2)}) collective-permute-start(bf16[4,32,3200]{2,1,0:T(8,128)(2,1)S(1)} %bitcast.42), channel_id=1, source_target_pairs={{0,4},{1,5},{2,6},{3,7},{4,0},{5,1},{6,2},{7,3},{8,12},{9,13},{10,... | collective-permute-start | bytes 2457608 | tf_op jit(solution)/shard_map/ppermute | solution.py:412
  33.4 17.2 %collective-permute-start = (bf16[4,32,3200]{2,1,0:T(8,128)(2,1)S(1)}, bf16[4,32,3200]{2,1,0:T(8,128)(2,1)}, u32[]{:S(2)}, u32[]{:S(2)}) collective-permute-start(bf16[4,32,3200]{2,1,0:T(8,128)(2,1)S(1)} %bitcast.43), channel_id=1, source_target_pairs={{0,2},{1,3},{2,0},{3,1},{4,6},{5,7},{6,4},{7,5},{8,10},{9,11},{10,... | collective-permute-start | bytes 2457608 | tf_op jit(solution)/shard_map/ppermute | solution.py:412
  34.9 79.9 %all-gather.11.cloned.1.call-start = ((), (), s32[]{:S(2)}) async-start(), calls=%async_computation.8 | async-start | bytes 1310720 | tf_op jit(solution)/shard_map/all_gather | solution.py:420
  50.6 16.5 %collective-permute-start.5 = (bf16[4,32,3200]{2,1,0:T(8,128)(2,1)S(1)}, bf16[4,32,3200]{2,1,0:T(8,128)(2,1)}, u32[]{:S(2)}, u32[]{:S(2)}) collective-permute-start(bf16[4,32,3200]{2,1,0:T(8,128)(2,1)S(1)} %bitcast.44), channel_id=1, source_target_pairs={{0,1},{1,0},{2,3},{3,2},{4,5},{5,4},{6,7},{7,6},{8,9},{9,8},{10,11... | collective-permute-start | bytes 2457608 | tf_op jit(solution)/shard_map/ppermute | solution.py:412
  50.6 16.5 %collective-permute-start.6 = (bf16[4,32,3200]{2,1,0:T(8,128)(2,1)}, bf16[4,32,3200]{2,1,0:T(8,128)(2,1)}, u32[]{:S(2)}, u32[]{:S(2)}) collective-permute-start(bf16[4,32,3200]{2,1,0:T(8,128)(2,1)} %collective-permute-done.refs_2_), channel_id=1, source_target_pairs={{0,1},{1,0},{2,3},{3,2},{4,5},{5,4},{6,7},{7,6},{8,9},{9,8},{10,11... | collective-permute-start | bytes 2457608 | tf_op jit(solution)/shard_map/ppermute | solution.py:412
  51.1 16.0 %collective-permute-start.7 = (bf16[4,32,3200]{2,1,0:T(8,128)(2,1)}, bf16[4,32,3200]{2,1,0:T(8,128)(2,1)}, u32[]{:S(2)}, u32[]{:S(2)}) collective-permute-start(bf16[4,32,3200]{2,1,0:T(8,128)(2,1)} %collective-permute-done.1.refs_3_), channel_id=1, source_target_pairs={{0,1},{1,0},{2,3},{3,2},{4,5},{5,4},{6,7},{7,6},{8,9},{9,8},{10,11... | collective-permute-start | bytes 2457608 | tf_op jit(solution)/shard_map/ppermute | solution.py:412
  53.9 12.2 %collective-permute-start.3 = (bf16[2,32,3200]{2,1,0:T(8,128)(2,1)}, bf16[2,32,3200]{2,1,0:T(8,128)(2,1)}, u32[]{:S(2)}, u32[]{:S(2)}) collective-permute-start(bf16[2,32,3200]{2,1,0:T(8,128)(2,1)} %slice.85), channel_id=1, source_target_pairs={{0,2},{1,3},{2,0},{3,1},{4,6},{5,7},{6,4},{7,5},{8,10},{9,11},{10,... | collective-permute-start | bytes 1228808 | tf_op jit(solution)/shard_map/ppermute | solution.py:412
  55.4 11.7 %collective-permute-start.4 = (bf16[2,32,3200]{2,1,0:T(8,128)(2,1)S(1)}, bf16[2,32,3200]{2,1,0:T(8,128)(2,1)}, u32[]{:S(2)}, u32[]{:S(2)}) collective-permute-start(bf16[2,32,3200]{2,1,0:T(8,128)(2,1)S(1)} %slice.86), channel_id=1, source_target_pairs={{0,4},{1,5},{2,6},{3,7},{4,0},{5,1},{6,2},{7,3},{8,12},{9,13},{10,... | collective-permute-start | bytes 1228808 | tf_op jit(solution)/shard_map/ppermute | solution.py:412
  68.5 31.0 %collective-permute-start.9 = (bf16[4,32,5120]{2,1,0:T(8,128)(2,1)}, bf16[4,32,5120]{2,1,0:T(8,128)(2,1)S(1)}, u32[]{:S(2)}, u32[]{:S(2)}) collective-permute-start(bf16[4,32,5120]{2,1,0:T(8,128)(2,1)} %bitcast.2.refs_1_), channel_id=1, source_target_pairs={{0,4},{1,5},{2,6},{3,7},{4,0},{5,1},{6,2},{7,3},{8,12},{9,13},{10,... | collective-permute-start | bytes 3932168 | tf_op jit(solution)/shard_map/ppermute | solution.py:412
  69.0 30.8 %collective-permute-start.8 = (bf16[4,32,5120]{2,1,0:T(8,128)(2,1)}, bf16[4,32,5120]{2,1,0:T(8,128)(2,1)}, u32[]{:S(2)}, u32[]{:S(2)}) collective-permute-start(bf16[4,32,5120]{2,1,0:T(8,128)(2,1)} %bitcast.2.refs_1_), channel_id=1, source_target_pairs={{0,2},{1,3},{2,0},{3,1},{4,6},{5,7},{6,4},{7,5},{8,10},{9,11},{10,... | collective-permute-start | bytes 3932168 | tf_op jit(solution)/shard_map/ppermute | solution.py:412
  69.6 138.2 %all-gather.7.cloned.1.call-start = ((), (), s32[]{:S(2)}) async-start(), calls=%async_computation.3 | async-start | bytes 8650752 | tf_op jit(solution)/shard_map/all_gather | solution.py:1162
  99.8 21.1 %collective-permute-start.14 = (bf16[4,32,5120]{2,1,0:T(8,128)(2,1)}, bf16[4,32,5120]{2,1,0:T(8,128)(2,1)}, u32[]{:S(2)}, u32[]{:S(2)}) collective-permute-start(bf16[4,32,5120]{2,1,0:T(8,128)(2,1)} %bitcast.2.refs_1_), channel_id=1, source_target_pairs={{0,1},{1,0},{2,3},{3,2},{4,5},{5,4},{6,7},{7,6},{8,9},{9,8},{10,11... | collective-permute-start | bytes 3932168 | tf_op jit(solution)/shard_map/ppermute | solution.py:412
  99.8 21.1 %collective-permute-start.15 = (bf16[4,32,5120]{2,1,0:T(8,128)(2,1)}, bf16[4,32,5120]{2,1,0:T(8,128)(2,1)}, u32[]{:S(2)}, u32[]{:S(2)}) collective-permute-start(bf16[4,32,5120]{2,1,0:T(8,128)(2,1)} %collective-permute-done.8.refs_2_), channel_id=1, source_target_pairs={{0,1},{1,0},{2,3},{3,2},{4,5},{5,4},{6,7},{7,6},{8,9},{9,8},{10,11... | collective-permute-start | bytes 3932168 | tf_op jit(solution)/shard_map/ppermute | solution.py:412
  100.3 20.6 %collective-permute-start.16 = (bf16[4,32,5120]{2,1,0:T(8,128)(2,1)S(1)}, bf16[4,32,5120]{2,1,0:T(8,128)(2,1)}, u32[]{:S(2)}, u32[]{:S(2)}) collective-permute-start(bf16[4,32,5120]{2,1,0:T(8,128)(2,1)S(1)} %collective-permute-done.9.refs_3_), channel_id=1, source_target_pairs={{0,1},{1,0},{2,3},{3,2},{4,5},{5,4},{6,7},{7,6},{8,9},{9,8},{10,11... | collective-permute-start | bytes 3932168 | tf_op jit(solution)/shard_map/ppermute | solution.py:412
  103.2 17.5 %collective-permute-start.12 = (bf16[2,32,5120]{2,1,0:T(8,128)(2,1)}, bf16[2,32,5120]{2,1,0:T(8,128)(2,1)}, u32[]{:S(2)}, u32[]{:S(2)}) collective-permute-start(bf16[2,32,5120]{2,1,0:T(8,128)(2,1)} %slice.92), channel_id=1, source_target_pairs={{0,2},{1,3},{2,0},{3,1},{4,6},{5,7},{6,4},{7,5},{8,10},{9,11},{10,... | collective-permute-start | bytes 1966088 | tf_op jit(solution)/shard_map/ppermute | solution.py:412
  103.7 17.2 %collective-permute-start.13 = (bf16[2,32,5120]{2,1,0:T(8,128)(2,1)}, bf16[2,32,5120]{2,1,0:T(8,128)(2,1)}, u32[]{:S(2)}, u32[]{:S(2)}) collective-permute-start(bf16[2,32,5120]{2,1,0:T(8,128)(2,1)} %slice.93), channel_id=1, source_target_pairs={{0,4},{1,5},{2,6},{3,7},{4,0},{5,1},{6,2},{7,3},{8,12},{9,13},{10,... | collective-permute-start | bytes 1966088 | tf_op jit(solution)/shard_map/ppermute | solution.py:412
  120.9 235.8 %reduce-scatter.4.cloned.1.call-start = ((), (), s32[]{:S(2)}) async-start(), calls=%async_computation.4 | async-start | bytes 1310720 | tf_op jit(solution)/shard_map/reduce_scatter | solution.py:895
  121.8 27.3 %collective-permute-start.18 = (bf16[4,32,4096]{2,1,0:T(8,128)(2,1)}, bf16[4,32,4096]{2,1,0:T(8,128)(2,1)S(1)}, u32[]{:S(2)}, u32[]{:S(2)}) collective-permute-start(bf16[4,32,4096]{2,1,0:T(8,128)(2,1)} %bitcast.56), channel_id=1, source_target_pairs={{0,4},{1,5},{2,6},{3,7},{4,0},{5,1},{6,2},{7,3},{8,12},{9,13},{10,... | collective-permute-start | bytes 3145736 | tf_op jit(solution)/shard_map/ppermute | solution.py:412
  123.3 27.0 %collective-permute-start.17 = (bf16[4,32,4096]{2,1,0:T(8,128)(2,1)}, bf16[4,32,4096]{2,1,0:T(8,128)(2,1)S(1)}, u32[]{:S(2)}, u32[]{:S(2)}) collective-permute-start(bf16[4,32,4096]{2,1,0:T(8,128)(2,1)} %bitcast.57), channel_id=1, source_target_pairs={{0,2},{1,3},{2,0},{3,1},{4,6},{5,7},{6,4},{7,5},{8,10},{9,11},{10,... | collective-permute-start | bytes 3145736 | tf_op jit(solution)/shard_map/ppermute | solution.py:412
  124.8 17.0 %collective-permute-start.21 = (bf16[512,512]{1,0:T(8,128)(2,1)}, bf16[512,512]{1,0:T(8,128)(2,1)S(1)}, u32[]{:S(2)}, u32[]{:S(2)}) collective-permute-start(bf16[512,512]{1,0:T(8,128)(2,1)} %get-tuple-element.330), channel_id=1, source_target_pairs={{0,1},{1,0},{2,3},{3,2},{4,5},{5,4},{6,7},{7,6},{8,9},{9,8},{10,11... | collective-permute-start | bytes 1572872 | tf_op jit(solution)/shard_map/ppermute | solution.py:412
  124.8 17.0 %collective-permute-start.22 = (bf16[512,512]{1,0:T(8,128)(2,1)}, bf16[512,512]{1,0:T(8,128)(2,1)S(1)}, u32[]{:S(2)}, u32[]{:S(2)}) collective-permute-start(bf16[512,512]{1,0:T(8,128)(2,1)} %get-tuple-element.332), channel_id=1, source_target_pairs={{0,1},{1,0},{2,3},{3,2},{4,5},{5,4},{6,7},{7,6},{8,9},{9,8},{10,11... | collective-permute-start | bytes 1572872 | tf_op jit(solution)/shard_map/ppermute | solution.py:412
  150.3 14.0 %collective-permute-start.23 = (bf16[4,32,4096]{2,1,0:T(8,128)(2,1)S(1)}, bf16[4,32,4096]{2,1,0:T(8,128)(2,1)S(1)}, u32[]{:S(2)}, u32[]{:S(2)}) collective-permute-start(bf16[4,32,4096]{2,1,0:T(8,128)(2,1)S(1)} %bitcast.58), channel_id=1, source_target_pairs={{0,1},{1,0},{2,3},{3,2},{4,5},{5,4},{6,7},{7,6},{8,9},{9,8},{10,11... | collective-permute-start | bytes 3145736 | tf_op jit(solution)/shard_map/ppermute | solution.py:412
  150.3 14.0 %collective-permute-start.24 = (bf16[4,32,4096]{2,1,0:T(8,128)(2,1)S(1)}, bf16[4,32,4096]{2,1,0:T(8,128)(2,1)S(1)}, u32[]{:S(2)}, u32[]{:S(2)}) collective-permute-start(bf16[4,32,4096]{2,1,0:T(8,128)(2,1)S(1)} %collective-permute-done.17.refs_2_), channel_id=1, source_target_pairs={{0,1},{1,0},{2,3},{3,2},{4,5},{5,4},{6,7},{7,6},{8,9},{9,8},{10,11... | collective-permute-start | bytes 3145736 | tf_op jit(solution)/shard_map/ppermute | solution.py:412
  150.8 13.5 %collective-permute-start.25 = (bf16[4,32,4096]{2,1,0:T(8,128)(2,1)S(1)}, bf16[4,32,4096]{2,1,0:T(8,128)(2,1)S(1)}, u32[]{:S(2)}, u32[]{:S(2)}) collective-permute-start(bf16[4,32,4096]{2,1,0:T(8,128)(2,1)S(1)} %collective-permute-done.18.refs_3_), channel_id=1, source_target_pairs={{0,1},{1,0},{2,3},{3,2},{4,5},{5,4},{6,7},{7,6},{8,9},{9,8},{10,11... | collective-permute-start | bytes 3145736 | tf_op jit(solution)/shard_map/ppermute | solution.py:412
  151.6 20.1 %collective-permute-start.26 = (bf16[2,32,4096]{2,1,0:T(8,128)(2,1)S(1)}, bf16[2,32,4096]{2,1,0:T(8,128)(2,1)S(1)}, u32[]{:S(2)}, u32[]{:S(2)}) collective-permute-start(bf16[2,32,4096]{2,1,0:T(8,128)(2,1)S(1)} %slice.100), channel_id=1, source_target_pairs={{0,2},{1,3},{2,0},{3,1},{4,6},{5,7},{6,4},{7,5},{8,10},{9,11},{10,... | collective-permute-start | bytes 1572872 | tf_op jit(solution)/shard_map/ppermute | solution.py:412
  153.1 18.5 %collective-permute-start.27 = (bf16[2,32,4096]{2,1,0:T(8,128)(2,1)S(1)}, bf16[2,32,4096]{2,1,0:T(8,128)(2,1)S(1)}, u32[]{:S(2)}, u32[]{:S(2)}) collective-permute-start(bf16[2,32,4096]{2,1,0:T(8,128)(2,1)S(1)} %slice.101), channel_id=1, source_target_pairs={{0,4},{1,5},{2,6},{3,7},{4,0},{5,1},{6,2},{7,3},{8,12},{9,13},{10,... | collective-permute-start | bytes 1572872 | tf_op jit(solution)/shard_map/ppermute | solution.py:412
  186.5 12.1 %collective-permute-start.31 = (bf16[512,2048]{1,0:T(8,128)(2,1)S(1)}, bf16[512,2048]{1,0:T(8,128)(2,1)S(1)}, u32[]{:S(2)}, u32[]{:S(2)}) collective-permute-start(bf16[512,2048]{1,0:T(8,128)(2,1)S(1)} %get-tuple-element.370), channel_id=1, source_target_pairs={{0,1},{1,0},{2,3},{3,2},{4,5},{5,4},{6,7},{7,6},{8,9},{9,8},{10,11... | collective-permute-start | bytes 6291464 | tf_op jit(solution)/shard_map/ppermute | solution.py:412
  207.8 25.4 %collective-permute-start.35 = (bf16[64,4096]{1,0:T(8,128)(2,1)}, bf16[64,4096]{1,0:T(8,128)(2,1)S(1)}, u32[]{:S(2)}, u32[]{:S(2)}) collective-permute-start(bf16[64,4096]{1,0:T(8,128)(2,1)} %get-tuple-element.398), channel_id=1, source_target_pairs={{0,2},{1,3},{2,0},{3,1},{4,6},{5,7},{6,4},{7,5},{8,10},{9,11},{10,... | collective-permute-start | bytes 1572872 | tf_op jit(solution)/shard_map/ppermute | solution.py:412
  208.7 24.5 %collective-permute-start.36 = (bf16[64,4096]{1,0:T(8,128)(2,1)}, bf16[64,4096]{1,0:T(8,128)(2,1)S(1)}, u32[]{:S(2)}, u32[]{:S(2)}) collective-permute-start(bf16[64,4096]{1,0:T(8,128)(2,1)} %get-tuple-element.399), channel_id=1, source_target_pairs={{0,4},{1,5},{2,6},{3,7},{4,0},{5,1},{6,2},{7,3},{8,12},{9,13},{10,... | collective-permute-start | bytes 1572872 | tf_op jit(solution)/shard_map/ppermute | solution.py:412
  209.8 23.4 %collective-permute-start.37 = (bf16[64,4096]{1,0:T(8,128)(2,1)}, bf16[64,4096]{1,0:T(8,128)(2,1)S(1)}, u32[]{:S(2)}, u32[]{:S(2)}) collective-permute-start(bf16[64,4096]{1,0:T(8,128)(2,1)} %get-tuple-element.400), channel_id=1, source_target_pairs={{0,2},{1,3},{2,0},{3,1},{4,6},{5,7},{6,4},{7,5},{8,10},{9,11},{10,... | collective-permute-start | bytes 1572872 | tf_op jit(solution)/shard_map/ppermute | solution.py:412
  211.3 22.6 %collective-permute-start.38 = (bf16[64,4096]{1,0:T(8,128)(2,1)}, bf16[64,4096]{1,0:T(8,128)(2,1)S(1)}, u32[]{:S(2)}, u32[]{:S(2)}) collective-permute-start(bf16[64,4096]{1,0:T(8,128)(2,1)} %get-tuple-element.401), channel_id=1, source_target_pairs={{0,4},{1,5},{2,6},{3,7},{4,0},{5,1},{6,2},{7,3},{8,12},{9,13},{10,... | collective-permute-start | bytes 1572872 | tf_op jit(solution)/shard_map/ppermute | solution.py:412
  234.0 7.4 %collective-permute-start.39 = (bf16[512,4096]{1,0:T(8,128)(2,1)}, bf16[512,4096]{1,0:T(8,128)(2,1)S(1)}, u32[]{:S(2)}, u32[]{:S(2)}) collective-permute-start(bf16[512,4096]{1,0:T(8,128)(2,1)} %get-tuple-element.414), channel_id=1, source_target_pairs={{0,1},{1,0},{2,3},{3,2},{4,5},{5,4},{6,7},{7,6},{8,9},{9,8},{10,11... | collective-permute-start | bytes 12582920 | tf_op jit(solution)/shard_map/ppermute | solution.py:412
  236.3 31.2 %collective-permute-start.42 = (bf16[64,4096]{1,0:T(8,128)(2,1)S(1)}, bf16[64,4096]{1,0:T(8,128)(2,1)S(1)}, u32[]{:S(2)}, u32[]{:S(2)}) collective-permute-start(bf16[64,4096]{1,0:T(8,128)(2,1)S(1)} %get-tuple-element.427), channel_id=1, source_target_pairs={{0,2},{1,3},{2,0},{3,1},{4,6},{5,7},{6,4},{7,5},{8,10},{9,11},{10,... | collective-permute-start | bytes 1572872 | tf_op jit(solution)/shard_map/ppermute | solution.py:412
  237.3 30.3 %collective-permute-start.43 = (bf16[64,4096]{1,0:T(8,128)(2,1)S(1)}, bf16[64,4096]{1,0:T(8,128)(2,1)S(1)}, u32[]{:S(2)}, u32[]{:S(2)}) collective-permute-start(bf16[64,4096]{1,0:T(8,128)(2,1)S(1)} %get-tuple-element.428), channel_id=1, source_target_pairs={{0,4},{1,5},{2,6},{3,7},{4,0},{5,1},{6,2},{7,3},{8,12},{9,13},{10,... | collective-permute-start | bytes 1572872 | tf_op jit(solution)/shard_map/ppermute | solution.py:412
  248.1 19.4 %collective-permute-start.40 = (bf16[64,4096]{1,0:T(8,128)(2,1)}, bf16[64,4096]{1,0:T(8,128)(2,1)S(1)}, u32[]{:S(2)}, u32[]{:S(2)}) collective-permute-start(bf16[64,4096]{1,0:T(8,128)(2,1)} %get-tuple-element.421), channel_id=1, source_target_pairs={{0,2},{1,3},{2,0},{3,1},{4,6},{5,7},{6,4},{7,5},{8,10},{9,11},{10,... | collective-permute-start | bytes 1572872 | tf_op jit(solution)/shard_map/ppermute | solution.py:412
  249.2 18.3 %collective-permute-start.41 = (bf16[64,4096]{1,0:T(8,128)(2,1)}, bf16[64,4096]{1,0:T(8,128)(2,1)S(1)}, u32[]{:S(2)}, u32[]{:S(2)}) collective-permute-start(bf16[64,4096]{1,0:T(8,128)(2,1)} %get-tuple-element.422), channel_id=1, source_target_pairs={{0,4},{1,5},{2,6},{3,7},{4,0},{5,1},{6,2},{7,3},{8,12},{9,13},{10,... | collective-permute-start | bytes 1572872 | tf_op jit(solution)/shard_map/ppermute | solution.py:412
  250.7 16.9 %collective-permute-start.44 = (bf16[512,1024]{1,0:T(8,128)(2,1)S(1)}, bf16[512,1024]{1,0:T(8,128)(2,1)S(1)}, u32[]{:S(2)}, u32[]{:S(2)}) collective-permute-start(bf16[512,1024]{1,0:T(8,128)(2,1)S(1)} %get-tuple-element.420), channel_id=1, source_target_pairs={{0,1},{1,0},{2,3},{3,2},{4,5},{5,4},{6,7},{7,6},{8,9},{9,8},{10,11... | collective-permute-start | bytes 3145736 | tf_op jit(solution)/shard_map/ppermute | solution.py:412
  267.6 13.8 %collective-permute-start.46 = (bf16[2,592,1024]{2,1,0:T(8,128)(2,1)S(1)}, bf16[2,592,1024]{2,1,0:T(8,128)(2,1)S(1)}, u32[]{:S(2)}, u32[]{:S(2)}) collective-permute-start(bf16[2,592,1024]{2,1,0:T(8,128)(2,1)S(1)} %get-tuple-element.524.refs_10_.refs_0_), channel_id=1, source_target_pairs={{0,1},{1,0},{2,3},{3,2},{4,5},{5,4},{6,7},{7,6},{8,9},{9,8},{10,11... | collective-permute-start | bytes 7274504 | tf_op jit(solution)/shard_map/ppermute | solution.py:412
  268.2 13.2 %collective-permute-start.45 = (bf16[1,512,1024]{2,1,0:T(8,128)(2,1)S(1)}, bf16[1,512,1024]{2,1,0:T(8,128)(2,1)S(1)}, u32[]{:S(2)}, u32[]{:S(2)}) collective-permute-start(bf16[1,512,1024]{2,1,0:T(8,128)(2,1)S(1)} %get-tuple-element.445.refs_0_.refs_6_), channel_id=1, source_target_pairs={{0,1},{1,0},{2,3},{3,2},{4,5},{5,4},{6,7},{7,6},{8,9},{9,8},{10,11... | collective-permute-start | bytes 3145736 | tf_op jit(solution)/shard_map/ppermute | solution.py:412
  273.8 38.7 %collective-permute-start.50 = (bf16[128,4096]{1,0:T(8,128)(2,1)}, bf16[128,4096]{1,0:T(8,128)(2,1)}, u32[]{:S(2)}, u32[]{:S(2)}) collective-permute-start(bf16[128,4096]{1,0:T(8,128)(2,1)} %get-tuple-element.464), channel_id=1, source_target_pairs={{0,2},{1,3},{2,0},{3,1},{4,6},{5,7},{6,4},{7,5},{8,10},{9,11},{10,... | collective-permute-start | bytes 3145736 | tf_op jit(solution)/shard_map/ppermute | solution.py:412
  274.4 38.1 %collective-permute-start.51 = (bf16[128,4096]{1,0:T(8,128)(2,1)}, bf16[128,4096]{1,0:T(8,128)(2,1)}, u32[]{:S(2)}, u32[]{:S(2)}) collective-permute-start(bf16[128,4096]{1,0:T(8,128)(2,1)} %get-tuple-element.465), channel_id=1, source_target_pairs={{0,4},{1,5},{2,6},{3,7},{4,0},{5,1},{6,2},{7,3},{8,12},{9,13},{10,... | collective-permute-start | bytes 3145736 | tf_op jit(solution)/shard_map/ppermute | solution.py:412
  294.7 18.1 %collective-permute-start.49 = (bf16[512,1024]{1,0:T(8,128)(2,1)S(1)}, bf16[512,1024]{1,0:T(8,128)(2,1)}, u32[]{:S(2)}, u32[]{:S(2)}) collective-permute-start(bf16[512,1024]{1,0:T(8,128)(2,1)S(1)} %get-tuple-element.456), channel_id=1, source_target_pairs={{0,1},{1,0},{2,3},{3,2},{4,5},{5,4},{6,7},{7,6},{8,9},{9,8},{10,11... | collective-permute-start | bytes 3145736 | tf_op jit(solution)/shard_map/ppermute | solution.py:412
  297.3 85.4 %reduce-scatter.6.cloned.1.call-start = ((), (), s32[]{:S(2)}) async-start(), calls=%async_computation.5 | async-start | bytes 1310720 | tf_op jit(solution)/shard_map/reduce_scatter | solution.py:913
  297.4 15.1 %collective-permute-start.47 = (bf16[64,4096]{1,0:T(8,128)(2,1)}, bf16[64,4096]{1,0:T(8,128)(2,1)S(1)}, u32[]{:S(2)}, u32[]{:S(2)}) collective-permute-start(bf16[64,4096]{1,0:T(8,128)(2,1)} %get-tuple-element.457), channel_id=1, source_target_pairs={{0,2},{1,3},{2,0},{3,1},{4,6},{5,7},{6,4},{7,5},{8,10},{9,11},{10,... | collective-permute-start | bytes 1572872 | tf_op jit(solution)/shard_map/ppermute | solution.py:412
  298.5 14.2 %collective-permute-start.48 = (bf16[64,4096]{1,0:T(8,128)(2,1)}, bf16[64,4096]{1,0:T(8,128)(2,1)S(1)}, u32[]{:S(2)}, u32[]{:S(2)}) collective-permute-start(bf16[64,4096]{1,0:T(8,128)(2,1)} %get-tuple-element.458), channel_id=1, source_target_pairs={{0,4},{1,5},{2,6},{3,7},{4,0},{5,1},{6,2},{7,3},{8,12},{9,13},{10,... | collective-permute-start | bytes 1572872 | tf_op jit(solution)/shard_map/ppermute | solution.py:412
  313.3 26.5 %collective-permute-start.52 = (bf16[3,512,1024]{2,1,0:T(8,128)(2,1)}, bf16[3,512,1024]{2,1,0:T(8,128)(2,1)}, u32[]{:S(2)}, u32[]{:S(2)}) collective-permute-start(bf16[3,512,1024]{2,1,0:T(8,128)(2,1)} %attn_bwd.3.refs_0_.refs_6_.refs_2_), channel_id=1, source_target_pairs={{0,1},{1,0},{2,3},{3,2},{4,5},{5,4},{6,7},{7,6},{8,9},{9,8},{10,11... | collective-permute-start | bytes 9437192 | tf_op jit(solution)/shard_map/ppermute | solution.py:412
  316.5 91.2 %reduce-scatter.8.cloned.1.call-start = ((), (), s32[]{:S(2)}) async-start(), calls=%async_computation.6 | async-start | bytes 1310720 | tf_op jit(solution)/shard_map/reduce_scatter | solution.py:913
  319.6 37.0 %collective-permute-start.56 = (bf16[128,4096]{1,0:T(8,128)(2,1)}, bf16[128,4096]{1,0:T(8,128)(2,1)}, u32[]{:S(2)}, u32[]{:S(2)}) collective-permute-start(bf16[128,4096]{1,0:T(8,128)(2,1)} %get-tuple-element.497), channel_id=1, source_target_pairs={{0,2},{1,3},{2,0},{3,1},{4,6},{5,7},{6,4},{7,5},{8,10},{9,11},{10,... | collective-permute-start | bytes 3145736 | tf_op jit(solution)/shard_map/ppermute | solution.py:412
  320.6 36.1 %collective-permute-start.57 = (bf16[128,4096]{1,0:T(8,128)(2,1)}, bf16[128,4096]{1,0:T(8,128)(2,1)}, u32[]{:S(2)}, u32[]{:S(2)}) collective-permute-start(bf16[128,4096]{1,0:T(8,128)(2,1)} %get-tuple-element.498), channel_id=1, source_target_pairs={{0,4},{1,5},{2,6},{3,7},{4,0},{5,1},{6,2},{7,3},{8,12},{9,13},{10,... | collective-permute-start | bytes 3145736 | tf_op jit(solution)/shard_map/ppermute | solution.py:412
  349.5 8.6 %collective-permute-start.54 = (bf16[64,2048]{1,0:T(8,128)(2,1)}, bf16[64,2048]{1,0:T(8,128)(2,1)S(1)}, u32[]{:S(2)}, u32[]{:S(2)}) collective-permute-start(bf16[64,2048]{1,0:T(8,128)(2,1)} %get-tuple-element.485), channel_id=1, source_target_pairs={{0,2},{1,3},{2,0},{3,1},{4,6},{5,7},{6,4},{7,5},{8,10},{9,11},{10,... | collective-permute-start | bytes 786440 | tf_op jit(solution)/shard_map/ppermute | solution.py:412
  351.0 8.3 %collective-permute-start.55 = (bf16[64,2048]{1,0:T(8,128)(2,1)}, bf16[64,2048]{1,0:T(8,128)(2,1)S(1)}, u32[]{:S(2)}, u32[]{:S(2)}) collective-permute-start(bf16[64,2048]{1,0:T(8,128)(2,1)} %get-tuple-element.486), channel_id=1, source_target_pairs={{0,4},{1,5},{2,6},{3,7},{4,0},{5,1},{6,2},{7,3},{8,12},{9,13},{10,... | collective-permute-start | bytes 786440 | tf_op jit(solution)/shard_map/ppermute | solution.py:412
  364.8 19.5 %collective-permute-start.60 = (bf16[128,2048]{1,0:T(8,128)(2,1)}, bf16[128,2048]{1,0:T(8,128)(2,1)S(1)}, u32[]{:S(2)}, u32[]{:S(2)}) collective-permute-start(bf16[128,2048]{1,0:T(8,128)(2,1)} %get-tuple-element.510), channel_id=1, source_target_pairs={{0,2},{1,3},{2,0},{3,1},{4,6},{5,7},{6,4},{7,5},{8,10},{9,11},{10,... | collective-permute-start | bytes 1572872 | tf_op jit(solution)/shard_map/ppermute | solution.py:412
  365.3 19.0 %collective-permute-start.61 = (bf16[128,2048]{1,0:T(8,128)(2,1)}, bf16[128,2048]{1,0:T(8,128)(2,1)S(1)}, u32[]{:S(2)}, u32[]{:S(2)}) collective-permute-start(bf16[128,2048]{1,0:T(8,128)(2,1)} %get-tuple-element.511), channel_id=1, source_target_pairs={{0,4},{1,5},{2,6},{3,7},{4,0},{5,1},{6,2},{7,3},{8,12},{9,13},{10,... | collective-permute-start | bytes 1572872 | tf_op jit(solution)/shard_map/ppermute | solution.py:412
  366.2 17.6 %collective-permute-start.58 = (bf16[64,2176]{1,0:T(8,128)(2,1)}, bf16[64,2176]{1,0:T(8,128)(2,1)}, u32[]{:S(2)}, u32[]{:S(2)}) collective-permute-start(bf16[64,2176]{1,0:T(8,128)(2,1)} %get-tuple-element.505), channel_id=1, source_target_pairs={{0,2},{1,3},{2,0},{3,1},{4,6},{5,7},{6,4},{7,5},{8,10},{9,11},{10,... | collective-permute-start | bytes 835592 | tf_op jit(solution)/shard_map/ppermute | solution.py:412
  367.3 17.0 %collective-permute-start.59 = (bf16[64,2176]{1,0:T(8,128)(2,1)}, bf16[64,2176]{1,0:T(8,128)(2,1)}, u32[]{:S(2)}, u32[]{:S(2)}) collective-permute-start(bf16[64,2176]{1,0:T(8,128)(2,1)} %get-tuple-element.506), channel_id=1, source_target_pairs={{0,4},{1,5},{2,6},{3,7},{4,0},{5,1},{6,2},{7,3},{8,12},{9,13},{10,... | collective-permute-start | bytes 835592 | tf_op jit(solution)/shard_map/ppermute | solution.py:412
  385.9 16.6 %collective-permute-start.62 = (bf16[128,2176]{1,0:T(8,128)(2,1)S(1)}, bf16[128,2176]{1,0:T(8,128)(2,1)S(1)}, u32[]{:S(2)}, u32[]{:S(2)}) collective-permute-start(bf16[128,2176]{1,0:T(8,128)(2,1)S(1)} %get-tuple-element.521), channel_id=1, source_target_pairs={{0,2},{1,3},{2,0},{3,1},{4,6},{5,7},{6,4},{7,5},{8,10},{9,11},{10,... | collective-permute-start | bytes 1671176 | tf_op jit(solution)/shard_map/ppermute | solution.py:412
  387.3 15.2 %collective-permute-start.63 = (bf16[128,2176]{1,0:T(8,128)(2,1)S(1)}, bf16[128,2176]{1,0:T(8,128)(2,1)S(1)}, u32[]{:S(2)}, u32[]{:S(2)}) collective-permute-start(bf16[128,2176]{1,0:T(8,128)(2,1)S(1)} %get-tuple-element.522), channel_id=1, source_target_pairs={{0,4},{1,5},{2,6},{3,7},{4,0},{5,1},{6,2},{7,3},{8,12},{9,13},{10,... | collective-permute-start | bytes 1671176 | tf_op jit(solution)/shard_map/ppermute | solution.py:412
  389.5 12.4 %collective-permute-start.65 = (bf16[32,2048]{1,0:T(8,128)(2,1)S(1)}, bf16[32,2048]{1,0:T(8,128)(2,1)S(1)}, u32[]{:S(2)}, u32[]{:S(2)}) collective-permute-start(bf16[32,2048]{1,0:T(8,128)(2,1)S(1)} %get-tuple-element.536), channel_id=1, source_target_pairs={{0,8},{1,9},{2,10},{3,11},{4,12},{5,13},{6,14},{7,15},{8,16},{9,17... | collective-permute-start | bytes 393224 | tf_op jit(solution)/shard_map/ppermute | solution.py:941
  390.7 11.2 %collective-permute-start.66 = (bf16[32,2048]{1,0:T(8,128)(2,1)S(1)}, bf16[32,2048]{1,0:T(8,128)(2,1)S(1)}, u32[]{:S(2)}, u32[]{:S(2)}) collective-permute-start(bf16[32,2048]{1,0:T(8,128)(2,1)S(1)} %get-tuple-element.537), channel_id=1, source_target_pairs={{0,16},{1,17},{2,18},{3,19},{4,20},{5,21},{6,22},{7,23},{8,24},{9,... | collective-permute-start | bytes 393224 | tf_op jit(solution)/shard_map/ppermute | solution.py:941
  393.4 8.4 %collective-permute-start.67 = (bf16[32,2048]{1,0:T(8,128)(2,1)S(1)}, bf16[32,2048]{1,0:T(8,128)(2,1)S(1)}, u32[]{:S(2)}, u32[]{:S(2)}) collective-permute-start(bf16[32,2048]{1,0:T(8,128)(2,1)S(1)} %get-tuple-element.538), channel_id=1, source_target_pairs={{0,24},{1,25},{2,26},{3,27},{4,28},{5,29},{6,30},{7,31},{8,0},{9,1... | collective-permute-start | bytes 393224 | tf_op jit(solution)/shard_map/ppermute | solution.py:941
  403.3 7.8 %collective-permute-start.64 = (bf16[32,2176]{1,0:T(8,128)(2,1)S(1)}, bf16[32,2176]{1,0:T(8,128)(2,1)S(1)}, u32[]{:S(2)}, u32[]{:S(2)}) collective-permute-start(bf16[32,2176]{1,0:T(8,128)(2,1)S(1)} %get-tuple-element.530), channel_id=1, source_target_pairs={{0,8},{1,9},{2,10},{3,11},{4,12},{5,13},{6,14},{7,15},{8,16},{9,17... | collective-permute-start | bytes 417800 | tf_op jit(solution)/shard_map/ppermute | solution.py:941
  404.8 10.3 %collective-permute-start.68 = (bf16[32,2176]{1,0:T(8,128)(2,1)S(1)}, bf16[32,2176]{1,0:T(8,128)(2,1)S(1)}, u32[]{:S(2)}, u32[]{:S(2)}) collective-permute-start(bf16[32,2176]{1,0:T(8,128)(2,1)S(1)} %get-tuple-element.542), channel_id=1, source_target_pairs={{0,16},{1,17},{2,18},{3,19},{4,20},{5,21},{6,22},{7,23},{8,24},{9,... | collective-permute-start | bytes 417800 | tf_op jit(solution)/shard_map/ppermute | solution.py:941
  405.7 9.4 %collective-permute-start.69 = (bf16[32,2176]{1,0:T(8,128)(2,1)S(1)}, bf16[32,2176]{1,0:T(8,128)(2,1)S(1)}, u32[]{:S(2)}, u32[]{:S(2)}) collective-permute-start(bf16[32,2176]{1,0:T(8,128)(2,1)S(1)} %get-tuple-element.543), channel_id=1, source_target_pairs={{0,24},{1,25},{2,26},{3,27},{4,28},{5,29},{6,30},{7,31},{8,0},{9,1... | collective-permute-start | bytes 417800 | tf_op jit(solution)/shard_map/ppermute | solution.py:941
  (93 other events, 746.4 us)
Sparse Core Ops, SparseCore 0:
  35.0 30.1 all-gather.8
  69.7 28.7 all-gather.10
  121.0 86.1 all-gather.6
  297.4 27.6 reduce-scatter.3
  327.4 25.7 reduce-scatter.5
  362.4 26.1 reduce-scatter.7

commit v2 on v1

--- a/solution.py
+++ b/solution.py
@@ -13,9 +13,9 @@
 BF = jnp.bfloat16
 F32 = jnp.float32
 PAIR = 128
-LIMITS = {'feed_back': 50, 'pass_on': 8, 'plane_sum': 8, 'place': 8, 'hidden_order': 8, 'memory_grad': 12, 'turn': 12, 'wgrad': 44, 'wgrad_down': 44, 'wgrad_mid': 44, 'finish': 12, 'line_parts': 12}
-FAR_OUTS = {'wgrad': (0, 1, 2), 'wgrad_down': (0, 1, 2, 3, 4, 5, 6), 'feed_up': (0, 1, 2), 'place_dot': (0,), 'feed_back': (0, 1), 'turn': (0, 1), 'wgrad_mid': (0, 1, 2)}
-FAR_INS = {'pass_on': (0, 1, 2, 3), 'plane_sum': (0, 1, 2), 'wgrad_mid': (0, 1, 2, 3, 4, 5, 6, 7, 8, 9, 10, 11), 'attn_bwd': (0, 1, 2, 3, 4)}
+LIMITS = {'feed_back': 50, 'pass_on': 8, 'plane_sum': 8, 'place': 8, 'hidden_order': 8, 'memory_grad': 12, 'turn': 12, 'wgrad': 44, 'wgrad_down': 44, 'wgrad_mid': 44, 'finish': 12, 'line_parts': 12, 'wgrad_a': 44}
+FAR_OUTS = {'wgrad': (0, 1, 2), 'wgrad_down': (0, 1, 2, 3, 4, 5, 6), 'feed_up': (0, 1, 2), 'place_dot': (0,), 'feed_back': (0, 1), 'wgrad_mid': (0, 1, 2), 'wgrad_a': (0, 1, 2)}
+FAR_INS = {'pass_on': (0, 1, 2, 3), 'plane_sum': (0, 1, 2), 'wgrad_mid': (0, 1, 2, 3, 4, 5, 6, 7, 8, 9, 10, 11), 'attn_bwd': (0, 1, 2, 3, 4), 'wgrad_a': (0, 1, 2, 3, 4, 5, 6, 7)}
 
 
 def dot(a, b):
@@ -1169,13 +1169,14 @@
     wcq, qc = place_dot(second, 3 * d, d, bits, h2, BF)
     wckv, kvc = place_dot(second, 0, 2 * d, bits, memory_pad, BF)
     h1_t, o_t = ((mine, swap(theirs, CORE)) for mine, theirs in (h1_turn, o_turn))
-    near3, second, qc, kvc, h2, x1, h1_t, o_t = fence(
-        near3, second, qc, kvc, h2, x1, h1_t, o_t
+    h2_t = turned(h2)
+    near3, second, qc, kvc, x1, h1_t, o_t, h2_t = fence(
+        near3, second, qc, kvc, x1, h1_t, o_t, h2_t
     )
 
     far3, cores3 = gather_far(near3), swap_cores(near3)
     o2, lse2 = attn_fwd((qc, 0), kvc, 0, blocks, slots_used, False)
-    near3, cores3, o2, h2, cotangent = fence(near3, cores3, o2, h2, cotangent)
+    near3, cores3, o2, cotangent = fence(near3, cores3, o2, cotangent)
 
     wco, y2 = place_dot(second, 4 * d, d, bits, o2, F32)
     x2 = x1 + y2
@@ -1191,8 +1192,8 @@
     wup, g, slope, g_send = feed_up(bits, h3, third, ff)
     wup, g, slope, g_send, h3, o2 = fence(wup, g, slope, g_send, h3, o2)
 
-    h2_t, h3_t, o2_t = turned(h2), turned(h3), turned(o2)
-    g_other, h2_t, h3_t, o2_t, g = fence(swap(g_send, CORE), h2_t, h3_t, o2_t, g)
+    h3_t, o2_t = turned(h3), turned(o2)
+    g_other, h3_t, o2_t, g = fence(swap(g_send, CORE), h3_t, o2_t, g)
 
     grad_down = wgrad_down(bits, g, g_other, dy3, dy3_other, cuts)
     grad_down, dy3, slope, wdown = fence(grad_down, dy3, slope, wdown)
@@ -1239,12 +1240,13 @@
     grad_hidden, sums1 = through_norm(dqkv, wqkv, hidden, gains[0:1], dx1)
     sums = jnp.stack([sums1, sums2, sums3], axis=1).reshape(6, d)
     sums = jnp.pad(sums, ((0, 122), (0, 0))).astype(BF)
-    dqkv_other, grad_hidden, sums_t = fence(swap(dqkv, CORE), grad_hidden, turned(sums))
+    dqkv_other, grad_hidden, sums = fence(swap(dqkv, CORE), grad_hidden, sums)
 
     grad_a = wgrad(
-        [o_t + (dy1[None], dy1_other[None]), h1_t + (dqkv, dqkv_other, 0, 1)]
-    )
-    grad_a, dqkv, dqkv_other, sums_t = fence(grad_a, dqkv, dqkv_other, sums_t)
+        [o_t + (dy1[None], dy1_other[None]), h1_t + (dqkv, dqkv_other, 0, 1)],
+        name="wgrad_a",
+    )
+    grad_a, dqkv, dqkv_other, sums_t = fence(grad_a, dqkv, dqkv_other, turned(sums))
 
     grad_b = wgrad([h1_t + (dqkv, dqkv_other, 1, 3)], extra=sums_t)
     far_a, grad_b, got3, dkvc, own_down, g = fence(

time: 431 us -> 425 us (0.986)
  waiting for transfers between devices: 55.6 us -> 48.4 us
  local copies, waits for them, and re-layouts: 39.3 us -> 46.2 us
  Pallas kernels: 224 us -> 218 us
    ppermute x64, waiting for transfers between devices: 51.2 us -> 44.4 us  [swap(): return lax.ppermute(a, ALL, [(i, i ^ bit) for i in range(32)])]
    pallas_call x42, Pallas kernels: 224 us -> 218 us  [run(): pl.pallas_call(body, grid_spec=pltpu.PrefetchScalarGridSpec(num_scalar_pr...]
    unnamed x164 -> x174, local copies, waits for them, and re-layouts: 30.1 us -> 35.4 us
  transfers between devices with their start and end apart: 76 -> 76, of which waited for: 26 -> 25; matrix products, arithmetic and copies ran while one was open for 5% -> 6% of each run, Pallas kernels for 53% -> 52%
where the time goes in v2:
time: 425 us; the launch traced here: 417 us
  Pallas kernels  218 us (51%)
  starting transfers between devices  51.4 us (12%)
  waiting for transfers between devices  48.4 us (11%)
  local copies, waits for them, and re-layouts  46.2 us (11%)
  blocking collectives  21.7 us (5%)
  between operations  16.8 us (4%)
  other arithmetic  12.6 us (3%)
    pallas_call x42, Pallas kernels, run(): pl.pallas_call(body, grid_spec=pltpu.PrefetchScalarGridSpec(num_scalar_pr...  218 us
    ppermute x64, waiting for transfers between devices, swap(): return lax.ppermute(a, ALL, [(i, i ^ bit) for i in range(32)])  44.4 us
    ppermute x64, starting transfers between devices, swap(): return lax.ppermute(a, ALL, [(i, i ^ bit) for i in range(32)])  42.1 us
    unnamed x174, local copies, waits for them, and re-layouts  35.4 us
    all_gather x1, blocking collectives, gather_line(): return lax.all_gather(w, 'gx', axis=0)  21.7 us
    ppermute x6, starting transfers between devices, line_parts(): lax.ppermute(part, ALL, [(i, (i + 8 * step) % 32) for i in range(32)])  8.86 us
  transfers between devices with their start and end apart: 76, of which 25 were waited for; matrix products, arithmetic and copies ran while one was open for 6% of the time, Pallas kernels for 52%

profile of v2, /device:TPU:0, one launch (start us, length us, event | category | flops | bytes accessed | tf_op | source)
XLA Modules:
  0.0 417.4 jit_solution(3163334868407869966)
XLA Ops:
  9.2 21.7 %all-gather = bf16[128,3200]{1,0:T(8,128)(2,1)S(1)} all-gather(bf16[32,3200]{1,0:T(8,128)(2,1)S(1)} %fusion.2), channel_id=2, replica_groups=mesh['gx'=4,'gy'=8] {'gx'}, dimensions={0}, use_global_device_ids=true | all-gather | bytes 1024000 | tf_op jit(solution)/shard_map/all_gather | solution.py:420
  35.6 3.3 turn.7
  40.4 1.6 subtract_multiply_fusion
  42.2 7.1 %collective-permute-done.1.refs_3_ = bf16[4,32,3200]{2,1,0:T(8,128)(2,1)} collective-permute-done((bf16[4,32,3200]{2,1,0:T(8,128)(2,1)S(1)}, bf16[4,32,3200]{2,1,0:T(8,128)(2,1)}, u32[]{:S(2)}, u32[]{:S(2)}) %collective-permute-start.1) | collective-permute-done | bytes 819232 | tf_op jit(solution)/shard_map/ppermute | solution.py:412
  52.2 1.8 slice.85
  57.6 8.6 %collective-permute-done.3.refs_4_ = bf16[2,32,3200]{2,1,0:T(8,128)(2,1)} collective-permute-done((bf16[2,32,3200]{2,1,0:T(8,128)(2,1)}, bf16[2,32,3200]{2,1,0:T(8,128)(2,1)}, u32[]{:S(2)}, u32[]{:S(2)}) %collective-permute-start.3) | collective-permute-done | bytes 409632 | tf_op jit(solution)/shard_map/ppermute | solution.py:412
  74.3 1.9 add_convert_fusion.2.refs_11_.refs_1_
  76.3 8.8 %place_dot.5 = (bf16[4,8,32,3072]{3,2,1,0:T(8,128)(2,1)}, bf16[512,3072]{1,0:T(8,128)(2,1)S(1)}) custom-call(s32[4]{0:T(128)S(1)} %pad_add_fusion.refs_0_, bf16[4,32,3200]{2,1,0:T(8,128)(2,1)S(1)} %bitcast.46, bf16[4,32,3200]{2,1,0:T(8,128)(2,1)} %collective-permute-done.refs_2_, bf16[4,32,3200]{2,1,0:T(8,128)(2,1)} %collective-permute-done.1.refs_3_, ...), custom_call_target="tpu_custom_call" | custom-call | flops 3221225472 | bytes 12582912 | tf_op jit(solution)/shard_map/place_dot/pallas_call | solution.py:41
  85.1 7.8 %attn_fwd.2 = (bf16[512,1024]{1,0:T(8,128)(2,1)S(1)}, f32[8,2,512]{2,1,0:T(2,128)S(1)}) custom-call(s32[1]{0:T(128)} %copy.34.refs_0_, bf16[512,3072]{1,0:T(8,128)(2,1)S(1)} %get-tuple-element.299.refs_1_.refs_2_.refs_3_, bf16[512,3072]{1,0:T(8,128)(2,1)S(1)} %get-tuple-element.299.refs_1_.refs_2_.refs_3_, ...), custom_call_target="tpu_custom_call" | custom-call | flops 4294967296 | bytes 4194304 | tf_op jit(solution)/shard_map/attn_fwd/pallas_call | solution.py:41
  93.9 5.5 %collective-permute-done.9.refs_3_ = bf16[4,32,5120]{2,1,0:T(8,128)(2,1)S(1)} collective-permute-done((bf16[4,32,5120]{2,1,0:T(8,128)(2,1)}, bf16[4,32,5120]{2,1,0:T(8,128)(2,1)S(1)}, u32[]{:S(2)}, u32[]{:S(2)}) %collective-permute-start.9) | collective-permute-done | bytes 1310752 | tf_op jit(solution)/shard_map/ppermute | solution.py:412
  100.3 2.0 slice.93
  106.0 1.6 copy-done.13
  108.8 2.0 turn.8
  112.4 2.0 turn.9
  116.0 4.7 %collective-permute-done.12.refs_4_ = bf16[2,32,5120]{2,1,0:T(8,128)(2,1)} collective-permute-done((bf16[2,32,5120]{2,1,0:T(8,128)(2,1)}, bf16[2,32,5120]{2,1,0:T(8,128)(2,1)}, u32[]{:S(2)}, u32[]{:S(2)}) %collective-permute-start.12) | collective-permute-done | bytes 655392 | tf_op jit(solution)/shard_map/ppermute | solution.py:412
  121.8 1.6 collective-permute-start.18
  126.6 4.0 place_dot.6
  131.7 1.6 copy-done.14
  133.3 2.0 turn.10
  136.2 3.7 place_dot.7
  139.8 6.4 %place_dot.8 = (bf16[4,8,32,2048]{3,2,1,0:T(8,128)(2,1)}, bf16[592,2048]{1,0:T(8,128)(2,1)S(1)}) custom-call(s32[4]{0:T(128)S(1)} %pad_add_fusion.refs_0_, bf16[4,32,5120]{2,1,0:T(8,128)(2,1)} %bitcast.2.refs_1_, bf16[4,32,5120]{2,1,0:T(8,128)(2,1)} %collective-permute-done.8.refs_2_, bf16[4,32,5120]{2,1,0:T(8,128)(2,1)S(1)} %collective-permute-done.9.refs_3_, ...), custom_call_target="tpu_custom_call" | custom-call | flops 2483027968 | bytes 8388608 | tf_op jit(solution)/shard_map/place_dot/pallas_call | solution.py:41
  146.3 2.8 collective-permute-done.18.refs_3_
  156.0 10.6 %attn_fwd.3 = (bf16[512,1024]{1,0:T(8,128)(2,1)S(1)}, f32[8,2,512]{2,1,0:T(2,128)S(1)}) custom-call(s32[1]{0:T(128)S(6)} %select_n.102.refs_0_, bf16[512,1024]{1,0:T(8,128)(2,1)S(1)} %get-tuple-element.337.refs_1_, bf16[592,2048]{1,0:T(8,128)(2,1)S(1)} %get-tuple-element.338.refs_2_.refs_3_, bf16[592,2048]{1,0:T(8,128)(2,1)S(1)} %get-tuple-element.338.refs_2_.refs_3_), custom_call_target="tpu_custom_call" | custom-call | flops 4966055936 | bytes 4194304 | tf_op jit(solution)/shard_map/attn_fwd/pallas_call | solution.py:41
  166.6 1.6 fusion.32
  168.2 4.1 place_dot.9
  174.5 2.2 collective-permute-done.30.refs_9_
  178.2 12.1 %feed_up.1 = (bf16[4,8,32,4096]{3,2,1,0:T(8,128)(2,1)}, bf16[512,4096]{1,0:T(8,128)(2,1)}, bf16[512,4096]{1,0:T(8,128)(2,1)}, bf16[512,2048]{1,0:T(8,128)(2,1)S(1)}) custom-call(s32[4]{0:T(128)S(1)} %pad_add_fusion.refs_0_, bf16[4,32,4096]{2,1,0:T(8,128)(2,1)S(1)} %bitcast.59, bf16[4,32,4096]{2,1,0:T(8,128)(2,1)S(1)} %collective-permute-done.17.refs_2_, ...), custom_call_target="tpu_custom_call" | custom-call | flops 4294967296 | bytes 25165824 | tf_op jit(solution)/shard_map/feed_up/pallas_call | solution.py:41
  190.7 2.0 turn.11
  193.6 2.0 turn.12
  199.2 8.3 %wgrad_down.1 = (bf16[128,4096]{1,0:T(8,128)(2,1)}, bf16[64,4096]{1,0:T(8,128)(2,1)}, bf16[64,4096]{1,0:T(8,128)(2,1)}, bf16[64,4096]{1,0:T(8,128)(2,1)}, bf16[6...) custom-call(s32[4]{0:T(128)S(1)} %pad_add_fusion.refs_0_, bf16[512,4096]{1,0:T(8,128)(2,1)S(1)} %copy-done, ...), custom_call_target="tpu_custom_call" | custom-call | flops 4294967296 | bytes 8388608 | tf_op jit(solution)/shard_map/wgrad_down/pallas_call | solution.py:41
  209.0 2.0 collective-permute-start.37
  212.7 20.1 %feed_back.1 = (bf16[512,4096]{1,0:T(8,128)(2,1)}, f32[512,1024]{1,0:T(8,128)}, bf16[512,1024]{1,0:T(8,128)(2,1)S(1)}, f32[2,1024]{1,0:T(2,128)S(1)}) custom-call(bf16[512,1024]{1,0:T(8,128)(2,1)S(1)} %copy-done.18, bf16[1024,4096]{1,0:T(8,128)(2,1)} %all-gather.7.cloned.1.call-done.refs_1_, bf16[512,4096]{1,0:T(8,128)(2,1)} %get-tuple-element.399.refs_2_, ...), custom_call_target="tpu_custom_call" | custom-call | flops 8589934592 | bytes 33554432 | tf_op jit(solution)/shard_map/feed_back/pallas_call | solution.py:41
  233.9 2.2 pass_on.5
  238.1 2.3 convolution_convert_fusion.refs_5_
  240.7 6.8 %wgrad.2 = (bf16[384,4096]{1,0:T(8,128)(2,1)}, bf16[64,4096]{1,0:T(8,128)(2,1)}, bf16[64,4096]{1,0:T(8,128)(2,1)}) custom-call(bf16[512,512]{1,0:T(8,128)(2,1)S(1)} %copy-done.58, bf16[512,512]{1,0:T(8,128)(2,1)S(1)} %collective-permute-done.33.refs_1_, bf16[1,512,4096]{2,1,0:T(8,128)(2,1)S(1)} %bitcast.54, bf16[1,512,4096]{2,1,0:T(8,128)(2,1)S(1)} %bitcast.55), custom_call_target="tpu_custom_call" | custom-call | flops 4294967296 | bytes 12582912 | tf_op jit(solution)/shard_map/wgrad/pallas_call | solution.py:41
  250.5 16.8 %attn_bwd.2 = (bf16[1,512,1024]{2,1,0:T(8,128)(2,1)S(1)}, bf16[2,592,1024]{2,1,0:T(8,128)(2,1)S(1)}) custom-call(s32[1]{0:T(128)S(6)} %select_n.102.refs_0_, bf16[512,1024]{1,0:T(8,128)(2,1)} %copy-done.50, bf16[592,2048]{1,0:T(8,128)(2,1)} %copy-done.48, bf16[592,2048]{1,0:T(8,128)(2,1)} %copy-done.48, bf16[512,1024]{1,0:T(8,128)(2,1)} %copy-done.30, ...), custom_call_target="tpu_custom_call" | custom-call | flops 12415139840 | bytes 8388608 | tf_op jit(solution)/shard_map/attn_bwd/pallas_call | solution.py:41
  268.4 5.0 %pass_on.6 = (bf16[128,4096]{1,0:T(8,128)(2,1)}, bf16[128,4096]{1,0:T(8,128)(2,1)}) custom-call(bf16[384,4096]{1,0:T(8,128)(2,1)} %get-tuple-element.456.refs_0_.refs_1_, bf16[384,4096]{1,0:T(8,128)(2,1)} %get-tuple-element.456.refs_0_.refs_1_, bf16[64,4096]{1,0:T(8,128)(2,1)} %copy-done.65, bf16[64,4096]{1,0:T(8,128)(2,1)} %copy-done.66), custom_call_target="tpu_custom_call" | custom-call | flops 524288 | bytes 5242880 | tf_op jit(solution)/shard_map/pass_on/pallas_call | solution.py:41
  274.5 4.8 %through_norm.2 = (f32[512,1024]{1,0:T(8,128)S(1)}, bf16[512,1024]{1,0:T(8,128)(2,1)S(1)}, bf16[512,1024]{1,0:T(8,128)(2,1)S(1)}, f32[2,1024]{1,0:T(2,128)S(1)}) custom-call(bf16[1,512,1024]{2,1,0:T(8,128)(2,1)S(1)} %get-tuple-element.440.refs_0_.refs_6_, bf16[1024,1024]{1,0:T(8,128)(2,1)S(1)} %bitcast.48, f32[512,1024]{1,0:T(8,128)S(1)} %copy-done.4, ...), custom_call_target="tpu_custom_call" | custom-call | flops 1073741824 | bytes 10485760 | tf_op jit(solution)/shard_map/through_norm/pallas_call | solution.py:41
  282.4 11.5 %wgrad_mid.1 = (bf16[384,4096]{1,0:T(8,128)(2,1)}, bf16[64,4096]{1,0:T(8,128)(2,1)}, bf16[64,4096]{1,0:T(8,128)(2,1)}) custom-call(bf16[512,512]{1,0:T(8,128)(2,1)} %copy-done.56, bf16[512,512]{1,0:T(8,128)(2,1)} %copy-done.85, bf16[1,512,1024]{2,1,0:T(8,128)(2,1)} %bitcast.60, bf16[1,512,1024]{2,1,0:T(8,128)(2,1)} %bitcast.66, bf16[512,512]{1,0:T(8,128)(2,1)} %copy-done.55, ...), custom_call_target="tpu_custom_call" | custom-call | flops 4294967296 | bytes 12582912 | tf_op jit(solution)/shard_map/wgrad_mid/pallas_call | solution.py:41
  294.0 2.6 plane_sum.3
  296.6 1.6 collective-permute-start.47
  299.8 12.5 %attn_bwd.3.refs_0_.refs_6_.refs_2_ = bf16[3,512,1024]{2,1,0:T(8,128)(2,1)} custom-call(s32[1]{0:T(128)} %copy.34.refs_0_, bf16[512,3072]{1,0:T(8,128)(2,1)} %copy-done.60, bf16[512,3072]{1,0:T(8,128)(2,1)} %copy-done.60, bf16[512,3072]{1,0:T(8,128)(2,1)} %copy-done.60, bf16[512,1024]{1,0:T(8,128)(2,1)} %copy-done.27, bf16[512,1024]{1,0:T(8,128)(2,1)} %copy-done.52, ...), custom_call_target="tpu_custom_call" | custom-call | flops 10737418240 | bytes 8388608 | tf_op jit(solution)/shard_map/attn_bwd/pallas_call | solution.py:41
  313.3 2.9 plane_sum.4
  316.3 2.9 pass_on.7
  321.1 2.8 copy-done.16
  323.9 9.8 %through_norm.3 = (f32[512,1024]{1,0:T(8,128)}, f32[2,1024]{1,0:T(2,128)S(1)}) custom-call(bf16[3,512,1024]{2,1,0:T(8,128)(2,1)} %attn_bwd.3.refs_0_.refs_6_.refs_2_, bf16[1024,3072]{1,0:T(8,128)(2,1)S(1)} %bitcast.41, f32[512,1024]{1,0:T(8,128)S(1)} %copy-done.2, f32[1,1024]{1,0:T(1,128)S(1)} %get-tuple-element.568.refs_3_, f32[512,1024]{1,0:T(8,128)S(1)} %copy-done.23), custom_call_target="tpu_custom_call" | custom-call | flops 3221225472 | bytes 14680064 | tf_op jit(solution)/shard_map/through_norm/pallas_call | solution.py:41
  333.9 1.6 copy-done.15
  336.8 6.5 %wgrad_a.1 = (bf16[384,2048]{1,0:T(8,128)(2,1)}, bf16[64,2048]{1,0:T(8,128)(2,1)}, bf16[64,2048]{1,0:T(8,128)(2,1)}) custom-call(bf16[512,512]{1,0:T(8,128)(2,1)} %copy-done.39, bf16[512,512]{1,0:T(8,128)(2,1)} %copy-done.67, bf16[1,512,1024]{2,1,0:T(8,128)(2,1)} %bitcast.49, bf16[1,512,1024]{2,1,0:T(8,128)(2,1)} %bitcast.26.refs_3_, ...), custom_call_target="tpu_custom_call" | custom-call | flops 2147483648 | bytes 6291456 | tf_op jit(solution)/shard_map/wgrad_a/pallas_call | solution.py:41
  343.3 1.6 collective-permute-start.54
  345.5 5.1 %wgrad.3 = (bf16[384,2176]{1,0:T(8,128)(2,1)}, bf16[64,2176]{1,0:T(8,128)(2,1)}, bf16[64,2176]{1,0:T(8,128)(2,1)}) custom-call(bf16[512,512]{1,0:T(8,128)(2,1)S(1)} %copy-done.38, bf16[512,512]{1,0:T(8,128)(2,1)S(1)} %copy-done.41, bf16[3,512,1024]{2,1,0:T(8,128)(2,1)} %attn_bwd.3.refs_0_.refs_6_.refs_2_, ...), custom_call_target="tpu_custom_call" | custom-call | flops 2281701376 | bytes 6684672 | tf_op jit(solution)/shard_map/wgrad/pallas_call | solution.py:41
  350.7 1.6 collective-permute-done.54.refs_2_
  353.6 2.9 plane_sum.5
  356.5 2.5 pass_on.8
  363.1 2.2 copy-done.1
  365.3 3.5 copy-done.11
  368.8 8.2 %feed_down.1 = f32[512,1024]{1,0:T(8,128)} custom-call(bf16[512,4096]{1,0:T(8,128)(2,1)S(1)} %copy-done.1, bf16[1024,4096]{1,0:T(8,128)(2,1)S(1)} %copy-done.11, f32[512,1024]{1,0:T(8,128)S(1)} %copy-done.6), custom_call_target="tpu_custom_call" | custom-call | flops 4294967296 | bytes 13631488 | tf_op jit(solution)/shard_map/feed_down/pallas_call | solution.py:41
  379.1 1.7 pass_on.9
  384.3 3.6 collective-permute-start.66
  388.2 1.7 hidden_order.3
  389.9 6.1 %memory_grad.1 = f32[588,1024]{1,0:T(8,128)} custom-call(bf16[2,592,1024]{2,1,0:T(8,128)(2,1)S(1)} %copy-done.47, bf16[1024,2048]{1,0:T(8,128)(2,1)S(1)} %bitcast.53), custom_call_target="tpu_custom_call" | custom-call | flops 2483027968 | bytes 10797056 | tf_op jit(solution)/shard_map/memory_grad/pallas_call | solution.py:41
  397.5 2.0 collective-permute-start.64
  402.4 1.6 slice.119
  404.1 1.6 fusion.36
  405.9 3.6 collective-permute-done.68.refs_2_
  (361 shorter events, 91.4 us)
Async XLA Ops:
  7.2 60.0 %all-gather.9.cloned.1.call-start = ((), (), s32[]{:S(2)}) async-start(), calls=%async_computation.7 | async-start | bytes 1638400 | tf_op jit(solution)/shard_map/all_gather | solution.py:420
  31.9 17.5 %collective-permute-start.1 = (bf16[4,32,3200]{2,1,0:T(8,128)(2,1)S(1)}, bf16[4,32,3200]{2,1,0:T(8,128)(2,1)}, u32[]{:S(2)}, u32[]{:S(2)}) collective-permute-start(bf16[4,32,3200]{2,1,0:T(8,128)(2,1)S(1)} %bitcast.42), channel_id=1, source_target_pairs={{0,4},{1,5},{2,6},{3,7},{4,0},{5,1},{6,2},{7,3},{8,12},{9,13},{10,... | collective-permute-start | bytes 2457608 | tf_op jit(solution)/shard_map/ppermute | solution.py:412
  33.4 17.2 %collective-permute-start = (bf16[4,32,3200]{2,1,0:T(8,128)(2,1)S(1)}, bf16[4,32,3200]{2,1,0:T(8,128)(2,1)}, u32[]{:S(2)}, u32[]{:S(2)}) collective-permute-start(bf16[4,32,3200]{2,1,0:T(8,128)(2,1)S(1)} %bitcast.43), channel_id=1, source_target_pairs={{0,2},{1,3},{2,0},{3,1},{4,6},{5,7},{6,4},{7,5},{8,10},{9,11},{10,... | collective-permute-start | bytes 2457608 | tf_op jit(solution)/shard_map/ppermute | solution.py:412
  34.9 81.0 %all-gather.11.cloned.1.call-start = ((), (), s32[]{:S(2)}) async-start(), calls=%async_computation.8 | async-start | bytes 1310720 | tf_op jit(solution)/shard_map/all_gather | solution.py:420
  50.6 16.5 %collective-permute-start.5 = (bf16[4,32,3200]{2,1,0:T(8,128)(2,1)S(1)}, bf16[4,32,3200]{2,1,0:T(8,128)(2,1)}, u32[]{:S(2)}, u32[]{:S(2)}) collective-permute-start(bf16[4,32,3200]{2,1,0:T(8,128)(2,1)S(1)} %bitcast.44), channel_id=1, source_target_pairs={{0,1},{1,0},{2,3},{3,2},{4,5},{5,4},{6,7},{7,6},{8,9},{9,8},{10,11... | collective-permute-start | bytes 2457608 | tf_op jit(solution)/shard_map/ppermute | solution.py:412
  50.6 16.5 %collective-permute-start.6 = (bf16[4,32,3200]{2,1,0:T(8,128)(2,1)}, bf16[4,32,3200]{2,1,0:T(8,128)(2,1)}, u32[]{:S(2)}, u32[]{:S(2)}) collective-permute-start(bf16[4,32,3200]{2,1,0:T(8,128)(2,1)} %collective-permute-done.refs_2_), channel_id=1, source_target_pairs={{0,1},{1,0},{2,3},{3,2},{4,5},{5,4},{6,7},{7,6},{8,9},{9,8},{10,11... | collective-permute-start | bytes 2457608 | tf_op jit(solution)/shard_map/ppermute | solution.py:412
  51.1 16.0 %collective-permute-start.7 = (bf16[4,32,3200]{2,1,0:T(8,128)(2,1)}, bf16[4,32,3200]{2,1,0:T(8,128)(2,1)}, u32[]{:S(2)}, u32[]{:S(2)}) collective-permute-start(bf16[4,32,3200]{2,1,0:T(8,128)(2,1)} %collective-permute-done.1.refs_3_), channel_id=1, source_target_pairs={{0,1},{1,0},{2,3},{3,2},{4,5},{5,4},{6,7},{7,6},{8,9},{9,8},{10,11... | collective-permute-start | bytes 2457608 | tf_op jit(solution)/shard_map/ppermute | solution.py:412
  53.9 12.2 %collective-permute-start.3 = (bf16[2,32,3200]{2,1,0:T(8,128)(2,1)}, bf16[2,32,3200]{2,1,0:T(8,128)(2,1)}, u32[]{:S(2)}, u32[]{:S(2)}) collective-permute-start(bf16[2,32,3200]{2,1,0:T(8,128)(2,1)} %slice.85), channel_id=1, source_target_pairs={{0,2},{1,3},{2,0},{3,1},{4,6},{5,7},{6,4},{7,5},{8,10},{9,11},{10,... | collective-permute-start | bytes 1228808 | tf_op jit(solution)/shard_map/ppermute | solution.py:412
  55.4 11.7 %collective-permute-start.4 = (bf16[2,32,3200]{2,1,0:T(8,128)(2,1)S(1)}, bf16[2,32,3200]{2,1,0:T(8,128)(2,1)}, u32[]{:S(2)}, u32[]{:S(2)}) collective-permute-start(bf16[2,32,3200]{2,1,0:T(8,128)(2,1)S(1)} %slice.86), channel_id=1, source_target_pairs={{0,4},{1,5},{2,6},{3,7},{4,0},{5,1},{6,2},{7,3},{8,12},{9,13},{10,... | collective-permute-start | bytes 1228808 | tf_op jit(solution)/shard_map/ppermute | solution.py:412
  68.5 31.0 %collective-permute-start.9 = (bf16[4,32,5120]{2,1,0:T(8,128)(2,1)}, bf16[4,32,5120]{2,1,0:T(8,128)(2,1)S(1)}, u32[]{:S(2)}, u32[]{:S(2)}) collective-permute-start(bf16[4,32,5120]{2,1,0:T(8,128)(2,1)} %bitcast.2.refs_1_), channel_id=1, source_target_pairs={{0,4},{1,5},{2,6},{3,7},{4,0},{5,1},{6,2},{7,3},{8,12},{9,13},{10,... | collective-permute-start | bytes 3932168 | tf_op jit(solution)/shard_map/ppermute | solution.py:412
  69.0 30.8 %collective-permute-start.8 = (bf16[4,32,5120]{2,1,0:T(8,128)(2,1)}, bf16[4,32,5120]{2,1,0:T(8,128)(2,1)}, u32[]{:S(2)}, u32[]{:S(2)}) collective-permute-start(bf16[4,32,5120]{2,1,0:T(8,128)(2,1)} %bitcast.2.refs_1_), channel_id=1, source_target_pairs={{0,2},{1,3},{2,0},{3,1},{4,6},{5,7},{6,4},{7,5},{8,10},{9,11},{10,... | collective-permute-start | bytes 3932168 | tf_op jit(solution)/shard_map/ppermute | solution.py:412
  69.6 137.9 %all-gather.7.cloned.1.call-start = ((), (), s32[]{:S(2)}) async-start(), calls=%async_computation.3 | async-start | bytes 8650752 | tf_op jit(solution)/shard_map/all_gather | solution.py:1162
  99.8 21.1 %collective-permute-start.14 = (bf16[4,32,5120]{2,1,0:T(8,128)(2,1)}, bf16[4,32,5120]{2,1,0:T(8,128)(2,1)}, u32[]{:S(2)}, u32[]{:S(2)}) collective-permute-start(bf16[4,32,5120]{2,1,0:T(8,128)(2,1)} %bitcast.2.refs_1_), channel_id=1, source_target_pairs={{0,1},{1,0},{2,3},{3,2},{4,5},{5,4},{6,7},{7,6},{8,9},{9,8},{10,11... | collective-permute-start | bytes 3932168 | tf_op jit(solution)/shard_map/ppermute | solution.py:412
  99.8 21.1 %collective-permute-start.15 = (bf16[4,32,5120]{2,1,0:T(8,128)(2,1)}, bf16[4,32,5120]{2,1,0:T(8,128)(2,1)}, u32[]{:S(2)}, u32[]{:S(2)}) collective-permute-start(bf16[4,32,5120]{2,1,0:T(8,128)(2,1)} %collective-permute-done.8.refs_2_), channel_id=1, source_target_pairs={{0,1},{1,0},{2,3},{3,2},{4,5},{5,4},{6,7},{7,6},{8,9},{9,8},{10,11... | collective-permute-start | bytes 3932168 | tf_op jit(solution)/shard_map/ppermute | solution.py:412
  100.3 20.6 %collective-permute-start.16 = (bf16[4,32,5120]{2,1,0:T(8,128)(2,1)S(1)}, bf16[4,32,5120]{2,1,0:T(8,128)(2,1)}, u32[]{:S(2)}, u32[]{:S(2)}) collective-permute-start(bf16[4,32,5120]{2,1,0:T(8,128)(2,1)S(1)} %collective-permute-done.9.refs_3_), channel_id=1, source_target_pairs={{0,1},{1,0},{2,3},{3,2},{4,5},{5,4},{6,7},{7,6},{8,9},{9,8},{10,11... | collective-permute-start | bytes 3932168 | tf_op jit(solution)/shard_map/ppermute | solution.py:412
  103.2 17.5 %collective-permute-start.12 = (bf16[2,32,5120]{2,1,0:T(8,128)(2,1)}, bf16[2,32,5120]{2,1,0:T(8,128)(2,1)}, u32[]{:S(2)}, u32[]{:S(2)}) collective-permute-start(bf16[2,32,5120]{2,1,0:T(8,128)(2,1)} %slice.92), channel_id=1, source_target_pairs={{0,2},{1,3},{2,0},{3,1},{4,6},{5,7},{6,4},{7,5},{8,10},{9,11},{10,... | collective-permute-start | bytes 1966088 | tf_op jit(solution)/shard_map/ppermute | solution.py:412
  103.7 17.2 %collective-permute-start.13 = (bf16[2,32,5120]{2,1,0:T(8,128)(2,1)}, bf16[2,32,5120]{2,1,0:T(8,128)(2,1)}, u32[]{:S(2)}, u32[]{:S(2)}) collective-permute-start(bf16[2,32,5120]{2,1,0:T(8,128)(2,1)} %slice.93), channel_id=1, source_target_pairs={{0,4},{1,5},{2,6},{3,7},{4,0},{5,1},{6,2},{7,3},{8,12},{9,13},{10,... | collective-permute-start | bytes 1966088 | tf_op jit(solution)/shard_map/ppermute | solution.py:412
  120.9 229.7 %reduce-scatter.4.cloned.1.call-start = ((), (), s32[]{:S(2)}) async-start(), calls=%async_computation.4 | async-start | bytes 1310720 | tf_op jit(solution)/shard_map/reduce_scatter | solution.py:895
  121.8 27.3 %collective-permute-start.18 = (bf16[4,32,4096]{2,1,0:T(8,128)(2,1)}, bf16[4,32,4096]{2,1,0:T(8,128)(2,1)S(1)}, u32[]{:S(2)}, u32[]{:S(2)}) collective-permute-start(bf16[4,32,4096]{2,1,0:T(8,128)(2,1)} %bitcast.56), channel_id=1, source_target_pairs={{0,4},{1,5},{2,6},{3,7},{4,0},{5,1},{6,2},{7,3},{8,12},{9,13},{10,... | collective-permute-start | bytes 3145736 | tf_op jit(solution)/shard_map/ppermute | solution.py:412
  123.3 27.0 %collective-permute-start.17 = (bf16[4,32,4096]{2,1,0:T(8,128)(2,1)}, bf16[4,32,4096]{2,1,0:T(8,128)(2,1)S(1)}, u32[]{:S(2)}, u32[]{:S(2)}) collective-permute-start(bf16[4,32,4096]{2,1,0:T(8,128)(2,1)} %bitcast.57), channel_id=1, source_target_pairs={{0,2},{1,3},{2,0},{3,1},{4,6},{5,7},{6,4},{7,5},{8,10},{9,11},{10,... | collective-permute-start | bytes 3145736 | tf_op jit(solution)/shard_map/ppermute | solution.py:412
  124.8 21.4 %collective-permute-start.21 = (bf16[512,512]{1,0:T(8,128)(2,1)}, bf16[512,512]{1,0:T(8,128)(2,1)S(1)}, u32[]{:S(2)}, u32[]{:S(2)}) collective-permute-start(bf16[512,512]{1,0:T(8,128)(2,1)} %copy-done.53), channel_id=1, source_target_pairs={{0,1},{1,0},{2,3},{3,2},{4,5},{5,4},{6,7},{7,6},{8,9},{9,8},{10,11... | collective-permute-start | bytes 1572872 | tf_op jit(solution)/shard_map/ppermute | solution.py:412
  124.8 21.4 %collective-permute-start.22 = (bf16[512,512]{1,0:T(8,128)(2,1)}, bf16[512,512]{1,0:T(8,128)(2,1)S(1)}, u32[]{:S(2)}, u32[]{:S(2)}) collective-permute-start(bf16[512,512]{1,0:T(8,128)(2,1)} %copy-done.54), channel_id=1, source_target_pairs={{0,1},{1,0},{2,3},{3,2},{4,5},{5,4},{6,7},{7,6},{8,9},{9,8},{10,11... | collective-permute-start | bytes 1572872 | tf_op jit(solution)/shard_map/ppermute | solution.py:412
  136.1 14.2 %collective-permute-start.23 = (bf16[512,512]{1,0:T(8,128)(2,1)S(1)}, bf16[512,512]{1,0:T(8,128)(2,1)S(1)}, u32[]{:S(2)}, u32[]{:S(2)}) collective-permute-start(bf16[512,512]{1,0:T(8,128)(2,1)S(1)} %get-tuple-element.331), channel_id=1, source_target_pairs={{0,1},{1,0},{2,3},{3,2},{4,5},{5,4},{6,7},{7,6},{8,9},{9,8},{10,11... | collective-permute-start | bytes 1572872 | tf_op jit(solution)/shard_map/ppermute | solution.py:412
  151.1 15.4 %collective-permute-start.24 = (bf16[4,32,4096]{2,1,0:T(8,128)(2,1)S(1)}, bf16[4,32,4096]{2,1,0:T(8,128)(2,1)S(1)}, u32[]{:S(2)}, u32[]{:S(2)}) collective-permute-start(bf16[4,32,4096]{2,1,0:T(8,128)(2,1)S(1)} %bitcast.58), channel_id=1, source_target_pairs={{0,1},{1,0},{2,3},{3,2},{4,5},{5,4},{6,7},{7,6},{8,9},{9,8},{10,11... | collective-permute-start | bytes 3145736 | tf_op jit(solution)/shard_map/ppermute | solution.py:412
  151.1 15.4 %collective-permute-start.25 = (bf16[4,32,4096]{2,1,0:T(8,128)(2,1)S(1)}, bf16[4,32,4096]{2,1,0:T(8,128)(2,1)S(1)}, u32[]{:S(2)}, u32[]{:S(2)}) collective-permute-start(bf16[4,32,4096]{2,1,0:T(8,128)(2,1)S(1)} %collective-permute-done.17.refs_2_), channel_id=1, source_target_pairs={{0,1},{1,0},{2,3},{3,2},{4,5},{5,4},{6,7},{7,6},{8,9},{9,8},{10,11... | collective-permute-start | bytes 3145736 | tf_op jit(solution)/shard_map/ppermute | solution.py:412
  151.6 15.0 %collective-permute-start.26 = (bf16[4,32,4096]{2,1,0:T(8,128)(2,1)S(1)}, bf16[4,32,4096]{2,1,0:T(8,128)(2,1)S(1)}, u32[]{:S(2)}, u32[]{:S(2)}) collective-permute-start(bf16[4,32,4096]{2,1,0:T(8,128)(2,1)S(1)} %collective-permute-done.18.refs_3_), channel_id=1, source_target_pairs={{0,1},{1,0},{2,3},{3,2},{4,5},{5,4},{6,7},{7,6},{8,9},{9,8},{10,11... | collective-permute-start | bytes 3145736 | tf_op jit(solution)/shard_map/ppermute | solution.py:412
  154.0 19.9 %collective-permute-start.27 = (bf16[2,32,4096]{2,1,0:T(8,128)(2,1)}, bf16[2,32,4096]{2,1,0:T(8,128)(2,1)S(1)}, u32[]{:S(2)}, u32[]{:S(2)}) collective-permute-start(bf16[2,32,4096]{2,1,0:T(8,128)(2,1)} %slice.100), channel_id=1, source_target_pairs={{0,2},{1,3},{2,0},{3,1},{4,6},{5,7},{6,4},{7,5},{8,10},{9,11},{10,... | collective-permute-start | bytes 1572872 | tf_op jit(solution)/shard_map/ppermute | solution.py:412
  155.4 18.4 %collective-permute-start.28 = (bf16[2,32,4096]{2,1,0:T(8,128)(2,1)}, bf16[2,32,4096]{2,1,0:T(8,128)(2,1)S(1)}, u32[]{:S(2)}, u32[]{:S(2)}) collective-permute-start(bf16[2,32,4096]{2,1,0:T(8,128)(2,1)} %slice.101), channel_id=1, source_target_pairs={{0,4},{1,5},{2,6},{3,7},{4,0},{5,1},{6,2},{7,3},{8,12},{9,13},{10,... | collective-permute-start | bytes 1572872 | tf_op jit(solution)/shard_map/ppermute | solution.py:412
  190.3 8.1 %collective-permute-start.32 = (bf16[512,2048]{1,0:T(8,128)(2,1)S(1)}, bf16[512,2048]{1,0:T(8,128)(2,1)S(1)}, u32[]{:S(2)}, u32[]{:S(2)}) collective-permute-start(bf16[512,2048]{1,0:T(8,128)(2,1)S(1)} %get-tuple-element.368), channel_id=1, source_target_pairs={{0,1},{1,0},{2,3},{3,2},{4,5},{5,4},{6,7},{7,6},{8,9},{9,8},{10,11... | collective-permute-start | bytes 6291464 | tf_op jit(solution)/shard_map/ppermute | solution.py:412
  207.5 25.4 %collective-permute-start.35 = (bf16[64,4096]{1,0:T(8,128)(2,1)}, bf16[64,4096]{1,0:T(8,128)(2,1)S(1)}, u32[]{:S(2)}, u32[]{:S(2)}) collective-permute-start(bf16[64,4096]{1,0:T(8,128)(2,1)} %get-tuple-element.393), channel_id=1, source_target_pairs={{0,2},{1,3},{2,0},{3,1},{4,6},{5,7},{6,4},{7,5},{8,10},{9,11},{10,... | collective-permute-start | bytes 1572872 | tf_op jit(solution)/shard_map/ppermute | solution.py:412
  207.5 25.4 %collective-permute-start.36 = (bf16[64,4096]{1,0:T(8,128)(2,1)}, bf16[64,4096]{1,0:T(8,128)(2,1)S(1)}, u32[]{:S(2)}, u32[]{:S(2)}) collective-permute-start(bf16[64,4096]{1,0:T(8,128)(2,1)} %get-tuple-element.394), channel_id=1, source_target_pairs={{0,4},{1,5},{2,6},{3,7},{4,0},{5,1},{6,2},{7,3},{8,12},{9,13},{10,... | collective-permute-start | bytes 1572872 | tf_op jit(solution)/shard_map/ppermute | solution.py:412
  209.0 24.0 %collective-permute-start.37 = (bf16[64,4096]{1,0:T(8,128)(2,1)}, bf16[64,4096]{1,0:T(8,128)(2,1)S(1)}, u32[]{:S(2)}, u32[]{:S(2)}) collective-permute-start(bf16[64,4096]{1,0:T(8,128)(2,1)} %get-tuple-element.395), channel_id=1, source_target_pairs={{0,2},{1,3},{2,0},{3,1},{4,6},{5,7},{6,4},{7,5},{8,10},{9,11},{10,... | collective-permute-start | bytes 1572872 | tf_op jit(solution)/shard_map/ppermute | solution.py:412
  211.0 22.1 %collective-permute-start.38 = (bf16[64,4096]{1,0:T(8,128)(2,1)}, bf16[64,4096]{1,0:T(8,128)(2,1)S(1)}, u32[]{:S(2)}, u32[]{:S(2)}) collective-permute-start(bf16[64,4096]{1,0:T(8,128)(2,1)} %get-tuple-element.396), channel_id=1, source_target_pairs={{0,4},{1,5},{2,6},{3,7},{4,0},{5,1},{6,2},{7,3},{8,12},{9,13},{10,... | collective-permute-start | bytes 1572872 | tf_op jit(solution)/shard_map/ppermute | solution.py:412
  236.0 31.3 %collective-permute-start.42 = (bf16[64,4096]{1,0:T(8,128)(2,1)S(1)}, bf16[64,4096]{1,0:T(8,128)(2,1)S(1)}, u32[]{:S(2)}, u32[]{:S(2)}) collective-permute-start(bf16[64,4096]{1,0:T(8,128)(2,1)S(1)} %get-tuple-element.422), channel_id=1, source_target_pairs={{0,2},{1,3},{2,0},{3,1},{4,6},{5,7},{6,4},{7,5},{8,10},{9,11},{10,... | collective-permute-start | bytes 1572872 | tf_op jit(solution)/shard_map/ppermute | solution.py:412
  236.5 30.8 %collective-permute-start.43 = (bf16[64,4096]{1,0:T(8,128)(2,1)S(1)}, bf16[64,4096]{1,0:T(8,128)(2,1)S(1)}, u32[]{:S(2)}, u32[]{:S(2)}) collective-permute-start(bf16[64,4096]{1,0:T(8,128)(2,1)S(1)} %get-tuple-element.423), channel_id=1, source_target_pairs={{0,4},{1,5},{2,6},{3,7},{4,0},{5,1},{6,2},{7,3},{8,12},{9,13},{10,... | collective-permute-start | bytes 1572872 | tf_op jit(solution)/shard_map/ppermute | solution.py:412
  247.4 19.9 %collective-permute-start.40 = (bf16[64,4096]{1,0:T(8,128)(2,1)}, bf16[64,4096]{1,0:T(8,128)(2,1)S(1)}, u32[]{:S(2)}, u32[]{:S(2)}) collective-permute-start(bf16[64,4096]{1,0:T(8,128)(2,1)} %get-tuple-element.416), channel_id=1, source_target_pairs={{0,2},{1,3},{2,0},{3,1},{4,6},{5,7},{6,4},{7,5},{8,10},{9,11},{10,... | collective-permute-start | bytes 1572872 | tf_op jit(solution)/shard_map/ppermute | solution.py:412
  249.0 18.4 %collective-permute-start.41 = (bf16[64,4096]{1,0:T(8,128)(2,1)}, bf16[64,4096]{1,0:T(8,128)(2,1)S(1)}, u32[]{:S(2)}, u32[]{:S(2)}) collective-permute-start(bf16[64,4096]{1,0:T(8,128)(2,1)} %get-tuple-element.417), channel_id=1, source_target_pairs={{0,4},{1,5},{2,6},{3,7},{4,0},{5,1},{6,2},{7,3},{8,12},{9,13},{10,... | collective-permute-start | bytes 1572872 | tf_op jit(solution)/shard_map/ppermute | solution.py:412
  250.5 16.9 %collective-permute-start.44 = (bf16[512,1024]{1,0:T(8,128)(2,1)S(1)}, bf16[512,1024]{1,0:T(8,128)(2,1)S(1)}, u32[]{:S(2)}, u32[]{:S(2)}) collective-permute-start(bf16[512,1024]{1,0:T(8,128)(2,1)S(1)} %get-tuple-element.415), channel_id=1, source_target_pairs={{0,1},{1,0},{2,3},{3,2},{4,5},{5,4},{6,7},{7,6},{8,9},{9,8},{10,11... | collective-permute-start | bytes 3145736 | tf_op jit(solution)/shard_map/ppermute | solution.py:412
  267.5 13.2 %collective-permute-start.46 = (bf16[2,592,1024]{2,1,0:T(8,128)(2,1)S(1)}, bf16[2,592,1024]{2,1,0:T(8,128)(2,1)S(1)}, u32[]{:S(2)}, u32[]{:S(2)}) collective-permute-start(bf16[2,592,1024]{2,1,0:T(8,128)(2,1)S(1)} %get-tuple-element.518.refs_10_.refs_0_), channel_id=1, source_target_pairs={{0,1},{1,0},{2,3},{3,2},{4,5},{5,4},{6,7},{7,6},{8,9},{9,8},{10,11... | collective-permute-start | bytes 7274504 | tf_op jit(solution)/shard_map/ppermute | solution.py:412
  268.0 12.6 %collective-permute-start.45 = (bf16[1,512,1024]{2,1,0:T(8,128)(2,1)S(1)}, bf16[1,512,1024]{2,1,0:T(8,128)(2,1)S(1)}, u32[]{:S(2)}, u32[]{:S(2)}) collective-permute-start(bf16[1,512,1024]{2,1,0:T(8,128)(2,1)S(1)} %get-tuple-element.440.refs_0_.refs_6_), channel_id=1, source_target_pairs={{0,1},{1,0},{2,3},{3,2},{4,5},{5,4},{6,7},{7,6},{8,9},{9,8},{10,11... | collective-permute-start | bytes 3145736 | tf_op jit(solution)/shard_map/ppermute | solution.py:412
  273.5 38.8 %collective-permute-start.50 = (bf16[128,4096]{1,0:T(8,128)(2,1)}, bf16[128,4096]{1,0:T(8,128)(2,1)}, u32[]{:S(2)}, u32[]{:S(2)}) collective-permute-start(bf16[128,4096]{1,0:T(8,128)(2,1)} %get-tuple-element.459), channel_id=1, source_target_pairs={{0,2},{1,3},{2,0},{3,1},{4,6},{5,7},{6,4},{7,5},{8,10},{9,11},{10,... | collective-permute-start | bytes 3145736 | tf_op jit(solution)/shard_map/ppermute | solution.py:412
  273.9 38.4 %collective-permute-start.51 = (bf16[128,4096]{1,0:T(8,128)(2,1)}, bf16[128,4096]{1,0:T(8,128)(2,1)}, u32[]{:S(2)}, u32[]{:S(2)}) collective-permute-start(bf16[128,4096]{1,0:T(8,128)(2,1)} %get-tuple-element.460), channel_id=1, source_target_pairs={{0,4},{1,5},{2,6},{3,7},{4,0},{5,1},{6,2},{7,3},{8,12},{9,13},{10,... | collective-permute-start | bytes 3145736 | tf_op jit(solution)/shard_map/ppermute | solution.py:412
  293.9 18.6 %collective-permute-start.49 = (bf16[512,1024]{1,0:T(8,128)(2,1)S(1)}, bf16[512,1024]{1,0:T(8,128)(2,1)}, u32[]{:S(2)}, u32[]{:S(2)}) collective-permute-start(bf16[512,1024]{1,0:T(8,128)(2,1)S(1)} %get-tuple-element.451), channel_id=1, source_target_pairs={{0,1},{1,0},{2,3},{3,2},{4,5},{5,4},{6,7},{7,6},{8,9},{9,8},{10,11... | collective-permute-start | bytes 3145736 | tf_op jit(solution)/shard_map/ppermute | solution.py:412
  296.6 80.4 %reduce-scatter.6.cloned.1.call-start = ((), (), s32[]{:S(2)}) async-start(), calls=%async_computation.5 | async-start | bytes 1310720 | tf_op jit(solution)/shard_map/reduce_scatter | solution.py:913
  296.6 15.6 %collective-permute-start.47 = (bf16[64,4096]{1,0:T(8,128)(2,1)}, bf16[64,4096]{1,0:T(8,128)(2,1)S(1)}, u32[]{:S(2)}, u32[]{:S(2)}) collective-permute-start(bf16[64,4096]{1,0:T(8,128)(2,1)} %get-tuple-element.452), channel_id=1, source_target_pairs={{0,2},{1,3},{2,0},{3,1},{4,6},{5,7},{6,4},{7,5},{8,10},{9,11},{10,... | collective-permute-start | bytes 1572872 | tf_op jit(solution)/shard_map/ppermute | solution.py:412
  298.3 14.2 %collective-permute-start.48 = (bf16[64,4096]{1,0:T(8,128)(2,1)}, bf16[64,4096]{1,0:T(8,128)(2,1)S(1)}, u32[]{:S(2)}, u32[]{:S(2)}) collective-permute-start(bf16[64,4096]{1,0:T(8,128)(2,1)} %get-tuple-element.453), channel_id=1, source_target_pairs={{0,4},{1,5},{2,6},{3,7},{4,0},{5,1},{6,2},{7,3},{8,12},{9,13},{10,... | collective-permute-start | bytes 1572872 | tf_op jit(solution)/shard_map/ppermute | solution.py:412
  313.1 20.8 %collective-permute-start.52 = (bf16[3,512,1024]{2,1,0:T(8,128)(2,1)}, bf16[3,512,1024]{2,1,0:T(8,128)(2,1)}, u32[]{:S(2)}, u32[]{:S(2)}) collective-permute-start(bf16[3,512,1024]{2,1,0:T(8,128)(2,1)} %attn_bwd.3.refs_0_.refs_6_.refs_2_), channel_id=1, source_target_pairs={{0,1},{1,0},{2,3},{3,2},{4,5},{5,4},{6,7},{7,6},{8,9},{9,8},{10,11... | collective-permute-start | bytes 9437192 | tf_op jit(solution)/shard_map/ppermute | solution.py:412
  316.2 86.3 %reduce-scatter.8.cloned.1.call-start = ((), (), s32[]{:S(2)}) async-start(), calls=%async_computation.6 | async-start | bytes 1310720 | tf_op jit(solution)/shard_map/reduce_scatter | solution.py:913
  319.1 31.5 %collective-permute-start.56 = (bf16[128,4096]{1,0:T(8,128)(2,1)}, bf16[128,4096]{1,0:T(8,128)(2,1)}, u32[]{:S(2)}, u32[]{:S(2)}) collective-permute-start(bf16[128,4096]{1,0:T(8,128)(2,1)} %get-tuple-element.491), channel_id=1, source_target_pairs={{0,2},{1,3},{2,0},{3,1},{4,6},{5,7},{6,4},{7,5},{8,10},{9,11},{10,... | collective-permute-start | bytes 3145736 | tf_op jit(solution)/shard_map/ppermute | solution.py:412
  319.6 31.0 %collective-permute-start.57 = (bf16[128,4096]{1,0:T(8,128)(2,1)S(1)}, bf16[128,4096]{1,0:T(8,128)(2,1)}, u32[]{:S(2)}, u32[]{:S(2)}) collective-permute-start(bf16[128,4096]{1,0:T(8,128)(2,1)S(1)} %get-tuple-element.492), channel_id=1, source_target_pairs={{0,4},{1,5},{2,6},{3,7},{4,0},{5,1},{6,2},{7,3},{8,12},{9,13},{10,... | collective-permute-start | bytes 3145736 | tf_op jit(solution)/shard_map/ppermute | solution.py:412
  343.3 8.9 %collective-permute-start.54 = (bf16[64,2048]{1,0:T(8,128)(2,1)}, bf16[64,2048]{1,0:T(8,128)(2,1)S(1)}, u32[]{:S(2)}, u32[]{:S(2)}) collective-permute-start(bf16[64,2048]{1,0:T(8,128)(2,1)} %get-tuple-element.479), channel_id=1, source_target_pairs={{0,2},{1,3},{2,0},{3,1},{4,6},{5,7},{6,4},{7,5},{8,10},{9,11},{10,... | collective-permute-start | bytes 786440 | tf_op jit(solution)/shard_map/ppermute | solution.py:412
  345.0 8.6 %collective-permute-start.55 = (bf16[64,2048]{1,0:T(8,128)(2,1)}, bf16[64,2048]{1,0:T(8,128)(2,1)S(1)}, u32[]{:S(2)}, u32[]{:S(2)}) collective-permute-start(bf16[64,2048]{1,0:T(8,128)(2,1)} %get-tuple-element.480), channel_id=1, source_target_pairs={{0,4},{1,5},{2,6},{3,7},{4,0},{5,1},{6,2},{7,3},{8,12},{9,13},{10,... | collective-permute-start | bytes 786440 | tf_op jit(solution)/shard_map/ppermute | solution.py:412
  359.1 20.0 %collective-permute-start.60 = (bf16[128,2048]{1,0:T(8,128)(2,1)}, bf16[128,2048]{1,0:T(8,128)(2,1)S(1)}, u32[]{:S(2)}, u32[]{:S(2)}) collective-permute-start(bf16[128,2048]{1,0:T(8,128)(2,1)} %get-tuple-element.504), channel_id=1, source_target_pairs={{0,2},{1,3},{2,0},{3,1},{4,6},{5,7},{6,4},{7,5},{8,10},{9,11},{10,... | collective-permute-start | bytes 1572872 | tf_op jit(solution)/shard_map/ppermute | solution.py:412
  359.5 19.6 %collective-permute-start.61 = (bf16[128,2048]{1,0:T(8,128)(2,1)}, bf16[128,2048]{1,0:T(8,128)(2,1)S(1)}, u32[]{:S(2)}, u32[]{:S(2)}) collective-permute-start(bf16[128,2048]{1,0:T(8,128)(2,1)} %get-tuple-element.505), channel_id=1, source_target_pairs={{0,4},{1,5},{2,6},{3,7},{4,0},{5,1},{6,2},{7,3},{8,12},{9,13},{10,... | collective-permute-start | bytes 1572872 | tf_op jit(solution)/shard_map/ppermute | solution.py:412
  360.1 18.5 %collective-permute-start.58 = (bf16[64,2176]{1,0:T(8,128)(2,1)}, bf16[64,2176]{1,0:T(8,128)(2,1)}, u32[]{:S(2)}, u32[]{:S(2)}) collective-permute-start(bf16[64,2176]{1,0:T(8,128)(2,1)} %get-tuple-element.499), channel_id=1, source_target_pairs={{0,2},{1,3},{2,0},{3,1},{4,6},{5,7},{6,4},{7,5},{8,10},{9,11},{10,... | collective-permute-start | bytes 835592 | tf_op jit(solution)/shard_map/ppermute | solution.py:412
  361.6 17.5 %collective-permute-start.59 = (bf16[64,2176]{1,0:T(8,128)(2,1)}, bf16[64,2176]{1,0:T(8,128)(2,1)}, u32[]{:S(2)}, u32[]{:S(2)}) collective-permute-start(bf16[64,2176]{1,0:T(8,128)(2,1)} %get-tuple-element.500), channel_id=1, source_target_pairs={{0,4},{1,5},{2,6},{3,7},{4,0},{5,1},{6,2},{7,3},{8,12},{9,13},{10,... | collective-permute-start | bytes 835592 | tf_op jit(solution)/shard_map/ppermute | solution.py:412
  380.7 16.0 %collective-permute-start.62 = (bf16[128,2176]{1,0:T(8,128)(2,1)S(1)}, bf16[128,2176]{1,0:T(8,128)(2,1)S(1)}, u32[]{:S(2)}, u32[]{:S(2)}) collective-permute-start(bf16[128,2176]{1,0:T(8,128)(2,1)S(1)} %get-tuple-element.515), channel_id=1, source_target_pairs={{0,2},{1,3},{2,0},{3,1},{4,6},{5,7},{6,4},{7,5},{8,10},{9,11},{10,... | collective-permute-start | bytes 1671176 | tf_op jit(solution)/shard_map/ppermute | solution.py:412
  382.0 14.7 %collective-permute-start.63 = (bf16[128,2176]{1,0:T(8,128)(2,1)S(1)}, bf16[128,2176]{1,0:T(8,128)(2,1)S(1)}, u32[]{:S(2)}, u32[]{:S(2)}) collective-permute-start(bf16[128,2176]{1,0:T(8,128)(2,1)S(1)} %get-tuple-element.516), channel_id=1, source_target_pairs={{0,4},{1,5},{2,6},{3,7},{4,0},{5,1},{6,2},{7,3},{8,12},{9,13},{10,... | collective-permute-start | bytes 1671176 | tf_op jit(solution)/shard_map/ppermute | solution.py:412
  384.3 11.7 %collective-permute-start.65 = (bf16[32,2048]{1,0:T(8,128)(2,1)S(1)}, bf16[32,2048]{1,0:T(8,128)(2,1)S(1)}, u32[]{:S(2)}, u32[]{:S(2)}) collective-permute-start(bf16[32,2048]{1,0:T(8,128)(2,1)S(1)} %get-tuple-element.530), channel_id=1, source_target_pairs={{0,8},{1,9},{2,10},{3,11},{4,12},{5,13},{6,14},{7,15},{8,16},{9,17... | collective-permute-start | bytes 393224 | tf_op jit(solution)/shard_map/ppermute | solution.py:941
  384.3 11.7 %collective-permute-start.66 = (bf16[32,2048]{1,0:T(8,128)(2,1)S(1)}, bf16[32,2048]{1,0:T(8,128)(2,1)S(1)}, u32[]{:S(2)}, u32[]{:S(2)}) collective-permute-start(bf16[32,2048]{1,0:T(8,128)(2,1)S(1)} %get-tuple-element.531), channel_id=1, source_target_pairs={{0,16},{1,17},{2,18},{3,19},{4,20},{5,21},{6,22},{7,23},{8,24},{9,... | collective-permute-start | bytes 393224 | tf_op jit(solution)/shard_map/ppermute | solution.py:941
  388.0 8.0 %collective-permute-start.67 = (bf16[32,2048]{1,0:T(8,128)(2,1)S(1)}, bf16[32,2048]{1,0:T(8,128)(2,1)S(1)}, u32[]{:S(2)}, u32[]{:S(2)}) collective-permute-start(bf16[32,2048]{1,0:T(8,128)(2,1)S(1)} %get-tuple-element.532), channel_id=1, source_target_pairs={{0,24},{1,25},{2,26},{3,27},{4,28},{5,29},{6,30},{7,31},{8,0},{9,1... | collective-permute-start | bytes 393224 | tf_op jit(solution)/shard_map/ppermute | solution.py:941
  397.5 8.5 %collective-permute-start.64 = (bf16[32,2176]{1,0:T(8,128)(2,1)S(1)}, bf16[32,2176]{1,0:T(8,128)(2,1)S(1)}, u32[]{:S(2)}, u32[]{:S(2)}) collective-permute-start(bf16[32,2176]{1,0:T(8,128)(2,1)S(1)} %get-tuple-element.524), channel_id=1, source_target_pairs={{0,8},{1,9},{2,10},{3,11},{4,12},{5,13},{6,14},{7,15},{8,16},{9,17... | collective-permute-start | bytes 417800 | tf_op jit(solution)/shard_map/ppermute | solution.py:941
  399.4 10.1 %collective-permute-start.68 = (bf16[32,2176]{1,0:T(8,128)(2,1)S(1)}, bf16[32,2176]{1,0:T(8,128)(2,1)S(1)}, u32[]{:S(2)}, u32[]{:S(2)}) collective-permute-start(bf16[32,2176]{1,0:T(8,128)(2,1)S(1)} %get-tuple-element.536), channel_id=1, source_target_pairs={{0,16},{1,17},{2,18},{3,19},{4,20},{5,21},{6,22},{7,23},{8,24},{9,... | collective-permute-start | bytes 417800 | tf_op jit(solution)/shard_map/ppermute | solution.py:941
  401.0 8.5 %collective-permute-start.69 = (bf16[32,2176]{1,0:T(8,128)(2,1)S(1)}, bf16[32,2176]{1,0:T(8,128)(2,1)S(1)}, u32[]{:S(2)}, u32[]{:S(2)}) collective-permute-start(bf16[32,2176]{1,0:T(8,128)(2,1)S(1)} %get-tuple-element.537), channel_id=1, source_target_pairs={{0,24},{1,25},{2,26},{3,27},{4,28},{5,29},{6,30},{7,31},{8,0},{9,1... | collective-permute-start | bytes 417800 | tf_op jit(solution)/shard_map/ppermute | solution.py:941
  (98 other events, 710.7 us)
Sparse Core Ops, SparseCore 0:
  35.0 30.1 all-gather.8
  69.7 28.7 all-gather.10
  121.1 83.1 all-gather.6
  296.7 28.1 reduce-scatter.3
  327.1 25.7 reduce-scatter.5
  356.7 26.0 reduce-scatter.7
